TPU v7x, 32 devices: a whole 2x2x4 slice. The times are simulated.
32 devices in a mesh: runs: 2 (over y), ja: 16 (over z, x, core).
Axes of the slice: x: 2, y: 2, z: 4, core: 2. Of those that a mesh axis runs over, the one named last changes fastest.
Arguments:
- pos_vel: float32 [6, 32768], P(None, ('runs', 'ja')), parts along dimension 1, may hold values from -4 to 4
- acc_jerk: float32 [6, 32768], P(None, ('runs', 'ja')), parts along dimension 1, may hold values from -5 to 5
- star_mass: float32 [32768], P(('runs', 'ja')), parts along dimension 0, may hold values from 1.2207031e-05 to 0.00030517578
- step_phase: float32 [32768], P(('runs', 'ja')), parts along dimension 0, may hold values from 0.25 to 1
- step_level: int32 [32768], P(('runs', 'ja')), parts along dimension 0, may hold values from 0 to 3
- counts: int32 [32], P(('runs', 'ja')), parts along dimension 0, may hold values from 1 to 256, 2048 in all
- star_order: int32 [32, 1024], P(('runs', 'ja')), parts along dimension 0, may hold values from 0 to 1023, each once within a row
Outputs:
- new_pos_vel: float32 [6, 32768], P(None, ('runs', 'ja')), parts along dimension 1
- new_acc_jerk: float32 [6, 32768], P(None, ('runs', 'ja')), parts along dimension 1
- active_state: float32 [12, 8192], P(None, ('runs', 'ja')), parts along dimension 1
There are 2 independent parts, one for each index of `runs`. A program takes and returns all parts, laid end to end along the dimension named above; each array names one. Nothing has to cross between parts.
Inputs may be any that keep to these rules, and one draw needn't show every extreme that they name: The counts sum to 2048; the largest is exactly 256. `star_order`: each row is a permutation of the local indices.
All inputs are finite; a program needn't handle non-finite values. No bound on the sum of `counts` on one device may be relied on, other than what follows from the above.
Results may differ from a plain program's by a relative error of at most 0.00002.
Values sent between devices are 32-bit elements; how exact they have to be, the bound alone decides.
No kernel may reach another device: no remote copies, remote signals or barrier semaphores. Data moves between devices by JAX's collectives and lax.ppermute only.
A program may use at most 64 MiB of HBM per device.

v0:
```python
import math

import jax
import jax.numpy as jnp
from jax import lax
from jax.sharding import PartitionSpec as P

A_DEV = 128


soft_sq = 0.01
base_step = 2.0


def predict(pos_vel, acc_jerk, age):
    half_sq = 0.5 * age * age
    sixth_cube = age * age * age / 6.0
    position = (
        pos_vel[0:3] + age * pos_vel[3:6] + half_sq * acc_jerk[0:3] + sixth_cube * acc_jerk[3:6]
    )
    velocity = pos_vel[3:6] + age * acc_jerk[0:3] + half_sq * acc_jerk[3:6]
    return jnp.concatenate([position, velocity], axis=0)


def pair_block(targets, sources):
    delta_x = sources[0:3, None, :] - targets[0:3, :, None]
    delta_v = sources[3:6, None, :] - targets[3:6, :, None]
    dist_sq = soft_sq + delta_x[0] * delta_x[0] + delta_x[1] * delta_x[1] + delta_x[2] * delta_x[2]
    inverse = lax.rsqrt(dist_sq)
    inverse_sq = inverse * inverse
    weight = sources[6][None, :] * inverse * inverse_sq
    radial = (
        3.0
        * (delta_x[0] * delta_v[0] + delta_x[1] * delta_v[1] + delta_x[2] * delta_v[2])
        * inverse_sq
    )
    accel_part = jnp.sum(weight[None] * delta_x, axis=2)
    jerk_part = jnp.sum(weight[None] * (delta_v - radial[None] * delta_x), axis=2)
    return jnp.concatenate([accel_part, jerk_part], axis=0)


def pair_forces(targets, sources):
    rows = targets.shape[1]
    block = math.gcd(rows, 512)
    split = targets.reshape(6, rows // block, block).transpose(1, 0, 2)
    result = lax.map(lambda part: pair_block(part, sources), split)
    return result.transpose(1, 0, 2).reshape(6, rows)


def correct(old_pv, old_aj, fresh, step_len):
    half = 0.5 * step_len
    twelfth = step_len * step_len / 12.0
    velocity = (
        old_pv[3:6] + half * (old_aj[0:3] + fresh[0:3]) + twelfth * (old_aj[3:6] - fresh[3:6])
    )
    position = old_pv[0:3] + half * (old_pv[3:6] + velocity) + twelfth * (old_aj[0:3] - fresh[0:3])
    return jnp.concatenate([position, velocity], axis=0)


def per_device(pos_vel, acc_jerk, star_mass, step_phase, step_level, counts, star_order):
    capacity = 2 * A_DEV
    per_owner = pos_vel.shape[1]
    slot_ids = star_order[0, :capacity]
    live = jnp.arange(capacity, dtype=jnp.int32) < counts[0]
    step_len = base_step * jnp.exp2(-step_level.astype(jnp.float32))
    is_active = jnp.zeros((per_owner,), jnp.float32).at[slot_ids].set(live.astype(jnp.float32))
    age = step_len * jnp.where(is_active > 0.5, jnp.float32(1.0), step_phase)
    predicted = predict(pos_vel, acc_jerk, age)
    sources = jnp.concatenate([predicted, star_mass[None, :]], axis=0)
    targets = predicted[:, slot_ids]
    every_slot = pair_forces(lax.all_gather(targets, "ja", axis=1, tiled=True), sources)
    fresh = lax.psum_scatter(every_slot, "ja", scatter_dimension=1, tiled=True)
    old_pv = pos_vel[:, slot_ids]
    old_aj = acc_jerk[:, slot_ids]
    corrected = correct(old_pv, old_aj, fresh, step_len[slot_ids])
    kept_pv = jnp.where(live[None, :], corrected, old_pv)
    kept_aj = jnp.where(live[None, :], fresh, old_aj)
    fresh_state = jnp.concatenate([corrected, fresh], axis=0)
    active_state = jnp.where(live[None, :], fresh_state, jnp.zeros_like(fresh_state))
    return (
        pos_vel.at[:, slot_ids].set(kept_pv),
        acc_jerk.at[:, slot_ids].set(kept_aj),
        active_state,
    )


def solution(mesh):
    in_specs = (
        P(None, ("runs", "ja")),
        P(None, ("runs", "ja")),
        P(("runs", "ja")),
        P(("runs", "ja")),
        P(("runs", "ja")),
        P(("runs", "ja")),
        P(("runs", "ja"), None),
    )
    out_specs = (P(None, ("runs", "ja")), P(None, ("runs", "ja")), P(None, ("runs", "ja")))
    return jax.shard_map(
        per_device, mesh=mesh, in_specs=in_specs, out_specs=out_specs, check_vma=False
    )
```

profile of v0, /device:TPU:1, one launch (start us, length us, event | category | flops | bytes accessed | tf_op | source)
XLA Modules:
  0.0 160.3 jit_solution(9039283092665602739)
XLA Ops:
  8.6 1.4 scatter_custom_fusion
  12.6 32.1 %all-gather = f32[6,4096]{0,1:T(8,128)S(1)} all-gather(f32[6,256]{0,1:T(8,128)S(1)} %bitcast.44), channel_id=2, replica_groups=mesh['runs'=2,'ja'=16] {'ja'}, dimensions={1}, use_global_device_ids=true | all-gather | bytes 104448 | tf_op jit(solution)/shard_map/all_gather | solution.py:71
  45.3 45.8 %while.10 = (s32[]{:T(128)}, f32[8,6,512]{2,1,0:T(8,128)S(1)}, f32[1,1024]{1,0:T(1,128)S(1)}, f32[3,1024]{1,0:T(4,128)S(1)}, f32[8,6,512]{2,1,0:T(8,128)S(1)}, /...) while((s32[]{:T(128)}, f32[8,6,512]{2,1,0:T(8,128)S(1)}, f32[1,1024]{1,0:T(1,128)S(1)}, ...), condition=%wide.region_4.5_spmd, body=%wide.region_1.4_spmd.sunk | while | flops 24117252 | bytes 33702004 | solution.py:46
  46.4 2.1 %fusion.17 = (f32[512,1024]{1,0:T(8,128)S(1)}, f32[512,1024]{1,0:T(8,128)S(1)}) fusion(f32[3,512,1024]{2,1,0:T(8,128)S(1)} %get-tuple-element.141, f32[3,512,1024]{2,1,0:T(8,128)S(1)} %get-tuple-element.142, f32[1024]{0:T(1024)S(1)} %bitcast.47), kind=kLoop, calls=%fused_computation.15.clone.1 | loop fusion | flops 8388608 | bytes 16781312 | tf_op jit(solution)/shard_map/while/body/eval_jaxpr/mul | solution.py:38
  48.5 2.5 %multiply_reduce_fusion.3 = (f32[3,512]{1,0:T(4,128)S(1)}, f32[3,512]{1,0:T(4,128)S(1)}) fusion(f32[512,1024]{1,0:T(8,128)S(1)} %get-tuple-element.143, f32[3,512]{1,0:T(4,128)S(1)} %get-tuple-element.140, f32[3,1024]{1,0:T(4,128)S(1)} %get-tuple-element.168, f32[512,1024]{1,0:T(8,128)S(1)} %get-tuple-element.144, ...), kind=kLoop, calls=%fused_computation.8.clone.1 | loop fusion | flops 12579840 | bytes 4243456 | tf_op jit(solution)/shard_map/while/body/eval_jaxpr/reduce_sum | solution.py:37
  52.1 2.1 %fusion.17 = (f32[512,1024]{1,0:T(8,128)S(1)}, f32[512,1024]{1,0:T(8,128)S(1)}) fusion(f32[3,512,1024]{2,1,0:T(8,128)S(1)} %get-tuple-element.141, f32[3,512,1024]{2,1,0:T(8,128)S(1)} %get-tuple-element.142, f32[1024]{0:T(1024)S(1)} %bitcast.47), kind=kLoop, calls=%fused_computation.15.clone.1 | loop fusion | flops 8388608 | bytes 16781312 | tf_op jit(solution)/shard_map/while/body/eval_jaxpr/mul | solution.py:38
  54.2 2.5 %multiply_reduce_fusion.3 = (f32[3,512]{1,0:T(4,128)S(1)}, f32[3,512]{1,0:T(4,128)S(1)}) fusion(f32[512,1024]{1,0:T(8,128)S(1)} %get-tuple-element.143, f32[3,512]{1,0:T(4,128)S(1)} %get-tuple-element.140, f32[3,1024]{1,0:T(4,128)S(1)} %get-tuple-element.168, f32[512,1024]{1,0:T(8,128)S(1)} %get-tuple-element.144, ...), kind=kLoop, calls=%fused_computation.8.clone.1 | loop fusion | flops 12579840 | bytes 4243456 | tf_op jit(solution)/shard_map/while/body/eval_jaxpr/reduce_sum | solution.py:37
  57.9 2.1 %fusion.17 = (f32[512,1024]{1,0:T(8,128)S(1)}, f32[512,1024]{1,0:T(8,128)S(1)}) fusion(f32[3,512,1024]{2,1,0:T(8,128)S(1)} %get-tuple-element.141, f32[3,512,1024]{2,1,0:T(8,128)S(1)} %get-tuple-element.142, f32[1024]{0:T(1024)S(1)} %bitcast.47), kind=kLoop, calls=%fused_computation.15.clone.1 | loop fusion | flops 8388608 | bytes 16781312 | tf_op jit(solution)/shard_map/while/body/eval_jaxpr/mul | solution.py:38
  60.0 2.5 %multiply_reduce_fusion.3 = (f32[3,512]{1,0:T(4,128)S(1)}, f32[3,512]{1,0:T(4,128)S(1)}) fusion(f32[512,1024]{1,0:T(8,128)S(1)} %get-tuple-element.143, f32[3,512]{1,0:T(4,128)S(1)} %get-tuple-element.140, f32[3,1024]{1,0:T(4,128)S(1)} %get-tuple-element.168, f32[512,1024]{1,0:T(8,128)S(1)} %get-tuple-element.144, ...), kind=kLoop, calls=%fused_computation.8.clone.1 | loop fusion | flops 12579840 | bytes 4243456 | tf_op jit(solution)/shard_map/while/body/eval_jaxpr/reduce_sum | solution.py:37
  63.6 2.1 %fusion.17 = (f32[512,1024]{1,0:T(8,128)S(1)}, f32[512,1024]{1,0:T(8,128)S(1)}) fusion(f32[3,512,1024]{2,1,0:T(8,128)S(1)} %get-tuple-element.141, f32[3,512,1024]{2,1,0:T(8,128)S(1)} %get-tuple-element.142, f32[1024]{0:T(1024)S(1)} %bitcast.47), kind=kLoop, calls=%fused_computation.15.clone.1 | loop fusion | flops 8388608 | bytes 16781312 | tf_op jit(solution)/shard_map/while/body/eval_jaxpr/mul | solution.py:38
  65.7 2.5 %multiply_reduce_fusion.3 = (f32[3,512]{1,0:T(4,128)S(1)}, f32[3,512]{1,0:T(4,128)S(1)}) fusion(f32[512,1024]{1,0:T(8,128)S(1)} %get-tuple-element.143, f32[3,512]{1,0:T(4,128)S(1)} %get-tuple-element.140, f32[3,1024]{1,0:T(4,128)S(1)} %get-tuple-element.168, f32[512,1024]{1,0:T(8,128)S(1)} %get-tuple-element.144, ...), kind=kLoop, calls=%fused_computation.8.clone.1 | loop fusion | flops 12579840 | bytes 4243456 | tf_op jit(solution)/shard_map/while/body/eval_jaxpr/reduce_sum | solution.py:37
  69.3 2.1 %fusion.17 = (f32[512,1024]{1,0:T(8,128)S(1)}, f32[512,1024]{1,0:T(8,128)S(1)}) fusion(f32[3,512,1024]{2,1,0:T(8,128)S(1)} %get-tuple-element.141, f32[3,512,1024]{2,1,0:T(8,128)S(1)} %get-tuple-element.142, f32[1024]{0:T(1024)S(1)} %bitcast.47), kind=kLoop, calls=%fused_computation.15.clone.1 | loop fusion | flops 8388608 | bytes 16781312 | tf_op jit(solution)/shard_map/while/body/eval_jaxpr/mul | solution.py:38
  71.4 2.5 %multiply_reduce_fusion.3 = (f32[3,512]{1,0:T(4,128)S(1)}, f32[3,512]{1,0:T(4,128)S(1)}) fusion(f32[512,1024]{1,0:T(8,128)S(1)} %get-tuple-element.143, f32[3,512]{1,0:T(4,128)S(1)} %get-tuple-element.140, f32[3,1024]{1,0:T(4,128)S(1)} %get-tuple-element.168, f32[512,1024]{1,0:T(8,128)S(1)} %get-tuple-element.144, ...), kind=kLoop, calls=%fused_computation.8.clone.1 | loop fusion | flops 12579840 | bytes 4243456 | tf_op jit(solution)/shard_map/while/body/eval_jaxpr/reduce_sum | solution.py:37
  75.0 2.1 %fusion.17 = (f32[512,1024]{1,0:T(8,128)S(1)}, f32[512,1024]{1,0:T(8,128)S(1)}) fusion(f32[3,512,1024]{2,1,0:T(8,128)S(1)} %get-tuple-element.141, f32[3,512,1024]{2,1,0:T(8,128)S(1)} %get-tuple-element.142, f32[1024]{0:T(1024)S(1)} %bitcast.47), kind=kLoop, calls=%fused_computation.15.clone.1 | loop fusion | flops 8388608 | bytes 16781312 | tf_op jit(solution)/shard_map/while/body/eval_jaxpr/mul | solution.py:38
  77.1 2.5 %multiply_reduce_fusion.3 = (f32[3,512]{1,0:T(4,128)S(1)}, f32[3,512]{1,0:T(4,128)S(1)}) fusion(f32[512,1024]{1,0:T(8,128)S(1)} %get-tuple-element.143, f32[3,512]{1,0:T(4,128)S(1)} %get-tuple-element.140, f32[3,1024]{1,0:T(4,128)S(1)} %get-tuple-element.168, f32[512,1024]{1,0:T(8,128)S(1)} %get-tuple-element.144, ...), kind=kLoop, calls=%fused_computation.8.clone.1 | loop fusion | flops 12579840 | bytes 4243456 | tf_op jit(solution)/shard_map/while/body/eval_jaxpr/reduce_sum | solution.py:37
  80.7 2.1 %fusion.17 = (f32[512,1024]{1,0:T(8,128)S(1)}, f32[512,1024]{1,0:T(8,128)S(1)}) fusion(f32[3,512,1024]{2,1,0:T(8,128)S(1)} %get-tuple-element.141, f32[3,512,1024]{2,1,0:T(8,128)S(1)} %get-tuple-element.142, f32[1024]{0:T(1024)S(1)} %bitcast.47), kind=kLoop, calls=%fused_computation.15.clone.1 | loop fusion | flops 8388608 | bytes 16781312 | tf_op jit(solution)/shard_map/while/body/eval_jaxpr/mul | solution.py:38
  82.8 2.5 %multiply_reduce_fusion.3 = (f32[3,512]{1,0:T(4,128)S(1)}, f32[3,512]{1,0:T(4,128)S(1)}) fusion(f32[512,1024]{1,0:T(8,128)S(1)} %get-tuple-element.143, f32[3,512]{1,0:T(4,128)S(1)} %get-tuple-element.140, f32[3,1024]{1,0:T(4,128)S(1)} %get-tuple-element.168, f32[512,1024]{1,0:T(8,128)S(1)} %get-tuple-element.144, ...), kind=kLoop, calls=%fused_computation.8.clone.1 | loop fusion | flops 12579840 | bytes 4243456 | tf_op jit(solution)/shard_map/while/body/eval_jaxpr/reduce_sum | solution.py:37
  86.5 2.1 %fusion.17 = (f32[512,1024]{1,0:T(8,128)S(1)}, f32[512,1024]{1,0:T(8,128)S(1)}) fusion(f32[3,512,1024]{2,1,0:T(8,128)S(1)} %get-tuple-element.141, f32[3,512,1024]{2,1,0:T(8,128)S(1)} %get-tuple-element.142, f32[1024]{0:T(1024)S(1)} %bitcast.47), kind=kLoop, calls=%fused_computation.15.clone.1 | loop fusion | flops 8388608 | bytes 16781312 | tf_op jit(solution)/shard_map/while/body/eval_jaxpr/mul | solution.py:38
  88.6 2.5 %multiply_reduce_fusion.3 = (f32[3,512]{1,0:T(4,128)S(1)}, f32[3,512]{1,0:T(4,128)S(1)}) fusion(f32[512,1024]{1,0:T(8,128)S(1)} %get-tuple-element.143, f32[3,512]{1,0:T(4,128)S(1)} %get-tuple-element.140, f32[3,1024]{1,0:T(4,128)S(1)} %get-tuple-element.168, f32[512,1024]{1,0:T(8,128)S(1)} %get-tuple-element.144, ...), kind=kLoop, calls=%fused_computation.8.clone.1 | loop fusion | flops 12579840 | bytes 4243456 | tf_op jit(solution)/shard_map/while/body/eval_jaxpr/reduce_sum | solution.py:37
  91.8 1.4 gather_fusion.1
  95.3 50.8 %reduce-scatter.2.cloned.1.call-done = f32[6,256]{1,0:T(8,128)} async-done(((f32[6,4096]{1,0:T(8,128)}), f32[6,256]{1,0:T(8,128)}) %reduce-scatter.2.cloned.1.call-update) | async-done | bytes 6160 | tf_op jit(solution)/shard_map/reduce_scatter | solution.py:72
  147.7 1.4 scatter_fusion.1
  150.0 1.4 scatter_fusion
  152.2 1.3 maximum_select_fusion
  (59 shorter events, 18.7 us)
Async XLA Ops:
  7.2 138.9 %reduce-scatter.2.cloned.1.call-start = ((), (), s32[]{:S(2)}) async-start(), calls=%async_computation.1 | async-start | bytes 139264 | tf_op jit(solution)/shard_map/reduce_scatter | solution.py:72
  12.6 32.7 %copy-start.3 = (f32[1024]{0:T(1024)S(1)}, f32[1024]{0:T(1024)}, u32[]{:S(2)}) copy-start(f32[1024]{0:T(1024)} %param.11) | copy-start | bytes 12292
  45.3 47.8 %copy-start = (f32[6,1024]{1,0:T(8,128)S(1)}, f32[6,1024]{1,0:T(8,128)}, u32[]{:S(2)}) copy-start(f32[6,1024]{1,0:T(8,128)} %param.10) | copy-start | bytes 73732
  45.3 48.1 %copy-start.1 = (f32[6,1024]{1,0:T(8,128)S(1)}, f32[6,1024]{1,0:T(8,128)}, u32[]{:S(2)}) copy-start(f32[6,1024]{1,0:T(8,128)} %param.9) | copy-start | bytes 73732
  91.1 0.6 copy-start.2
Sparse Core Ops, SparseCore 0:
  91.9 54.1 reduce-scatter.1
where the time goes:
time: 163 us; the launch traced here: 160 us
  waiting for transfers between devices  50.8 us (31%)
  other arithmetic  50.4 us (31%)
  blocking collectives  32.1 us (20%)
  between operations  14.8 us (9%)
  local copies, waits for them, and re-layouts  11.8 us (7%)
    reduce_scatter x1, waiting for transfers between devices, per_device(): fresh = lax.psum_scatter(every_slot, 'ja', scatter_dimension=1, tiled=True)  50.8 us
    all_gather x1, blocking collectives, per_device(): lax.all_gather(targets, 'ja', axis=1, tiled=True)  32.1 us
    reduce_sum x8, other arithmetic, pair_block(): accel_part = jnp.sum(weight[None] * delta_x, axis=2)  20 us
    mul x8, other arithmetic, pair_block(): radial[None] * delta_x  16.6 us
    sub x8, other arithmetic, pair_block(): delta_v = sources[3:6, None, :] - targets[3:6, :, None]  8.53 us
  transfers between devices with their start and end apart: 1, of which 1 were waited for; matrix products, arithmetic and copies ran while one was open for 2% of the time, Pallas kernels for 0%

commit v1 on v0

v1 whole, which is shorter than its diff:
```python
import functools

import jax
import jax.numpy as jnp
from jax import lax
from jax.experimental import pallas as pl
from jax.experimental.pallas import tpu as pltpu
from jax.sharding import PartitionSpec as P

soft_sq = 0.01
base_step = 2.0
f32 = jnp.float32
bf16 = jnp.bfloat16

CHUNK = 256
FACTOR_ROWS = 64
PARAMS = pltpu.CompilerParams(vmem_limit_bytes=48 << 20)


def round_bf16(values):
    return values.astype(bf16).astype(f32)


def split(values, terms):
    out = []
    for _ in range(terms - 1):
        head = round_bf16(values)
        out.append(head)
        values = values - head
    return out + [round_bf16(values)]


def dot3(a, b):
    return a[0:1] * b[0:1] + a[1:2] * b[1:2] + a[2:3] * b[2:3]


def star_pieces(state):
    x, u = state[0:3], state[3:6]
    grid = jnp.floor(x * 4.0 + 0.5) * 0.25
    low = x - grid
    low1 = round_bf16(low)
    low2 = round_bf16(low - low1)
    low = low1 + low2
    return (
        grid,
        low1,
        low2,
        split(u, 3),
        split(dot3(grid, grid), 2),
        2.0 * dot3(grid, low) + dot3(low, low),
        dot3(grid + low, u),
    )


def source_factors(state):
    grid, low1, low2, (u1, u2, u3), grid_sq, rest, xu = star_pieces(state)
    one = jnp.ones_like(state[0:1])
    rows = [grid] + grid_sq + [one] * 2 + split(rest, 3) + [one] * 3
    rows += [grid] * 2 + [low1] * 3 + [low2] * 2 + [u1] * 3 + [u2] * 2 + [u3] + split(xu, 3)
    used = sum(r.shape[0] for r in rows)
    return jnp.concatenate(rows + [jnp.zeros((FACTOR_ROWS - used, state.shape[1]), f32)], axis=0)


def target_factors(state):
    grid, low1, low2, (u1, u2, u3), grid_sq, rest, xu = star_pieces(state)
    one = jnp.ones_like(state[0:1])
    z1, z3 = jnp.zeros_like(one), jnp.zeros_like(grid)
    dist = [-2.0 * grid] + [one] * 2 + grid_sq + [one] * 3 + split(rest + soft_sq, 3)
    dist += [-2.0 * low1, -2.0 * low2, -2.0 * grid, -2.0 * low1, -2.0 * low2, -2.0 * grid, -2.0 * low1]
    dist += [z3] * 6 + [z1] * 3
    radial = [-u1] + [z1] * 7 + split(xu, 3)
    radial += [-u2, -u3, -u1, -u2, z3, -u1, z3]
    radial += [-grid, -low1, -low2, -grid, -low1, -grid] + [one] * 3
    used = sum(r.shape[0] for r in dist)
    pad = [jnp.zeros((FACTOR_ROWS - used, state.shape[1]), f32)]
    return jnp.concatenate(
        [jnp.concatenate(radial + pad, axis=0), jnp.concatenate(dist + pad, axis=0)], axis=1
    )


def sum_factors(state):
    mass = state[6:7]
    mass_x, mass_u = mass * state[0:3], mass * state[3:6]
    by_weight = jnp.concatenate([mass_x, mass_u, mass, jnp.zeros_like(mass)], axis=0)
    by_radial = jnp.concatenate(
        [jnp.zeros_like(mass_x), -3.0 * mass_x, jnp.zeros_like(mass), 3.0 * mass], axis=0
    )
    return (
        jnp.concatenate(split(by_weight, 3), axis=0).astype(bf16),
        jnp.concatenate(split(by_radial, 3), axis=0).astype(bf16),
    )


def add_pairs(state, factors_t, acc_ref, products, weights):
    slots = factors_t.shape[1] // 2
    chunks = state.shape[1] // CHUNK
    factors_s = source_factors(state).T.astype(bf16)
    by_weight, by_radial = sum_factors(state)

    def multiply(c):
        products[c][...] = jnp.dot(
            factors_s[c * CHUNK : (c + 1) * CHUNK], factors_t, preferred_element_type=f32
        )

    def weigh(c):
        for g in range(0, CHUNK, 16):
            for lane in range(0, slots, 128):
                cols = slice(lane, lane + 128)
                radial = products[c][g : g + 16, cols]
                dist_sq = products[c][g : g + 16, slots + lane : slots + lane + 128]
                inverse = lax.rsqrt(dist_sq)
                inverse_sq = inverse * inverse
                weight = inverse * inverse_sq
                radial = weight * (inverse_sq * radial)
                weight_hi, radial_hi = weight.astype(bf16), radial.astype(bf16)
                weights[c][g : g + 16, cols] = weight_hi
                weights[c][CHUNK + g : CHUNK + g + 16, cols] = (weight - weight_hi.astype(f32)).astype(bf16)
                weights[c][2 * CHUNK + g : 2 * CHUNK + g + 16, cols] = radial_hi
                weights[c][3 * CHUNK + g : 3 * CHUNK + g + 16, cols] = (radial - radial_hi.astype(f32)).astype(bf16)

    def total(c):
        span = slice(c * CHUNK, (c + 1) * CHUNK)
        left = [by_weight[:, span]] * 2 + [by_radial[:, span]] * 2
        acc_ref[...] += jnp.dot(jnp.concatenate(left, axis=1), weights[c][...], preferred_element_type=f32)

    multiply(0)
    for c in range(chunks):
        if c + 1 < chunks:
            multiply(c + 1)
        weigh(c)
        if c > 0:
            total(c - 1)
    total(chunks - 1)


def add_blocks(sources_ref, factors_t, acc_ref, products, weights):
    blocks = sources_ref.shape[0] // 8
    together = 2 if blocks % 2 == 0 else 1

    def step(i, _):
        rows = [sources_ref[pl.ds(pl.multiple_of((i * together + b) * 8, 8), 8), :] for b in range(together)]
        add_pairs(jnp.concatenate(rows, axis=1), factors_t, acc_ref, products, weights)
        return 0

    if blocks == together:
        step(0, 0)
    else:
        lax.fori_loop(0, blocks // together, step, 0)


def pair_scratch(blocks, stars, slots):
    chunks = stars * (2 if blocks % 2 == 0 else 1) // CHUNK
    return [pltpu.VMEM((CHUNK, 2 * slots), f32)] * chunks + [pltpu.VMEM((4 * CHUNK, slots), bf16)] * chunks


def one_hot(order_ref, stars, slots):
    row = lax.broadcasted_iota(jnp.int32, (stars, slots), 0)
    return jnp.where(row == order_ref[0:1, 0:slots], 1.0, 0.0).astype(f32).astype(bf16)


def live_slots(count_ref, slots):
    return jnp.where(lax.broadcasted_iota(jnp.int32, (1, slots), 1) < count_ref[0], 1.0, 0.0)


def spread(hot, live):
    rows = jnp.broadcast_to(live, (16, live.shape[1])).astype(bf16)
    return lax.dot_general(rows, hot, (((1,), (1,)), ((), ())), preferred_element_type=f32)[0:1]


def exact_product(rows, hot, contract):
    height = rows.shape[0]
    terms = jnp.concatenate(split(rows, 3), axis=0).astype(bf16)
    out = lax.dot_general(terms, hot, (((1,), (contract,)), ((), ())), preferred_element_type=f32)
    return out[0:height] + out[height : 2 * height] + out[2 * height : 3 * height]


def prepare_kernel(slots, count_ref, pv_ref, aj_ref, mass_ref, phase_ref, level_ref, order_ref, src_ref, old_ref, fac_ref):
    stars = pv_ref.shape[1]
    hot = one_hot(order_ref, stars, slots)
    active = spread(hot, live_slots(count_ref, slots))
    level = level_ref[...]
    step_len = base_step * jnp.where((level & 1) > 0, 0.5, 1.0) * jnp.where((level & 2) > 0, 0.25, 1.0)
    age = step_len * jnp.where(active > 0.5, 1.0, phase_ref[...])
    half_sq = 0.5 * age * age
    sixth_cube = age * age * age / 6.0
    x, v, a, j = pv_ref[0:3], pv_ref[3:6], aj_ref[0:3], aj_ref[3:6]
    position = x + age * v + half_sq * a + sixth_cube * j
    velocity = v + age * a + half_sq * j
    src_ref[...] = jnp.concatenate([position, velocity, mass_ref[...], step_len], axis=0)
    rows = jnp.concatenate([position, velocity, step_len, jnp.zeros_like(step_len), x, v, a, j, x, a[0:1]], axis=0)
    old = exact_product(rows[0:24], hot, 0)
    old_ref[...] = old
    fac_ref[...] = target_factors(old[0:8]).astype(bf16)


def pair_kernel(fresh, src_ref, fac_ref, *refs):
    if fresh:
        out_ref, acc_ref, *scratch = refs
        acc_ref[...] = jnp.zeros_like(acc_ref)
    else:
        in_ref, out_ref, acc_ref, *scratch = refs
        acc_ref[...] = in_ref[...]
    half = len(scratch) // 2
    add_blocks(src_ref, fac_ref[...], acc_ref, scratch[:half], scratch[half:])
    out_ref[...] = acc_ref[...]


def finish_kernel(count_ref, src_ref, fac_ref, in_ref, old_ref, order_ref, pv_ref, aj_ref, new_pv_ref, new_aj_ref, state_ref, acc_ref, *scratch):
    stars, slots = pv_ref.shape[1], in_ref.shape[1]
    acc_ref[...] = in_ref[...]
    half = len(scratch) // 2
    add_blocks(src_ref, fac_ref[...], acc_ref, scratch[:half], scratch[half:])
    sums = acc_ref[0:8] + acc_ref[8:16] + acc_ref[16:24]
    here, there = old_ref[0:3], old_ref[3:6]
    a1 = sums[0:3] - here * sums[6:7]
    j1 = sums[3:6] - there * sums[6:7] + here * sums[7:8]
    step_len = old_ref[6:7]
    x0, v0, a0, j0 = old_ref[8:11], old_ref[11:14], old_ref[14:17], old_ref[17:20]
    half_step = 0.5 * step_len
    twelfth = step_len * step_len / 12.0
    v1 = v0 + half_step * (a0 + a1) + twelfth * (j0 - j1)
    x1 = x0 + half_step * (v0 + v1) + twelfth * (a0 - a1)
    live = live_slots(count_ref, slots)
    state = jnp.where(live > 0.5, jnp.concatenate([x1, v1, a1, j1], axis=0), 0.0)
    state_ref[...] = state
    hot = one_hot(order_ref, stars, slots)
    rows = jnp.concatenate([state, jnp.broadcast_to(live, (4, slots))], axis=0)
    moved = exact_product(rows, hot, 1)
    active = moved[12:13] > 0.5
    new_pv_ref[...] = jnp.where(active, moved[0:6], pv_ref[...])
    new_aj_ref[...] = jnp.where(active, moved[6:12], aj_ref[...])


VMEM = pl.BlockSpec(memory_space=pltpu.VMEM)
SMEM = pl.BlockSpec(memory_space=pltpu.SMEM)


def cost(blocks, stars, slots):
    pairs = blocks * stars * slots
    return pl.CostEstimate(flops=2 * 256 * 6 * pairs, bytes_accessed=64 * blocks * stars, transcendentals=pairs)


def call_pairs(sources, factors, acc):
    blocks, stars, slots = sources.shape[0] // 8, sources.shape[1], factors.shape[1] // 2
    operands = [sources, factors] + ([] if acc is None else [acc])
    return pl.pallas_call(
        functools.partial(pair_kernel, acc is None),
        out_shape=jax.ShapeDtypeStruct((24, slots), f32),
        in_specs=[VMEM] * len(operands),
        out_specs=VMEM,
        scratch_shapes=[pltpu.VMEM((24, slots), f32)] + pair_scratch(blocks, stars, slots),
        compiler_params=PARAMS,
        cost_estimate=cost(blocks, stars, slots),
        name="pairs_%d" % blocks,
    )(*operands)


def per_device(n, slots, pos_vel, acc_jerk, star_mass, step_phase, step_level, counts, star_order):
    stars = pos_vel.shape[1]
    row = lambda values: values.reshape(1, stars)
    own, old, factors = pl.pallas_call(
        functools.partial(prepare_kernel, slots),
        out_shape=(
            jax.ShapeDtypeStruct((8, stars), f32),
            jax.ShapeDtypeStruct((24, slots), f32),
            jax.ShapeDtypeStruct((FACTOR_ROWS, 2 * slots), bf16),
        ),
        in_specs=[SMEM] + [VMEM] * 6,
        out_specs=(VMEM,) * 3,
        compiler_params=PARAMS,
        name="prepare",
    )(counts, pos_vel, acc_jerk, row(star_mass), row(step_phase), row(step_level), star_order)

    def swap(values, bit):
        return lax.ppermute(values, "ja", [(i, i ^ bit) for i in range(n)])

    held, arrived, acc = own, own, None
    bit = n // 2
    while True:
        if bit > 1:
            coming = swap(held, bit)
        across = swap(arrived, 1)
        acc = call_pairs(arrived, factors, acc)
        if bit == 1:
            break
        acc = call_pairs(across, factors, acc)
        arrived = coming
        if bit > 2:
            held = jnp.concatenate([held, arrived], axis=0)
        bit //= 2

    blocks = across.shape[0] // 8
    return pl.pallas_call(
        finish_kernel,
        out_shape=(
            jax.ShapeDtypeStruct(pos_vel.shape, f32),
            jax.ShapeDtypeStruct(acc_jerk.shape, f32),
            jax.ShapeDtypeStruct((12, slots), f32),
        ),
        in_specs=[SMEM] + [VMEM] * 7,
        out_specs=(VMEM,) * 3,
        scratch_shapes=[pltpu.VMEM((24, slots), f32)] + pair_scratch(blocks, stars, slots),
        compiler_params=PARAMS,
        cost_estimate=cost(blocks, stars, slots),
        name="finish",
    )(counts, across, factors, acc, old, star_order, pos_vel, acc_jerk)


A_DEV = 128


def solution(mesh):
    in_specs = (
        P(None, ("runs", "ja")),
        P(None, ("runs", "ja")),
        P(("runs", "ja")),
        P(("runs", "ja")),
        P(("runs", "ja")),
        P(("runs", "ja")),
        P(("runs", "ja"), None),
    )
    out_specs = (P(None, ("runs", "ja")), P(None, ("runs", "ja")), P(None, ("runs", "ja")))
    return jax.shard_map(
        functools.partial(per_device, mesh.shape["ja"], 2 * A_DEV),
        mesh=mesh,
        in_specs=in_specs,
        out_specs=out_specs,
        check_vma=False,
    )
```

time: 163 us -> 33 us (0.20); the launches traced: 160 us -> 32.4 us
  other arithmetic: 50.4 us -> 0.02 us
  waiting for transfers between devices: 50.8 us -> 0.48 us
  blocking collectives: 32.1 us -> 0 us
  Pallas kernels: 0 us -> 18.7 us
  between operations: 14.8 us -> 1.42 us
  starting transfers between devices: 0.04 us -> 8.22 us
  local copies, waits for them, and re-layouts: 11.8 us -> 3.62 us
    reduce_scatter x1 -> x0, waiting for transfers between devices: 50.8 us -> none  [per_device(): fresh = lax.psum_scatter(every_slot, 'ja', scatter_dimension=1, tiled=True)]
    all_gather x1 -> x0, blocking collectives: 32.1 us -> none  [per_device(): lax.all_gather(targets, 'ja', axis=1, tiled=True)]
    reduce_sum x8 -> x0, other arithmetic: 20 us -> none  [pair_block(): accel_part = jnp.sum(weight[None] * delta_x, axis=2)]
    pallas_call x0 -> x9, Pallas kernels: none -> 18.7 us  [the longest x7 13.1 us: call_pairs(): pl.pallas_call(functools.partial(pair_kernel, acc is None), out_shape=jax...]
    mul x10 -> x0, other arithmetic: 17.4 us -> none  [the longest x8 16.6 us: pair_block(): radial[None] * delta_x]
    sub x8 -> x0, other arithmetic: 8.53 us -> none  [pair_block(): delta_v = sources[3:6, None, :] - targets[3:6, :, None]]
    ppermute x0 -> x7, starting transfers between devices: none -> 8.22 us  [swap(): return lax.ppermute(values, 'ja', [(i, i ^ bit) for i in range(n)])]
    scatter x3 -> x0, local copies, waits for them, and re-layouts: 4.15 us -> none  [the longest x1 1.41 us: per_device(): jnp.zeros((per_owner,), jnp.float32).at[slot_ids]]
  transfers between devices with their start and end apart: 1 -> 7, of which waited for: 1 -> 1; matrix products, arithmetic and copies ran while one was open for 2% -> 0% of each run, Pallas kernels for 0% -> 40%
where the time goes in v1:
time: 33 us; the launch traced here: 32.4 us
  Pallas kernels  18.7 us (57%)
  starting transfers between devices  8.22 us (25%)
  local copies, waits for them, and re-layouts  3.62 us (11%)
  between operations  1.42 us (4%)
  waiting for transfers between devices  0.48 us (1%)
    pallas_call x7, Pallas kernels, call_pairs(): pl.pallas_call(functools.partial(pair_kernel, acc is None), out_shape=jax...  13.1 us
    ppermute x7, starting transfers between devices, swap(): return lax.ppermute(values, 'ja', [(i, i ^ bit) for i in range(n)])  8.22 us
    pallas_call x1, Pallas kernels, per_device(): pl.pallas_call(finish_kernel, out_shape=(jax.ShapeDtypeStruct(pos_vel.sha...  5.02 us
    unnamed x18, local copies, waits for them, and re-layouts  3.62 us
  transfers between devices with their start and end apart: 7, of which 1 were waited for; matrix products, arithmetic and copies ran while one was open for 0% of the time, Pallas kernels for 40%

profile of v1, /device:TPU:1, one launch (start us, length us, event | category | flops | bytes accessed | tf_op | source)
XLA Modules:
  0.0 32.4 jit_solution(5742504246899742854)
XLA Ops:
  1.3 0.0 copy-done.4
  1.3 0.8 %copy-done = f32[6,1024]{1,0:T(8,128)S(1)} copy-done((f32[6,1024]{1,0:T(8,128)S(1)}, f32[6,1024]{1,0:T(8,128)}, u32[]{:S(2)}) %copy-start) | copy-done | bytes 24600
  2.1 0.8 %copy-done.2 = f32[6,1024]{1,0:T(8,128)S(1)} copy-done((f32[6,1024]{1,0:T(8,128)S(1)}, f32[6,1024]{1,0:T(8,128)}, u32[]{:S(2)}) %copy-start.2) | copy-done | bytes 24600
  2.8 0.7 %copy-done.5 = f32[1024]{0:T(1024)S(1)} copy-done((f32[1024]{0:T(1024)S(1)}, f32[1024]{0:T(1024)}, u32[]{:S(2)}) %copy-start.5) | copy-done | bytes 4120
  3.5 0.7 %copy-done.6 = s32[1024]{0:T(1024)S(1)} copy-done((s32[1024]{0:T(1024)S(1)}, s32[1024]{0:T(1024)}, u32[]{:S(2)}) %copy-start.6) | copy-done | bytes 4120
  4.2 0.7 %copy-done.7 = s32[1,1024]{1,0:T(1,128)S(1)} copy-done((s32[1,1024]{1,0:T(1,128)S(1)}, s32[1,1024]{1,0:T(1,128)}, u32[]{:S(2)}) %copy-start.7) | copy-done | bytes 4120
  4.9 0.6 %prepare.1 = (f32[8,1024]{1,0:T(8,128)S(1)}, f32[24,256]{1,0:T(8,128)S(1)}, bf16[64,512]{1,0:T(8,128)(2,1)S(1)}) custom-call(s32[1]{0:T(128)S(6)} %copy.10.count_ref, f32[6,1024]{1,0:T(8,128)S(1)} %copy-done, f32[6,1024]{1,0:T(8,128)S(1)} %copy-done.2, f32[1,1024]{1,0:T(1,128)S(1)} %bitcast.3, f32[1,1024]{1,0:T(1,128)S(1)} %bitcast.4, ...), custom_call_target="tpu_custom_call" | custom-call | tf_op jit(solution)/shard_map/prepare/pallas_call | solution.py:261
  5.5 0.1 collective-permute-start.6
  5.6 3.8 %collective-permute-start = (f32[8,1024]{1,0:T(8,128)S(1)}, f32[8,1024]{1,0:T(8,128)S(1)}, u32[]{:S(2)}, u32[]{:S(2)}) collective-permute-start(f32[8,1024]{1,0:T(8,128)S(1)} %get-tuple-element.6.src_ref), channel_id=1, source_target_pairs={{0,8},{1,9},{2,10},{3,11},{4,12},{5,13},{6,14},{7,15},{8,0},{9,1},... | collective-permute-start | bytes 98312 | tf_op jit(solution)/shard_map/ppermute | solution.py:275
  9.4 1.2 %pairs_1.4.refs_0_ = f32[24,256]{1,0:T(8,128)S(1)} custom-call(f32[8,1024]{1,0:T(8,128)S(1)} %get-tuple-element.6.src_ref, bf16[64,512]{1,0:T(8,128)(2,1)S(1)} %get-tuple-element.7.fac_ref), custom_call_target="tpu_custom_call" | custom-call | flops 805306368 | bytes 65536 | tf_op jit(solution)/shard_map/pairs_1/pallas_call | solution.py:246
  10.6 0.5 %collective-permute-done.src_ref = f32[8,1024]{1,0:T(8,128)S(1)} collective-permute-done((f32[8,1024]{1,0:T(8,128)S(1)}, f32[8,1024]{1,0:T(8,128)S(1)}, u32[]{:S(2)}, u32[]{:S(2)}) %collective-permute-start) | collective-permute-done | bytes 32800 | tf_op jit(solution)/shard_map/ppermute | solution.py:275
  11.1 1.0 %collective-permute-start.1 = (f32[16,1024]{1,0:T(8,128)S(1)}, f32[16,1024]{1,0:T(8,128)S(1)}, u32[]{:S(2)}, u32[]{:S(2)}) collective-permute-start(f32[16,1024]{1,0:T(8,128)S(1)} %pad_maximum_fusion.1), channel_id=1, source_target_pairs={{0,4},{1,5},{2,6},{3,7},{4,0},{5,1},{6,2},{7,3},{8,12},{9,13},{10,... | collective-permute-start | bytes 196616 | tf_op jit(solution)/shard_map/ppermute | solution.py:275
  12.1 1.5 %collective-permute-start.5 = (f32[8,1024]{1,0:T(8,128)S(1)}, f32[8,1024]{1,0:T(8,128)S(1)}, u32[]{:S(2)}, u32[]{:S(2)}) collective-permute-start(f32[8,1024]{1,0:T(8,128)S(1)} %collective-permute-done.src_ref), channel_id=1, source_target_pairs={{0,1},{1,0},{2,3},{3,2},{4,5},{5,4},{6,7},{7,6},{8,9},{9,8},{10,11... | collective-permute-start | bytes 98312 | tf_op jit(solution)/shard_map/ppermute | solution.py:275
  13.6 1.2 %pairs_1.5.refs_0_ = f32[24,256]{1,0:T(8,128)S(1)} custom-call(f32[8,1024]{1,0:T(8,128)S(1)} %collective-permute-done.6.src_ref, bf16[64,512]{1,0:T(8,128)(2,1)S(1)} %get-tuple-element.7.fac_ref, f32[24,256]{1,0:T(8,128)S(1)} %pairs_1.4.refs_0_), custom_call_target="tpu_custom_call" | custom-call | flops 805306368 | bytes 65536 | tf_op jit(solution)/shard_map/pairs_1/pallas_call | solution.py:246
  14.8 1.2 %pairs_1.6.refs_0_ = f32[24,256]{1,0:T(8,128)S(1)} custom-call(f32[8,1024]{1,0:T(8,128)S(1)} %collective-permute-done.src_ref, bf16[64,512]{1,0:T(8,128)(2,1)S(1)} %get-tuple-element.7.fac_ref, f32[24,256]{1,0:T(8,128)S(1)} %pairs_1.5.refs_0_), custom_call_target="tpu_custom_call" | custom-call | flops 805306368 | bytes 65536 | tf_op jit(solution)/shard_map/pairs_1/pallas_call | solution.py:246
  16.0 1.2 %pairs_1.7.refs_0_ = f32[24,256]{1,0:T(8,128)S(1)} custom-call(f32[8,1024]{1,0:T(8,128)S(1)} %collective-permute-done.5.src_ref, bf16[64,512]{1,0:T(8,128)(2,1)S(1)} %get-tuple-element.7.fac_ref, f32[24,256]{1,0:T(8,128)S(1)} %pairs_1.6.refs_0_), custom_call_target="tpu_custom_call" | custom-call | flops 805306368 | bytes 65536 | tf_op jit(solution)/shard_map/pairs_1/pallas_call | solution.py:246
  17.3 1.3 %collective-permute-start.2 = (f32[32,1024]{1,0:T(8,128)S(1)}, f32[32,1024]{1,0:T(8,128)S(1)}, u32[]{:S(2)}, u32[]{:S(2)}) collective-permute-start(f32[32,1024]{1,0:T(8,128)S(1)} %pad_maximum_fusion), channel_id=1, source_target_pairs={{0,2},{1,3},{2,0},{3,1},{4,6},{5,7},{6,4},{7,5},{8,10},{9,11},{10,... | collective-permute-start | bytes 393224 | tf_op jit(solution)/shard_map/ppermute | solution.py:275
  18.6 0.3 collective-permute-start.4
  18.9 2.0 %pairs_2.2.refs_0_ = f32[24,256]{1,0:T(8,128)S(1)} custom-call(f32[16,1024]{1,0:T(8,128)S(1)} %collective-permute-done.1.src_ref, bf16[64,512]{1,0:T(8,128)(2,1)S(1)} %get-tuple-element.7.fac_ref, f32[24,256]{1,0:T(8,128)S(1)} %pairs_1.7.refs_0_), custom_call_target="tpu_custom_call" | custom-call | flops 1610612736 | bytes 131072 | tf_op jit(solution)/shard_map/pairs_2/pallas_call | solution.py:246
  20.9 2.0 %pairs_2.3.refs_0_ = f32[24,256]{1,0:T(8,128)S(1)} custom-call(f32[16,1024]{1,0:T(8,128)S(1)} %collective-permute-done.4.src_ref, bf16[64,512]{1,0:T(8,128)(2,1)S(1)} %get-tuple-element.7.fac_ref, f32[24,256]{1,0:T(8,128)S(1)} %pairs_2.2.refs_0_), custom_call_target="tpu_custom_call" | custom-call | flops 1610612736 | bytes 131072 | tf_op jit(solution)/shard_map/pairs_2/pallas_call | solution.py:246
  22.9 0.0 copy-start.3
  23.0 0.3 collective-permute-start.3
  23.3 4.1 %pairs_4.1.in_ref = f32[24,256]{1,0:T(8,128)S(1)} custom-call(f32[32,1024]{1,0:T(8,128)S(1)} %collective-permute-done.2.src_ref, bf16[64,512]{1,0:T(8,128)(2,1)S(1)} %get-tuple-element.7.fac_ref, f32[24,256]{1,0:T(8,128)S(1)} %pairs_2.3.refs_0_), custom_call_target="tpu_custom_call" | custom-call | flops 3221225472 | bytes 262144 | tf_op jit(solution)/shard_map/pairs_4/pallas_call | solution.py:246
  27.4 5.0 %finish.1 = (f32[6,1024]{1,0:T(8,128)}, f32[6,1024]{1,0:T(8,128)}, f32[12,256]{1,0:T(8,128)}) custom-call(s32[1]{0:T(128)S(6)} %copy.10.count_ref, f32[32,1024]{1,0:T(8,128)S(1)} %collective-permute-done.3.src_ref, bf16[64,512]{1,0:T(8,128)(2,1)S(1)} %get-tuple-element.7.fac_ref, f32[24,256]{1,0:T(8,128)S(1)} %pairs_4.1.in_ref, ...), custom_call_target="tpu_custom_call" | custom-call | flops 3221225472 | bytes 262144 | tf_op jit(solution)/shard_map/finish/pallas_call | solution.py:293
  (19 shorter events, 0.1 us)
Async XLA Ops:
  0.6 0.7 %copy-start.4 = (f32[1024]{0:T(1024)S(1)}, f32[1024]{0:T(1024)}, u32[]{:S(2)}) copy-start(f32[1024]{0:T(1024)} %param.9) | copy-start | bytes 12292
  1.3 0.8 %copy-start = (f32[6,1024]{1,0:T(8,128)S(1)}, f32[6,1024]{1,0:T(8,128)}, u32[]{:S(2)}) copy-start(f32[6,1024]{1,0:T(8,128)} %pv_ref.3) | copy-start | bytes 73732
  2.1 0.8 %copy-start.2 = (f32[6,1024]{1,0:T(8,128)S(1)}, f32[6,1024]{1,0:T(8,128)}, u32[]{:S(2)}) copy-start(f32[6,1024]{1,0:T(8,128)} %aj_ref.3) | copy-start | bytes 73732
  2.8 0.7 %copy-start.5 = (f32[1024]{0:T(1024)S(1)}, f32[1024]{0:T(1024)}, u32[]{:S(2)}) copy-start(f32[1024]{0:T(1024)} %param.10) | copy-start | bytes 12292
  3.5 0.7 %copy-start.6 = (s32[1024]{0:T(1024)S(1)}, s32[1024]{0:T(1024)}, u32[]{:S(2)}) copy-start(s32[1024]{0:T(1024)} %param.11) | copy-start | bytes 12292
  4.2 0.7 %copy-start.7 = (s32[1,1024]{1,0:T(1,128)S(1)}, s32[1,1024]{1,0:T(1,128)}, u32[]{:S(2)}) copy-start(s32[1,1024]{1,0:T(1,128)} %order_ref.3) | copy-start | bytes 12292
  5.5 8.0 %collective-permute-start.6 = (f32[8,1024]{1,0:T(8,128)S(1)}, f32[8,1024]{1,0:T(8,128)S(1)}, u32[]{:S(2)}, u32[]{:S(2)}) collective-permute-start(f32[8,1024]{1,0:T(8,128)S(1)} %get-tuple-element.6.src_ref), channel_id=1, source_target_pairs={{0,1},{1,0},{2,3},{3,2},{4,5},{5,4},{6,7},{7,6},{8,9},{9,8},{10,11... | collective-permute-start | bytes 98312 | tf_op jit(solution)/shard_map/ppermute | solution.py:275
  5.6 5.4 %collective-permute-start = (f32[8,1024]{1,0:T(8,128)S(1)}, f32[8,1024]{1,0:T(8,128)S(1)}, u32[]{:S(2)}, u32[]{:S(2)}) collective-permute-start(f32[8,1024]{1,0:T(8,128)S(1)} %get-tuple-element.6.src_ref), channel_id=1, source_target_pairs={{0,8},{1,9},{2,10},{3,11},{4,12},{5,13},{6,14},{7,15},{8,0},{9,1},... | collective-permute-start | bytes 98312 | tf_op jit(solution)/shard_map/ppermute | solution.py:275
  11.1 6.2 %collective-permute-start.1 = (f32[16,1024]{1,0:T(8,128)S(1)}, f32[16,1024]{1,0:T(8,128)S(1)}, u32[]{:S(2)}, u32[]{:S(2)}) collective-permute-start(f32[16,1024]{1,0:T(8,128)S(1)} %pad_maximum_fusion.1), channel_id=1, source_target_pairs={{0,4},{1,5},{2,6},{3,7},{4,0},{5,1},{6,2},{7,3},{8,12},{9,13},{10,... | collective-permute-start | bytes 196616 | tf_op jit(solution)/shard_map/ppermute | solution.py:275
  12.1 3.9 %collective-permute-start.5 = (f32[8,1024]{1,0:T(8,128)S(1)}, f32[8,1024]{1,0:T(8,128)S(1)}, u32[]{:S(2)}, u32[]{:S(2)}) collective-permute-start(f32[8,1024]{1,0:T(8,128)S(1)} %collective-permute-done.src_ref), channel_id=1, source_target_pairs={{0,1},{1,0},{2,3},{3,2},{4,5},{5,4},{6,7},{7,6},{8,9},{9,8},{10,11... | collective-permute-start | bytes 98312 | tf_op jit(solution)/shard_map/ppermute | solution.py:275
  17.3 5.7 %collective-permute-start.2 = (f32[32,1024]{1,0:T(8,128)S(1)}, f32[32,1024]{1,0:T(8,128)S(1)}, u32[]{:S(2)}, u32[]{:S(2)}) collective-permute-start(f32[32,1024]{1,0:T(8,128)S(1)} %pad_maximum_fusion), channel_id=1, source_target_pairs={{0,2},{1,3},{2,0},{3,1},{4,6},{5,7},{6,4},{7,5},{8,10},{9,11},{10,... | collective-permute-start | bytes 393224 | tf_op jit(solution)/shard_map/ppermute | solution.py:275
  18.6 2.3 %collective-permute-start.4 = (f32[16,1024]{1,0:T(8,128)S(1)}, f32[16,1024]{1,0:T(8,128)S(1)}, u32[]{:S(2)}, u32[]{:S(2)}) collective-permute-start(f32[16,1024]{1,0:T(8,128)S(1)} %collective-permute-done.1.src_ref), channel_id=1, source_target_pairs={{0,1},{1,0},{2,3},{3,2},{4,5},{5,4},{6,7},{7,6},{8,9},{9,8},{10,11... | collective-permute-start | bytes 196616 | tf_op jit(solution)/shard_map/ppermute | solution.py:275
  22.9 4.5 %copy-start.1 = (f32[6,1024]{1,0:T(8,128)S(1)}, f32[6,1024]{1,0:T(8,128)}, u32[]{:S(2)}) copy-start(f32[6,1024]{1,0:T(8,128)} %pv_ref.3) | copy-start | bytes 73732
  22.9 4.5 %copy-start.3 = (f32[6,1024]{1,0:T(8,128)S(1)}, f32[6,1024]{1,0:T(8,128)}, u32[]{:S(2)}) copy-start(f32[6,1024]{1,0:T(8,128)} %aj_ref.3) | copy-start | bytes 73732
  22.9 4.5 %copy-start.8 = (s32[1,1024]{1,0:T(1,128)S(1)}, s32[1,1024]{1,0:T(1,128)}, u32[]{:S(2)}) copy-start(s32[1,1024]{1,0:T(1,128)} %order_ref.3) | copy-start | bytes 12292
  23.0 4.4 %collective-permute-start.3 = (f32[32,1024]{1,0:T(8,128)S(1)}, f32[32,1024]{1,0:T(8,128)S(1)}, u32[]{:S(2)}, u32[]{:S(2)}) collective-permute-start(f32[32,1024]{1,0:T(8,128)S(1)} %collective-permute-done.2.src_ref), channel_id=1, source_target_pairs={{0,1},{1,0},{2,3},{3,2},{4,5},{5,4},{6,7},{7,6},{8,9},{9,8},{10,11... | collective-permute-start | bytes 393224 | tf_op jit(solution)/shard_map/ppermute | solution.py:275

commit v2 on v1

--- a/solution.py
+++ b/solution.py
@@ -12,9 +12,10 @@
 f32 = jnp.float32
 bf16 = jnp.bfloat16
 
-CHUNK = 256
-FACTOR_ROWS = 64
-PARAMS = pltpu.CompilerParams(vmem_limit_bytes=48 << 20)
+CHUNK = 128
+TOGETHER = 4
+FACTOR_ROWS = 128
+PARAMS = pltpu.CompilerParams(vmem_limit_bytes=32 << 20)
 
 
 def round_bf16(values):
@@ -30,77 +31,91 @@
     return out + [round_bf16(values)]
 
 
-def dot3(a, b):
-    return a[0:1] * b[0:1] + a[1:2] * b[1:2] + a[2:3] * b[2:3]
-
-
-def star_pieces(state):
-    x, u = state[0:3], state[3:6]
-    grid = jnp.floor(x * 4.0 + 0.5) * 0.25
-    low = x - grid
-    low1 = round_bf16(low)
-    low2 = round_bf16(low - low1)
-    low = low1 + low2
-    return (
-        grid,
-        low1,
-        low2,
-        split(u, 3),
-        split(dot3(grid, grid), 2),
-        2.0 * dot3(grid, low) + dot3(low, low),
-        dot3(grid + low, u),
-    )
+def four_terms(state):
+    grid = jnp.floor(state * 4.0 + 0.5) * 0.25
+    low = state - grid
+    low1, low2, low3 = split(low, 3)
+    return grid, low1, low2, low3, low
+
+
+def row_index(state):
+    return lax.broadcasted_iota(jnp.int32, state.shape, 0)
+
+
+def down3(state):
+    return jnp.concatenate([state[5:8], state[0:5]], axis=0)
 
 
 def source_factors(state):
-    grid, low1, low2, (u1, u2, u3), grid_sq, rest, xu = star_pieces(state)
-    one = jnp.ones_like(state[0:1])
-    rows = [grid] + grid_sq + [one] * 2 + split(rest, 3) + [one] * 3
-    rows += [grid] * 2 + [low1] * 3 + [low2] * 2 + [u1] * 3 + [u2] * 2 + [u3] + split(xu, 3)
-    used = sum(r.shape[0] for r in rows)
-    return jnp.concatenate(rows + [jnp.zeros((FACTOR_ROWS - used, state.shape[1]), f32)], axis=0)
+    row = row_index(state)
+    grid, low1, low2, low3, low = four_terms(state)
+    square = jnp.where(row == 6, 1.0, grid * grid)
+    rest = jnp.where(row < 3, (2.0 * grid + low) * low, (grid + low) * down3(grid + low))
+    rest1, rest2, rest3 = [jnp.where(row == 6, 1.0, term) for term in split(rest, 3)]
+    square1 = round_bf16(square)
+    square2 = jnp.where(row == 6, 1.0, square - square1)
+    groups = [grid, square1, square2, grid, grid, grid, low1, low1, low1, low2, low2, low3, rest1, rest2, rest3]
+    pad = [jnp.zeros_like(state)] * (FACTOR_ROWS // 8 - len(groups))
+    return jnp.concatenate(groups + pad, axis=0).astype(bf16)
 
 
 def target_factors(state):
-    grid, low1, low2, (u1, u2, u3), grid_sq, rest, xu = star_pieces(state)
-    one = jnp.ones_like(state[0:1])
-    z1, z3 = jnp.zeros_like(one), jnp.zeros_like(grid)
-    dist = [-2.0 * grid] + [one] * 2 + grid_sq + [one] * 3 + split(rest + soft_sq, 3)
-    dist += [-2.0 * low1, -2.0 * low2, -2.0 * grid, -2.0 * low1, -2.0 * low2, -2.0 * grid, -2.0 * low1]
-    dist += [z3] * 6 + [z1] * 3
-    radial = [-u1] + [z1] * 7 + split(xu, 3)
-    radial += [-u2, -u3, -u1, -u2, z3, -u1, z3]
-    radial += [-grid, -low1, -low2, -grid, -low1, -grid] + [one] * 3
-    used = sum(r.shape[0] for r in dist)
-    pad = [jnp.zeros((FACTOR_ROWS - used, state.shape[1]), f32)]
+    grid, low1, low2, low3, low = four_terms(state)
+    zero, one = jnp.zeros_like(state), jnp.ones_like(state)
+    z1, z2, z3 = zero[0:1], zero[0:2], zero[0:3]
+
+    def add3(values):
+        return values[0:1] + values[1:2] + values[2:3]
+
+    def near(values):
+        return jnp.concatenate([-2.0 * values[0:3], z3, z2], axis=0)
+
+    def crossed(values):
+        return jnp.concatenate([-values[3:6], -values[0:3], z2], axis=0)
+
+    def sums(first, second, scalar):
+        return jnp.concatenate([first, second, scalar, z1], axis=0)
+
+    square1, square2 = split(add3(grid[0:3] * grid[0:3]), 2)
+    rest = split(add3((2.0 * grid[0:3] + low[0:3]) * low[0:3]) + soft_sq, 3)
+    moved = split(add3((grid + low)[0:3] * (grid + low)[3:6]), 3)
+    o3 = one[0:3]
+    dist = [near(grid), sums(o3, z3, square1), sums(o3, z3, square2), near(low1), near(low2), near(low3)]
+    dist += [near(grid), near(low1), near(low2), near(grid), near(low1), near(grid)]
+    dist += [sums(o3, z3, term) for term in rest]
+    radial = [crossed(grid), zero, zero, crossed(low1), crossed(low2), crossed(low3)]
+    radial += [crossed(grid), crossed(low1), crossed(low2), crossed(grid), crossed(low1), crossed(grid)]
+    radial += [sums(z3, o3, term) for term in moved]
+    pad = [zero] * (FACTOR_ROWS // 8 - len(dist))
     return jnp.concatenate(
         [jnp.concatenate(radial + pad, axis=0), jnp.concatenate(dist + pad, axis=0)], axis=1
-    )
+    ).astype(bf16)
 
 
 def sum_factors(state):
-    mass = state[6:7]
-    mass_x, mass_u = mass * state[0:3], mass * state[3:6]
-    by_weight = jnp.concatenate([mass_x, mass_u, mass, jnp.zeros_like(mass)], axis=0)
-    by_radial = jnp.concatenate(
-        [jnp.zeros_like(mass_x), -3.0 * mass_x, jnp.zeros_like(mass), 3.0 * mass], axis=0
-    )
+    row = row_index(state)
+    mass = jnp.broadcast_to(state[6:7], state.shape)
+    by_weight = mass * jnp.where(row < 6, state, jnp.where(row == 6, 1.0, 0.0))
+    by_radial = mass * jnp.where(row < 3, 0.0, jnp.where(row < 6, -3.0 * down3(state), jnp.where(row == 7, 3.0, 0.0)))
     return (
         jnp.concatenate(split(by_weight, 3), axis=0).astype(bf16),
         jnp.concatenate(split(by_radial, 3), axis=0).astype(bf16),
     )
 
 
-def add_pairs(state, factors_t, acc_ref, products, weights):
+def add_pairs(states, factors_t, acc_ref, products, weights):
     slots = factors_t.shape[1] // 2
-    chunks = state.shape[1] // CHUNK
-    factors_s = source_factors(state).T.astype(bf16)
-    by_weight, by_radial = sum_factors(state)
+    per = states[0].shape[1] // CHUNK
+    ready = {}
+
+    def prepare(b):
+        ready[b] = (source_factors(states[b]).T,) + sum_factors(states[b])
+
+    def span(c):
+        return slice(c % per * CHUNK, (c % per + 1) * CHUNK)
 
     def multiply(c):
-        products[c][...] = jnp.dot(
-            factors_s[c * CHUNK : (c + 1) * CHUNK], factors_t, preferred_element_type=f32
-        )
+        products[c][...] = jnp.dot(ready[c // per][0][span(c)], factors_t, preferred_element_type=f32)
 
     def weigh(c):
         for g in range(0, CHUNK, 16):
@@ -119,12 +134,16 @@
                 weights[c][3 * CHUNK + g : 3 * CHUNK + g + 16, cols] = (radial - radial_hi.astype(f32)).astype(bf16)
 
     def total(c):
-        span = slice(c * CHUNK, (c + 1) * CHUNK)
-        left = [by_weight[:, span]] * 2 + [by_radial[:, span]] * 2
+        _, by_weight, by_radial = ready[c // per]
+        left = [by_weight[:, span(c)]] * 2 + [by_radial[:, span(c)]] * 2
         acc_ref[...] += jnp.dot(jnp.concatenate(left, axis=1), weights[c][...], preferred_element_type=f32)
 
+    chunks = len(states) * per
+    prepare(0)
     multiply(0)
     for c in range(chunks):
+        if (c + 2) % per == 0 and (c + 2) // per < len(states):
+            prepare((c + 2) // per)
         if c + 1 < chunks:
             multiply(c + 1)
         weigh(c)
@@ -133,13 +152,17 @@
     total(chunks - 1)
 
 
+def blocks_together(blocks):
+    return next(t for t in range(TOGETHER, 0, -1) if blocks % t == 0)
+
+
 def add_blocks(sources_ref, factors_t, acc_ref, products, weights):
     blocks = sources_ref.shape[0] // 8
-    together = 2 if blocks % 2 == 0 else 1
+    together = blocks_together(blocks)
 
     def step(i, _):
         rows = [sources_ref[pl.ds(pl.multiple_of((i * together + b) * 8, 8), 8), :] for b in range(together)]
-        add_pairs(jnp.concatenate(rows, axis=1), factors_t, acc_ref, products, weights)
+        add_pairs(rows, factors_t, acc_ref, products, weights)
         return 0
 
     if blocks == together:
@@ -149,7 +172,7 @@
 
 
 def pair_scratch(blocks, stars, slots):
-    chunks = stars * (2 if blocks % 2 == 0 else 1) // CHUNK
+    chunks = stars * blocks_together(blocks) // CHUNK
     return [pltpu.VMEM((CHUNK, 2 * slots), f32)] * chunks + [pltpu.VMEM((4 * CHUNK, slots), bf16)] * chunks
 
 
@@ -174,23 +197,42 @@
     return out[0:height] + out[height : 2 * height] + out[2 * height : 3 * height]
 
 
-def prepare_kernel(slots, count_ref, pv_ref, aj_ref, mass_ref, phase_ref, level_ref, order_ref, src_ref, old_ref, fac_ref):
+def fetch(pairs, sems):
+    copies = [pltpu.make_async_copy(src, dst, sems.at[i]) for i, (src, dst) in enumerate(pairs)]
+    for copy in copies:
+        copy.start()
+
+    def wait(*places):
+        for i in places:
+            copies[i].wait()
+
+    return wait
+
+
+def prepare_kernel(slots, count_hbm, pv_hbm, aj_hbm, mass_hbm, phase_hbm, level_hbm, order_hbm, src_ref, old_ref, fac_ref, count_ref, pv_ref, aj_ref, mass_ref, phase_ref, level_ref, order_ref, sems):
+    hbm = (order_hbm, count_hbm, phase_hbm, level_hbm, mass_hbm, pv_hbm, aj_hbm)
+    here = (order_ref, count_ref, phase_ref, level_ref, mass_ref, pv_ref, aj_ref)
+    wait = fetch(tuple(zip(hbm, here)), sems)
     stars = pv_ref.shape[1]
+    wait(0, 1)
     hot = one_hot(order_ref, stars, slots)
     active = spread(hot, live_slots(count_ref, slots))
+    wait(2, 3, 4, 5, 6)
     level = level_ref[...]
     step_len = base_step * jnp.where((level & 1) > 0, 0.5, 1.0) * jnp.where((level & 2) > 0, 0.25, 1.0)
     age = step_len * jnp.where(active > 0.5, 1.0, phase_ref[...])
     half_sq = 0.5 * age * age
     sixth_cube = age * age * age / 6.0
-    x, v, a, j = pv_ref[0:3], pv_ref[3:6], aj_ref[0:3], aj_ref[3:6]
+    pv, aj = pv_ref[...], aj_ref[...]
+    x, v, a, j = pv[0:3], pv[3:6], aj[0:3], aj[3:6]
     position = x + age * v + half_sq * a + sixth_cube * j
     velocity = v + age * a + half_sq * j
-    src_ref[...] = jnp.concatenate([position, velocity, mass_ref[...], step_len], axis=0)
-    rows = jnp.concatenate([position, velocity, step_len, jnp.zeros_like(step_len), x, v, a, j, x, a[0:1]], axis=0)
-    old = exact_product(rows[0:24], hot, 0)
+    state = jnp.concatenate([position, velocity, mass_ref[...], step_len], axis=0)
+    src_ref[...] = state
+    gap = jnp.zeros((2, stars), f32)
+    old = exact_product(jnp.concatenate([state, pv, gap, aj, gap], axis=0), hot, 0)
     old_ref[...] = old
-    fac_ref[...] = target_factors(old[0:8]).astype(bf16)
+    fac_ref[...] = target_factors(old[0:8])
 
 
 def pair_kernel(fresh, src_ref, fac_ref, *refs):
@@ -205,21 +247,23 @@
     out_ref[...] = acc_ref[...]
 
 
-def finish_kernel(count_ref, src_ref, fac_ref, in_ref, old_ref, order_ref, pv_ref, aj_ref, new_pv_ref, new_aj_ref, state_ref, acc_ref, *scratch):
+def finish_kernel(count_hbm, src_ref, fac_ref, in_ref, old_ref, order_hbm, pv_hbm, aj_hbm, new_pv_ref, new_aj_ref, state_ref, count_ref, order_ref, pv_ref, aj_ref, sems, acc_ref, *scratch):
+    wait = fetch(((count_hbm, count_ref), (order_hbm, order_ref), (pv_hbm, pv_ref), (aj_hbm, aj_ref)), sems)
     stars, slots = pv_ref.shape[1], in_ref.shape[1]
     acc_ref[...] = in_ref[...]
     half = len(scratch) // 2
     add_blocks(src_ref, fac_ref[...], acc_ref, scratch[:half], scratch[half:])
     sums = acc_ref[0:8] + acc_ref[8:16] + acc_ref[16:24]
-    here, there = old_ref[0:3], old_ref[3:6]
+    old = old_ref[...]
+    here, there, step_len = old[0:3], old[3:6], old[7:8]
     a1 = sums[0:3] - here * sums[6:7]
     j1 = sums[3:6] - there * sums[6:7] + here * sums[7:8]
-    step_len = old_ref[6:7]
-    x0, v0, a0, j0 = old_ref[8:11], old_ref[11:14], old_ref[14:17], old_ref[17:20]
+    x0, v0, a0, j0 = old[8:11], old[11:14], old[16:19], old[19:22]
     half_step = 0.5 * step_len
     twelfth = step_len * step_len / 12.0
     v1 = v0 + half_step * (a0 + a1) + twelfth * (j0 - j1)
     x1 = x0 + half_step * (v0 + v1) + twelfth * (a0 - a1)
+    wait(0, 1, 2, 3)
     live = live_slots(count_ref, slots)
     state = jnp.where(live > 0.5, jnp.concatenate([x1, v1, a1, j1], axis=0), 0.0)
     state_ref[...] = state
@@ -232,7 +276,7 @@
 
 
 VMEM = pl.BlockSpec(memory_space=pltpu.VMEM)
-SMEM = pl.BlockSpec(memory_space=pltpu.SMEM)
+HBM = pl.BlockSpec(memory_space=pltpu.HBM)
 
 
 def cost(blocks, stars, slots):
@@ -265,8 +309,12 @@
             jax.ShapeDtypeStruct((24, slots), f32),
             jax.ShapeDtypeStruct((FACTOR_ROWS, 2 * slots), bf16),
         ),
-        in_specs=[SMEM] + [VMEM] * 6,
+        in_specs=[HBM] * 7,
         out_specs=(VMEM,) * 3,
+        scratch_shapes=[pltpu.SMEM((1,), jnp.int32), pltpu.VMEM(pos_vel.shape, f32), pltpu.VMEM(acc_jerk.shape, f32)]
+        + [pltpu.VMEM((1, stars), f32)] * 2
+        + [pltpu.VMEM((1, stars), jnp.int32)] * 2
+        + [pltpu.SemaphoreType.DMA((7,))],
         compiler_params=PARAMS,
         name="prepare",
     )(counts, pos_vel, acc_jerk, row(star_mass), row(step_phase), row(step_level), star_order)
@@ -284,7 +332,7 @@
         if bit == 1:
             break
         acc = call_pairs(across, factors, acc)
-        arrived = coming
+        arrived, acc = lax.optimization_barrier((coming, acc))
         if bit > 2:
             held = jnp.concatenate([held, arrived], axis=0)
         bit //= 2
@@ -297,9 +345,12 @@
             jax.ShapeDtypeStruct(acc_jerk.shape, f32),
             jax.ShapeDtypeStruct((12, slots), f32),
         ),
-        in_specs=[SMEM] + [VMEM] * 7,
+        in_specs=[HBM] + [VMEM] * 4 + [HBM] * 3,
         out_specs=(VMEM,) * 3,
-        scratch_shapes=[pltpu.VMEM((24, slots), f32)] + pair_scratch(blocks, stars, slots),
+        scratch_shapes=[pltpu.SMEM((1,), jnp.int32), pltpu.VMEM((1, stars), jnp.int32)]
+        + [pltpu.VMEM(pos_vel.shape, f32), pltpu.VMEM(acc_jerk.shape, f32), pltpu.SemaphoreType.DMA((4,))]
+        + [pltpu.VMEM((24, slots), f32)]
+        + pair_scratch(blocks, stars, slots),
         compiler_params=PARAMS,
         cost_estimate=cost(blocks, stars, slots),
         name="finish",

time: 33 us -> 33.3 us (level)
  Pallas kernels: 18.7 us -> 15.6 us
  waiting for transfers between devices: 0.48 us -> 3.3 us
  starting transfers between devices: 8.22 us -> 8.84 us
    pallas_call x7, Pallas kernels: 13.1 us -> 10.2 us  [call_pairs(): pl.pallas_call(functools.partial(pair_kernel, acc is None), out_shape=jax...]
    ppermute x7, waiting for transfers between devices: 0.48 us -> 3.3 us  [swap(): return lax.ppermute(values, 'ja', [(i, i ^ bit) for i in range(n)])]
    pallas_call x1, Pallas kernels: 5.02 us -> 4.2 us  [per_device(): pl.pallas_call(finish_kernel, out_shape=(jax.ShapeDtypeStruct(pos_vel.sha...]
    pallas_call x1, Pallas kernels: 0.62 us -> 1.24 us  [per_device(): pl.pallas_call(functools.partial(prepare_kernel, slots), out_shape=(jax.S...]
    ppermute x7, starting transfers between devices: 8.22 us -> 8.84 us  [swap(): return lax.ppermute(values, 'ja', [(i, i ^ bit) for i in range(n)])]
  transfers between devices with their start and end apart: 7 -> 7, of which waited for: 1 -> 2; matrix products, arithmetic and copies ran while one was open for 0% -> 0% of each run, Pallas kernels for 40% -> 31%
where the time goes in v2:
time: 33.3 us; the launch traced here: 33 us
  Pallas kernels  15.6 us (47%)
  starting transfers between devices  8.84 us (27%)
  local copies, waits for them, and re-layouts  3.62 us (11%)
  waiting for transfers between devices  3.3 us (10%)
  between operations  1.57 us (5%)
    pallas_call x7, Pallas kernels, call_pairs(): pl.pallas_call(functools.partial(pair_kernel, acc is None), out_shape=jax...  10.2 us
    ppermute x7, starting transfers between devices, swap(): return lax.ppermute(values, 'ja', [(i, i ^ bit) for i in range(n)])  8.84 us
    pallas_call x1, Pallas kernels, per_device(): pl.pallas_call(finish_kernel, out_shape=(jax.ShapeDtypeStruct(pos_vel.sha...  4.2 us
    unnamed x18, local copies, waits for them, and re-layouts  3.62 us
    ppermute x7, waiting for transfers between devices, swap(): return lax.ppermute(values, 'ja', [(i, i ^ bit) for i in range(n)])  3.3 us
    pallas_call x1, Pallas kernels, per_device(): pl.pallas_call(functools.partial(prepare_kernel, slots), out_shape=(jax.S...  1.24 us
  transfers between devices with their start and end apart: 7, of which 2 were waited for; matrix products, arithmetic and copies ran while one was open for 0% of the time, Pallas kernels for 31%

profile of v2, /device:TPU:1, one launch (start us, length us, event | category | flops | bytes accessed | tf_op | source)
XLA Modules:
  0.0 33.0 jit_solution(4487521278142124853)
XLA Ops:
  1.3 0.0 copy-done.4
  1.3 0.8 %copy-done = f32[6,1024]{1,0:T(8,128)S(1)} copy-done((f32[6,1024]{1,0:T(8,128)S(1)}, f32[6,1024]{1,0:T(8,128)}, u32[]{:S(2)}) %copy-start) | copy-done | bytes 24600
  2.1 0.8 %copy-done.2 = f32[6,1024]{1,0:T(8,128)S(1)} copy-done((f32[6,1024]{1,0:T(8,128)S(1)}, f32[6,1024]{1,0:T(8,128)}, u32[]{:S(2)}) %copy-start.2) | copy-done | bytes 24600
  2.8 0.7 %copy-done.5 = f32[1024]{0:T(1024)S(1)} copy-done((f32[1024]{0:T(1024)S(1)}, f32[1024]{0:T(1024)}, u32[]{:S(2)}) %copy-start.5) | copy-done | bytes 4120
  3.5 0.7 %copy-done.6 = s32[1024]{0:T(1024)S(1)} copy-done((s32[1024]{0:T(1024)S(1)}, s32[1024]{0:T(1024)}, u32[]{:S(2)}) %copy-start.6) | copy-done | bytes 4120
  4.2 0.7 %copy-done.7 = s32[1,1024]{1,0:T(1,128)S(1)} copy-done((s32[1,1024]{1,0:T(1,128)S(1)}, s32[1,1024]{1,0:T(1,128)}, u32[]{:S(2)}) %copy-start.7) | copy-done | bytes 4120
  4.9 1.2 %prepare.1 = (f32[8,1024]{1,0:T(8,128)S(1)}, f32[24,256]{1,0:T(8,128)S(1)}, bf16[128,512]{1,0:T(8,128)(2,1)S(1)}) custom-call(s32[1]{0:T(128)S(6)} %copy.10.count_hbm, f32[6,1024]{1,0:T(8,128)S(1)} %copy-done, f32[6,1024]{1,0:T(8,128)S(1)} %copy-done.2, f32[1,1024]{1,0:T(1,128)S(1)} %bitcast.3, f32[1,1024]{1,0:T(1,128)S(1)} %bitcast.4, ...), custom_call_target="tpu_custom_call" | custom-call | tf_op jit(solution)/shard_map/prepare/pallas_call | solution.py:305
  6.2 0.1 collective-permute-start.1
  6.3 3.8 %collective-permute-start = (f32[8,1024]{1,0:T(8,128)S(1)}, f32[8,1024]{1,0:T(8,128)S(1)}, u32[]{:S(2)}, u32[]{:S(2)}) collective-permute-start(f32[8,1024]{1,0:T(8,128)S(1)} %get-tuple-element.12.src_ref), channel_id=1, source_target_pairs={{0,8},{1,9},{2,10},{3,11},{4,12},{5,13},{6,14},{7,15},{8,0},{9,1},... | collective-permute-start | bytes 98312 | tf_op jit(solution)/shard_map/ppermute | solution.py:323
  10.0 1.0 %pairs_1.4.refs_0_ = f32[24,256]{1,0:T(8,128)S(1)} custom-call(f32[8,1024]{1,0:T(8,128)S(1)} %get-tuple-element.12.src_ref, bf16[128,512]{1,0:T(8,128)(2,1)S(1)} %get-tuple-element.13.fac_ref), custom_call_target="tpu_custom_call" | custom-call | flops 805306368 | bytes 65536 | tf_op jit(solution)/shard_map/pairs_1/pallas_call | solution.py:290
  11.1 1.0 %pairs_1.5.refs_0_ = f32[24,256]{1,0:T(8,128)S(1)} custom-call(f32[8,1024]{1,0:T(8,128)S(1)} %collective-permute-done.1.src_ref, bf16[128,512]{1,0:T(8,128)(2,1)S(1)} %get-tuple-element.13.fac_ref, f32[24,256]{1,0:T(8,128)S(1)} %pairs_1.4.refs_0_), custom_call_target="tpu_custom_call" | custom-call | flops 805306368 | bytes 65536 | tf_op jit(solution)/shard_map/pairs_1/pallas_call | solution.py:290
  12.1 0.4 %collective-permute-start.3 = (f32[8,1024]{1,0:T(8,128)S(1)}, f32[8,1024]{1,0:T(8,128)S(1)}, u32[]{:S(2)}, u32[]{:S(2)}) collective-permute-start(f32[8,1024]{1,0:T(8,128)S(1)} %collective-permute-done.src_ref), channel_id=1, source_target_pairs={{0,1},{1,0},{2,3},{3,2},{4,5},{5,4},{6,7},{7,6},{8,9},{9,8},{10,11... | collective-permute-start | bytes 98312 | tf_op jit(solution)/shard_map/ppermute | solution.py:323
  12.5 1.0 %pairs_1.6.refs_0_ = f32[24,256]{1,0:T(8,128)S(1)} custom-call(f32[8,1024]{1,0:T(8,128)S(1)} %collective-permute-done.src_ref, bf16[128,512]{1,0:T(8,128)(2,1)S(1)} %get-tuple-element.13.fac_ref, f32[24,256]{1,0:T(8,128)S(1)} %pairs_1.5.refs_0_), custom_call_target="tpu_custom_call" | custom-call | flops 805306368 | bytes 65536 | tf_op jit(solution)/shard_map/pairs_1/pallas_call | solution.py:290
  13.5 1.4 %collective-permute-start.2 = (f32[16,1024]{1,0:T(8,128)S(1)}, f32[16,1024]{1,0:T(8,128)S(1)}, u32[]{:S(2)}, u32[]{:S(2)}) collective-permute-start(f32[16,1024]{1,0:T(8,128)S(1)} %pad_maximum_fusion.1), channel_id=1, source_target_pairs={{0,4},{1,5},{2,6},{3,7},{4,0},{5,1},{6,2},{7,3},{8,12},{9,13},{10,... | collective-permute-start | bytes 196616 | tf_op jit(solution)/shard_map/ppermute | solution.py:323
  15.0 1.0 %pairs_1.7.refs_0_ = f32[24,256]{1,0:T(8,128)S(1)} custom-call(f32[8,1024]{1,0:T(8,128)S(1)} %collective-permute-done.3.src_ref, bf16[128,512]{1,0:T(8,128)(2,1)S(1)} %get-tuple-element.13.fac_ref, f32[24,256]{1,0:T(8,128)S(1)} %pairs_1.6.refs_0_), custom_call_target="tpu_custom_call" | custom-call | flops 805306368 | bytes 65536 | tf_op jit(solution)/shard_map/pairs_1/pallas_call | solution.py:290
  16.0 1.1 %collective-permute-done.2.src_ref = f32[16,1024]{1,0:T(8,128)S(1)} collective-permute-done((f32[16,1024]{1,0:T(8,128)S(1)}, f32[16,1024]{1,0:T(8,128)S(1)}, u32[]{:S(2)}, u32[]{:S(2)}) %collective-permute-start.2) | collective-permute-done | bytes 65568 | tf_op jit(solution)/shard_map/ppermute | solution.py:323
  17.1 1.0 %collective-permute-start.5 = (f32[16,1024]{1,0:T(8,128)S(1)}, f32[16,1024]{1,0:T(8,128)S(1)}, u32[]{:S(2)}, u32[]{:S(2)}) collective-permute-start(f32[16,1024]{1,0:T(8,128)S(1)} %collective-permute-done.2.src_ref), channel_id=1, source_target_pairs={{0,1},{1,0},{2,3},{3,2},{4,5},{5,4},{6,7},{7,6},{8,9},{9,8},{10,11... | collective-permute-start | bytes 196616 | tf_op jit(solution)/shard_map/ppermute | solution.py:323
  18.1 1.6 %pairs_2.2.refs_0_ = f32[24,256]{1,0:T(8,128)S(1)} custom-call(f32[16,1024]{1,0:T(8,128)S(1)} %collective-permute-done.2.src_ref, bf16[128,512]{1,0:T(8,128)(2,1)S(1)} %get-tuple-element.13.fac_ref, f32[24,256]{1,0:T(8,128)S(1)} %pairs_1.7.refs_0_), custom_call_target="tpu_custom_call" | custom-call | flops 1610612736 | bytes 131072 | tf_op jit(solution)/shard_map/pairs_2/pallas_call | solution.py:290
  19.7 1.4 %collective-permute-start.4 = (f32[32,1024]{1,0:T(8,128)S(1)}, f32[32,1024]{1,0:T(8,128)S(1)}, u32[]{:S(2)}, u32[]{:S(2)}) collective-permute-start(f32[32,1024]{1,0:T(8,128)S(1)} %pad_maximum_fusion), channel_id=1, source_target_pairs={{0,2},{1,3},{2,0},{3,1},{4,6},{5,7},{6,4},{7,5},{8,10},{9,11},{10,... | collective-permute-start | bytes 393224 | tf_op jit(solution)/shard_map/ppermute | solution.py:323
  21.1 1.6 %pairs_2.3.refs_0_ = f32[24,256]{1,0:T(8,128)S(1)} custom-call(f32[16,1024]{1,0:T(8,128)S(1)} %collective-permute-done.5.src_ref, bf16[128,512]{1,0:T(8,128)(2,1)S(1)} %get-tuple-element.13.fac_ref, f32[24,256]{1,0:T(8,128)S(1)} %pairs_2.2.refs_0_), custom_call_target="tpu_custom_call" | custom-call | flops 1610612736 | bytes 131072 | tf_op jit(solution)/shard_map/pairs_2/pallas_call | solution.py:290
  22.8 2.2 %collective-permute-done.4.src_ref = f32[32,1024]{1,0:T(8,128)S(1)} collective-permute-done((f32[32,1024]{1,0:T(8,128)S(1)}, f32[32,1024]{1,0:T(8,128)S(1)}, u32[]{:S(2)}, u32[]{:S(2)}) %collective-permute-start.4) | collective-permute-done | bytes 131104 | tf_op jit(solution)/shard_map/ppermute | solution.py:323
  24.9 0.8 %collective-permute-start.6 = (f32[32,1024]{1,0:T(8,128)S(1)}, f32[32,1024]{1,0:T(8,128)S(1)}, u32[]{:S(2)}, u32[]{:S(2)}) collective-permute-start(f32[32,1024]{1,0:T(8,128)S(1)} %collective-permute-done.4.src_ref), channel_id=1, source_target_pairs={{0,1},{1,0},{2,3},{3,2},{4,5},{5,4},{6,7},{7,6},{8,9},{9,8},{10,11... | collective-permute-start | bytes 393224 | tf_op jit(solution)/shard_map/ppermute | solution.py:323
  25.7 2.8 %pairs_4.1.in_ref = f32[24,256]{1,0:T(8,128)S(1)} custom-call(f32[32,1024]{1,0:T(8,128)S(1)} %collective-permute-done.4.src_ref, bf16[128,512]{1,0:T(8,128)(2,1)S(1)} %get-tuple-element.13.fac_ref, f32[24,256]{1,0:T(8,128)S(1)} %pairs_2.3.refs_0_), custom_call_target="tpu_custom_call" | custom-call | flops 3221225472 | bytes 262144 | tf_op jit(solution)/shard_map/pairs_4/pallas_call | solution.py:290
  28.6 4.2 %finish.1 = (f32[6,1024]{1,0:T(8,128)}, f32[6,1024]{1,0:T(8,128)}, f32[12,256]{1,0:T(8,128)}) custom-call(s32[1]{0:T(128)S(6)} %copy.10.count_hbm, f32[32,1024]{1,0:T(8,128)S(1)} %collective-permute-done.6.src_ref, bf16[128,512]{1,0:T(8,128)(2,1)S(1)} %get-tuple-element.13.fac_ref, f32[24,256]{1,0:T(8,128)S(1)} %pairs_4.1.in_ref, ...), custom_call_target="tpu_custom_call" | custom-call | flops 3221225472 | bytes 262144 | tf_op jit(solution)/shard_map/finish/pallas_call | solution.py:341
  (19 shorter events, 0.1 us)
Async XLA Ops:
  0.6 0.7 %copy-start.4 = (f32[1024]{0:T(1024)S(1)}, f32[1024]{0:T(1024)}, u32[]{:S(2)}) copy-start(f32[1024]{0:T(1024)} %param.9) | copy-start | bytes 12292
  1.3 0.8 %copy-start = (f32[6,1024]{1,0:T(8,128)S(1)}, f32[6,1024]{1,0:T(8,128)}, u32[]{:S(2)}) copy-start(f32[6,1024]{1,0:T(8,128)} %pv_hbm.3) | copy-start | bytes 73732
  2.1 0.8 %copy-start.2 = (f32[6,1024]{1,0:T(8,128)S(1)}, f32[6,1024]{1,0:T(8,128)}, u32[]{:S(2)}) copy-start(f32[6,1024]{1,0:T(8,128)} %aj_hbm.3) | copy-start | bytes 73732
  2.8 0.7 %copy-start.5 = (f32[1024]{0:T(1024)S(1)}, f32[1024]{0:T(1024)}, u32[]{:S(2)}) copy-start(f32[1024]{0:T(1024)} %param.10) | copy-start | bytes 12292
  3.5 0.7 %copy-start.6 = (s32[1024]{0:T(1024)S(1)}, s32[1024]{0:T(1024)}, u32[]{:S(2)}) copy-start(s32[1024]{0:T(1024)} %param.11) | copy-start | bytes 12292
  4.2 0.7 %copy-start.7 = (s32[1,1024]{1,0:T(1,128)S(1)}, s32[1,1024]{1,0:T(1,128)}, u32[]{:S(2)}) copy-start(s32[1,1024]{1,0:T(1,128)} %order_hbm.3) | copy-start | bytes 12292
  6.2 4.9 %collective-permute-start.1 = (f32[8,1024]{1,0:T(8,128)S(1)}, f32[8,1024]{1,0:T(8,128)S(1)}, u32[]{:S(2)}, u32[]{:S(2)}) collective-permute-start(f32[8,1024]{1,0:T(8,128)S(1)} %get-tuple-element.12.src_ref), channel_id=1, source_target_pairs={{0,1},{1,0},{2,3},{3,2},{4,5},{5,4},{6,7},{7,6},{8,9},{9,8},{10,11... | collective-permute-start | bytes 98312 | tf_op jit(solution)/shard_map/ppermute | solution.py:323
  6.3 5.8 %collective-permute-start = (f32[8,1024]{1,0:T(8,128)S(1)}, f32[8,1024]{1,0:T(8,128)S(1)}, u32[]{:S(2)}, u32[]{:S(2)}) collective-permute-start(f32[8,1024]{1,0:T(8,128)S(1)} %get-tuple-element.12.src_ref), channel_id=1, source_target_pairs={{0,8},{1,9},{2,10},{3,11},{4,12},{5,13},{6,14},{7,15},{8,0},{9,1},... | collective-permute-start | bytes 98312 | tf_op jit(solution)/shard_map/ppermute | solution.py:323
  12.1 2.9 %collective-permute-start.3 = (f32[8,1024]{1,0:T(8,128)S(1)}, f32[8,1024]{1,0:T(8,128)S(1)}, u32[]{:S(2)}, u32[]{:S(2)}) collective-permute-start(f32[8,1024]{1,0:T(8,128)S(1)} %collective-permute-done.src_ref), channel_id=1, source_target_pairs={{0,1},{1,0},{2,3},{3,2},{4,5},{5,4},{6,7},{7,6},{8,9},{9,8},{10,11... | collective-permute-start | bytes 98312 | tf_op jit(solution)/shard_map/ppermute | solution.py:323
  13.5 3.6 %collective-permute-start.2 = (f32[16,1024]{1,0:T(8,128)S(1)}, f32[16,1024]{1,0:T(8,128)S(1)}, u32[]{:S(2)}, u32[]{:S(2)}) collective-permute-start(f32[16,1024]{1,0:T(8,128)S(1)} %pad_maximum_fusion.1), channel_id=1, source_target_pairs={{0,4},{1,5},{2,6},{3,7},{4,0},{5,1},{6,2},{7,3},{8,12},{9,13},{10,... | collective-permute-start | bytes 196616 | tf_op jit(solution)/shard_map/ppermute | solution.py:323
  17.1 4.0 %collective-permute-start.5 = (f32[16,1024]{1,0:T(8,128)S(1)}, f32[16,1024]{1,0:T(8,128)S(1)}, u32[]{:S(2)}, u32[]{:S(2)}) collective-permute-start(f32[16,1024]{1,0:T(8,128)S(1)} %collective-permute-done.2.src_ref), channel_id=1, source_target_pairs={{0,1},{1,0},{2,3},{3,2},{4,5},{5,4},{6,7},{7,6},{8,9},{9,8},{10,11... | collective-permute-start | bytes 196616 | tf_op jit(solution)/shard_map/ppermute | solution.py:323
  19.7 5.2 %collective-permute-start.4 = (f32[32,1024]{1,0:T(8,128)S(1)}, f32[32,1024]{1,0:T(8,128)S(1)}, u32[]{:S(2)}, u32[]{:S(2)}) collective-permute-start(f32[32,1024]{1,0:T(8,128)S(1)} %pad_maximum_fusion), channel_id=1, source_target_pairs={{0,2},{1,3},{2,0},{3,1},{4,6},{5,7},{6,4},{7,5},{8,10},{9,11},{10,... | collective-permute-start | bytes 393224 | tf_op jit(solution)/shard_map/ppermute | solution.py:323
  22.7 5.8 %copy-start.1 = (f32[6,1024]{1,0:T(8,128)S(1)}, f32[6,1024]{1,0:T(8,128)}, u32[]{:S(2)}) copy-start(f32[6,1024]{1,0:T(8,128)} %pv_hbm.3) | copy-start | bytes 73732
  22.7 5.9 %copy-start.3 = (f32[6,1024]{1,0:T(8,128)S(1)}, f32[6,1024]{1,0:T(8,128)}, u32[]{:S(2)}) copy-start(f32[6,1024]{1,0:T(8,128)} %aj_hbm.3) | copy-start | bytes 73732
  22.7 5.8 %copy-start.8 = (s32[1,1024]{1,0:T(1,128)S(1)}, s32[1,1024]{1,0:T(1,128)}, u32[]{:S(2)}) copy-start(s32[1,1024]{1,0:T(1,128)} %order_hbm.3) | copy-start | bytes 12292
  24.9 3.6 %collective-permute-start.6 = (f32[32,1024]{1,0:T(8,128)S(1)}, f32[32,1024]{1,0:T(8,128)S(1)}, u32[]{:S(2)}, u32[]{:S(2)}) collective-permute-start(f32[32,1024]{1,0:T(8,128)S(1)} %collective-permute-done.4.src_ref), channel_id=1, source_target_pairs={{0,1},{1,0},{2,3},{3,2},{4,5},{5,4},{6,7},{7,6},{8,9},{9,8},{10,11... | collective-permute-start | bytes 393224 | tf_op jit(solution)/shard_map/ppermute | solution.py:323

commit v3 on v2

--- a/solution.py
+++ b/solution.py
@@ -152,37 +152,41 @@
     total(chunks - 1)
 
 
-def blocks_together(blocks):
-    return next(t for t in range(TOGETHER, 0, -1) if blocks % t == 0)
-
-
-def add_blocks(sources_ref, factors_t, acc_ref, products, weights):
-    blocks = sources_ref.shape[0] // 8
-    together = blocks_together(blocks)
-
-    def step(i, _):
-        rows = [sources_ref[pl.ds(pl.multiple_of((i * together + b) * 8, 8), 8), :] for b in range(together)]
+def blocks_together(shapes):
+    counts = [shape[0] // 8 for shape in shapes]
+    if sum(counts) <= TOGETHER:
+        return sum(counts)
+    return next(t for t in range(TOGETHER, 0, -1) if all(c % t == 0 for c in counts))
+
+
+def add_blocks(sources, factors_t, acc_ref, scratch):
+    together = blocks_together([ref.shape for ref in sources])
+    products, weights = scratch[: len(scratch) // 2], scratch[len(scratch) // 2 :]
+
+    def block(ref, b):
+        return ref[pl.ds(pl.multiple_of(b * 8, 8), 8), :]
+
+    if sum(ref.shape[0] // 8 for ref in sources) == together:
+        rows = [ref[b : b + 8] for ref in sources for b in range(0, ref.shape[0], 8)]
         add_pairs(rows, factors_t, acc_ref, products, weights)
-        return 0
-
-    if blocks == together:
-        step(0, 0)
-    else:
-        lax.fori_loop(0, blocks // together, step, 0)
-
-
-def pair_scratch(blocks, stars, slots):
-    chunks = stars * blocks_together(blocks) // CHUNK
+        return
+    for ref in sources:
+
+        def step(i, _):
+            add_pairs([block(ref, i * together + b) for b in range(together)], factors_t, acc_ref, products, weights)
+            return 0
+
+        lax.fori_loop(0, ref.shape[0] // 8 // together, step, 0)
+
+
+def pair_scratch(sources, slots):
+    chunks = sources[0].shape[1] * blocks_together([s.shape for s in sources]) // CHUNK
     return [pltpu.VMEM((CHUNK, 2 * slots), f32)] * chunks + [pltpu.VMEM((4 * CHUNK, slots), bf16)] * chunks
 
 
-def one_hot(order_ref, stars, slots):
-    row = lax.broadcasted_iota(jnp.int32, (stars, slots), 0)
-    return jnp.where(row == order_ref[0:1, 0:slots], 1.0, 0.0).astype(f32).astype(bf16)
-
-
-def live_slots(count_ref, slots):
-    return jnp.where(lax.broadcasted_iota(jnp.int32, (1, slots), 1) < count_ref[0], 1.0, 0.0)
+def one_hot(order, stars):
+    row = lax.broadcasted_iota(jnp.int32, (stars, order.shape[1]), 0)
+    return jnp.where(row == order, 1.0, 0.0).astype(f32).astype(bf16)
 
 
 def spread(hot, live):
@@ -197,27 +201,21 @@
     return out[0:height] + out[height : 2 * height] + out[2 * height : 3 * height]
 
 
-def fetch(pairs, sems):
-    copies = [pltpu.make_async_copy(src, dst, sems.at[i]) for i, (src, dst) in enumerate(pairs)]
+def prepare_kernel(slots, *refs):
+    inputs, (src_ref, old_ref, fac_ref), here, sems = refs[:7], refs[7:10], refs[10:17], refs[17]
+    copies = [pltpu.make_async_copy(src, dst, sems.at[i]) for i, (src, dst) in enumerate(zip(inputs, here))]
     for copy in copies:
         copy.start()
-
-    def wait(*places):
-        for i in places:
-            copies[i].wait()
-
-    return wait
-
-
-def prepare_kernel(slots, count_hbm, pv_hbm, aj_hbm, mass_hbm, phase_hbm, level_hbm, order_hbm, src_ref, old_ref, fac_ref, count_ref, pv_ref, aj_ref, mass_ref, phase_ref, level_ref, order_ref, sems):
-    hbm = (order_hbm, count_hbm, phase_hbm, level_hbm, mass_hbm, pv_hbm, aj_hbm)
-    here = (order_ref, count_ref, phase_ref, level_ref, mass_ref, pv_ref, aj_ref)
-    wait = fetch(tuple(zip(hbm, here)), sems)
+    pv_ref, aj_ref, mass_ref, phase_ref, level_ref, count_ref, order_ref = here
     stars = pv_ref.shape[1]
-    wait(0, 1)
-    hot = one_hot(order_ref, stars, slots)
-    active = spread(hot, live_slots(count_ref, slots))
-    wait(2, 3, 4, 5, 6)
+    copies[5].wait()
+    copies[6].wait()
+    order = order_ref[0:1, 0:slots]
+    hot = one_hot(order, stars)
+    live = jnp.where(lax.broadcasted_iota(jnp.int32, (1, slots), 1) < count_ref[...], 1.0, 0.0)
+    active = spread(hot, live)
+    for copy in copies[:5]:
+        copy.wait()
     level = level_ref[...]
     step_len = base_step * jnp.where((level & 1) > 0, 0.5, 1.0) * jnp.where((level & 2) > 0, 0.25, 1.0)
     age = step_len * jnp.where(active > 0.5, 1.0, phase_ref[...])
@@ -231,28 +229,28 @@
     src_ref[...] = state
     gap = jnp.zeros((2, stars), f32)
     old = exact_product(jnp.concatenate([state, pv, gap, aj, gap], axis=0), hot, 0)
-    old_ref[...] = old
+    old_ref[...] = jnp.concatenate([old[0:22], live, order.astype(f32)], axis=0)
     fac_ref[...] = target_factors(old[0:8])
 
 
-def pair_kernel(fresh, src_ref, fac_ref, *refs):
+def pair_kernel(parts, fresh, *refs):
+    sources, fac_ref, refs = refs[:parts], refs[parts], refs[parts + 1 :]
     if fresh:
         out_ref, acc_ref, *scratch = refs
         acc_ref[...] = jnp.zeros_like(acc_ref)
     else:
         in_ref, out_ref, acc_ref, *scratch = refs
         acc_ref[...] = in_ref[...]
-    half = len(scratch) // 2
-    add_blocks(src_ref, fac_ref[...], acc_ref, scratch[:half], scratch[half:])
+    add_blocks(sources, fac_ref[...], acc_ref, scratch)
     out_ref[...] = acc_ref[...]
 
 
-def finish_kernel(count_hbm, src_ref, fac_ref, in_ref, old_ref, order_hbm, pv_hbm, aj_hbm, new_pv_ref, new_aj_ref, state_ref, count_ref, order_ref, pv_ref, aj_ref, sems, acc_ref, *scratch):
-    wait = fetch(((count_hbm, count_ref), (order_hbm, order_ref), (pv_hbm, pv_ref), (aj_hbm, aj_ref)), sems)
+def finish_kernel(parts, *refs):
+    sources, refs = refs[:parts], refs[parts:]
+    fac_ref, in_ref, old_ref, pv_ref, aj_ref, new_pv_ref, new_aj_ref, state_ref, acc_ref, *scratch = refs
     stars, slots = pv_ref.shape[1], in_ref.shape[1]
     acc_ref[...] = in_ref[...]
-    half = len(scratch) // 2
-    add_blocks(src_ref, fac_ref[...], acc_ref, scratch[:half], scratch[half:])
+    add_blocks(sources, fac_ref[...], acc_ref, scratch)
     sums = acc_ref[0:8] + acc_ref[8:16] + acc_ref[16:24]
     old = old_ref[...]
     here, there, step_len = old[0:3], old[3:6], old[7:8]
@@ -263,11 +261,10 @@
     twelfth = step_len * step_len / 12.0
     v1 = v0 + half_step * (a0 + a1) + twelfth * (j0 - j1)
     x1 = x0 + half_step * (v0 + v1) + twelfth * (a0 - a1)
-    wait(0, 1, 2, 3)
-    live = live_slots(count_ref, slots)
+    live = old[22:23]
     state = jnp.where(live > 0.5, jnp.concatenate([x1, v1, a1, j1], axis=0), 0.0)
     state_ref[...] = state
-    hot = one_hot(order_ref, stars, slots)
+    hot = one_hot(old[23:24].astype(jnp.int32), stars)
     rows = jnp.concatenate([state, jnp.broadcast_to(live, (4, slots))], axis=0)
     moved = exact_product(rows, hot, 1)
     active = moved[12:13] > 0.5
@@ -279,29 +276,30 @@
 HBM = pl.BlockSpec(memory_space=pltpu.HBM)
 
 
-def cost(blocks, stars, slots):
-    pairs = blocks * stars * slots
-    return pl.CostEstimate(flops=2 * 256 * 6 * pairs, bytes_accessed=64 * blocks * stars, transcendentals=pairs)
+def cost(sources, slots):
+    pairs = sum(s.size // 8 for s in sources) * slots
+    return pl.CostEstimate(flops=pairs, bytes_accessed=4 * pairs // slots, transcendentals=pairs)
 
 
 def call_pairs(sources, factors, acc):
-    blocks, stars, slots = sources.shape[0] // 8, sources.shape[1], factors.shape[1] // 2
-    operands = [sources, factors] + ([] if acc is None else [acc])
+    slots = factors.shape[1] // 2
+    operands = list(sources) + [factors] + ([] if acc is None else [acc])
     return pl.pallas_call(
-        functools.partial(pair_kernel, acc is None),
+        functools.partial(pair_kernel, len(sources), acc is None),
         out_shape=jax.ShapeDtypeStruct((24, slots), f32),
         in_specs=[VMEM] * len(operands),
         out_specs=VMEM,
-        scratch_shapes=[pltpu.VMEM((24, slots), f32)] + pair_scratch(blocks, stars, slots),
+        scratch_shapes=[pltpu.VMEM((24, slots), f32)] + pair_scratch(sources, slots),
         compiler_params=PARAMS,
-        cost_estimate=cost(blocks, stars, slots),
-        name="pairs_%d" % blocks,
+        cost_estimate=cost(sources, slots),
+        name="pairs",
     )(*operands)
 
 
 def per_device(n, slots, pos_vel, acc_jerk, star_mass, step_phase, step_level, counts, star_order):
     stars = pos_vel.shape[1]
-    row = lambda values: values.reshape(1, stars)
+    inputs = [pos_vel, acc_jerk] + [values.reshape(1, -1) for values in (star_mass, step_phase, step_level, counts)]
+    inputs.append(star_order)
     own, old, factors = pl.pallas_call(
         functools.partial(prepare_kernel, slots),
         out_shape=(
@@ -311,50 +309,57 @@
         ),
         in_specs=[HBM] * 7,
         out_specs=(VMEM,) * 3,
-        scratch_shapes=[pltpu.SMEM((1,), jnp.int32), pltpu.VMEM(pos_vel.shape, f32), pltpu.VMEM(acc_jerk.shape, f32)]
-        + [pltpu.VMEM((1, stars), f32)] * 2
-        + [pltpu.VMEM((1, stars), jnp.int32)] * 2
-        + [pltpu.SemaphoreType.DMA((7,))],
+        scratch_shapes=[pltpu.VMEM(values.shape, values.dtype) for values in inputs] + [pltpu.SemaphoreType.DMA((7,))],
         compiler_params=PARAMS,
         name="prepare",
-    )(counts, pos_vel, acc_jerk, row(star_mass), row(step_phase), row(step_level), star_order)
+    )(*[pltpu.with_memory_space_constraint(values, pltpu.HBM) if values.size > 1 else values for values in inputs])
 
     def swap(values, bit):
         return lax.ppermute(values, "ja", [(i, i ^ bit) for i in range(n)])
 
-    held, arrived, acc = own, own, None
-    bit = n // 2
-    while True:
-        if bit > 1:
-            coming = swap(held, bit)
+    def after(acc, *values):
+        return lax.optimization_barrier(values + (acc,))
+
+    def pairs(acc, *sources):
+        return call_pairs(sources, factors, acc)
+
+    across = swap(own, 1)
+    held, arrived, bit = own, own, n // 2
+    coming = swap(own, bit)
+    acc = pairs(None, own)
+    acc = pairs(acc, across)
+    while bit > 4:
+        arrived, acc = after(acc, coming)
+        held = jnp.concatenate([held, arrived], axis=0)
+        bit //= 2
         across = swap(arrived, 1)
-        acc = call_pairs(arrived, factors, acc)
-        if bit == 1:
-            break
-        acc = call_pairs(across, factors, acc)
-        arrived, acc = lax.optimization_barrier((coming, acc))
-        if bit > 2:
-            held = jnp.concatenate([held, arrived], axis=0)
-        bit //= 2
-
-    blocks = across.shape[0] // 8
+        beside = swap(held, 2) if bit == 4 else None
+        coming = swap(held, bit)
+        acc = pairs(acc, arrived)
+        acc = pairs(acc, across)
+    arrived, beside, acc = after(acc, coming, beside)
+    beside_across = swap(beside, 1)
+    across = swap(arrived, 1)
+    coming = swap(arrived, 2)
+    acc = pairs(acc, arrived, beside)
+    acc = pairs(acc, across, beside_across)
+    last, acc = after(acc, coming)
+    across = swap(last, 1)
+    acc = pairs(acc, last)
     return pl.pallas_call(
-        finish_kernel,
+        functools.partial(finish_kernel, 1),
         out_shape=(
             jax.ShapeDtypeStruct(pos_vel.shape, f32),
             jax.ShapeDtypeStruct(acc_jerk.shape, f32),
             jax.ShapeDtypeStruct((12, slots), f32),
         ),
-        in_specs=[HBM] + [VMEM] * 4 + [HBM] * 3,
+        in_specs=[VMEM] * 6,
         out_specs=(VMEM,) * 3,
-        scratch_shapes=[pltpu.SMEM((1,), jnp.int32), pltpu.VMEM((1, stars), jnp.int32)]
-        + [pltpu.VMEM(pos_vel.shape, f32), pltpu.VMEM(acc_jerk.shape, f32), pltpu.SemaphoreType.DMA((4,))]
-        + [pltpu.VMEM((24, slots), f32)]
-        + pair_scratch(blocks, stars, slots),
+        scratch_shapes=[pltpu.VMEM((24, slots), f32)] + pair_scratch([across], slots),
         compiler_params=PARAMS,
-        cost_estimate=cost(blocks, stars, slots),
+        cost_estimate=cost([across], slots),
         name="finish",
-    )(counts, across, factors, acc, old, star_order, pos_vel, acc_jerk)
+    )(across, factors, acc, old, pos_vel, acc_jerk)
 
 
 A_DEV = 128

time: 33.3 us -> 26.2 us (0.79)
  local copies, waits for them, and re-layouts: 3.62 us -> 0.03 us
  waiting for transfers between devices: 3.3 us -> 0.03 us
    unnamed x18 -> x5, local copies, waits for them, and re-layouts: 3.62 us -> 0.02 us
    ppermute x7 -> x9, waiting for transfers between devices: 3.3 us -> 0.03 us  [swap(): return lax.ppermute(values, 'ja', [(i, i ^ bit) for i in range(n)])]
    pallas_call x8, Pallas kernels: 14.4 us -> 13.9 us  [the longest x7 11.4 us: call_pairs(): pl.pallas_call(functools.partial(pair_kernel, len(sources), acc is None),...]
    ppermute x7 -> x9, starting transfers between devices: 8.84 us -> 9.09 us  [swap(): return lax.ppermute(values, 'ja', [(i, i ^ bit) for i in range(n)])]
  transfers between devices with their start and end apart: 7 -> 9, of which waited for: 2 -> 0; matrix products, arithmetic and copies ran while one was open for 0% -> 0% of each run, Pallas kernels for 31% -> 44%
where the time goes in v3:
time: 26.2 us; the launch traced here: 26 us
  Pallas kernels  15.4 us (59%)
  starting transfers between devices  9.09 us (35%)
  between operations  1.42 us (5%)
    pallas_call x7, Pallas kernels, call_pairs(): pl.pallas_call(functools.partial(pair_kernel, len(sources), acc is None),...  11.4 us
    ppermute x9, starting transfers between devices, swap(): return lax.ppermute(values, 'ja', [(i, i ^ bit) for i in range(n)])  9.09 us
    pallas_call x1, Pallas kernels, per_device(): pl.pallas_call(functools.partial(finish_kernel, 1), out_shape=(jax.ShapeD...  2.56 us
    pallas_call x1, Pallas kernels, per_device(): pl.pallas_call(functools.partial(prepare_kernel, slots), out_shape=(jax.S...  1.47 us
  transfers between devices with their start and end apart: 9, of which 0 were waited for; matrix products, arithmetic and copies ran while one was open for 0% of the time, Pallas kernels for 44%

profile of v3, /device:TPU:1, one launch (start us, length us, event | category | flops | bytes accessed | tf_op | source)
XLA Modules:
  0.0 26.0 jit_solution(1345213823820084412)
XLA Ops:
  1.3 1.5 %prepare.1 = (f32[8,1024]{1,0:T(8,128)S(1)}, f32[24,256]{1,0:T(8,128)S(1)}, bf16[128,512]{1,0:T(8,128)(2,1)S(1)}) custom-call(f32[6,1024]{1,0:T(8,128)} %refs_4_.1, f32[6,1024]{1,0:T(8,128)} %refs_5_.1, f32[1,1024]{1,0:T(1,128)} %bitcast.5, f32[1,1024]{1,0:T(1,128)} %bitcast.6, s32[1,1024]{1,0:T(1,128)} %bitcast.7, s32[1,1]{1,0:T(1,128)} %bitcast.4.refs_5_, ...), custom_call_target="tpu_custom_call" | custom-call | tf_op jit(solution)/shard_map/prepare/pallas_call | solution.py:303
  2.8 0.1 collective-permute-start.1
  2.9 3.8 %collective-permute-start = (f32[8,1024]{1,0:T(8,128)S(1)}, f32[8,1024]{1,0:T(8,128)S(1)}, u32[]{:S(2)}, u32[]{:S(2)}) collective-permute-start(f32[8,1024]{1,0:T(8,128)S(1)} %get-tuple-element.13.refs_0_), channel_id=1, source_target_pairs={{0,8},{1,9},{2,10},{3,11},{4,12},{5,13},{6,14},{7,15},{8,0},{9,1},... | collective-permute-start | bytes 98312 | tf_op jit(solution)/shard_map/ppermute | solution.py:318
  6.7 1.0 %pairs.7.refs_2_ = f32[24,256]{1,0:T(8,128)S(1)} custom-call(f32[8,1024]{1,0:T(8,128)S(1)} %get-tuple-element.13.refs_0_, bf16[128,512]{1,0:T(8,128)(2,1)S(1)} %get-tuple-element.14.refs_1_.refs_2_), custom_call_target="tpu_custom_call" | custom-call | flops 262144 | bytes 4096 | tf_op jit(solution)/shard_map/pairs/pallas_call | solution.py:287
  7.7 0.0 collective-permute-done.1.refs_0_
  7.7 1.0 %pairs.8.refs_2_ = f32[24,256]{1,0:T(8,128)S(1)} custom-call(f32[8,1024]{1,0:T(8,128)S(1)} %collective-permute-done.1.refs_0_, bf16[128,512]{1,0:T(8,128)(2,1)S(1)} %get-tuple-element.14.refs_1_.refs_2_, f32[24,256]{1,0:T(8,128)S(1)} %pairs.7.refs_2_), custom_call_target="tpu_custom_call" | custom-call | flops 262144 | bytes 4096 | tf_op jit(solution)/shard_map/pairs/pallas_call | solution.py:287
  8.7 0.0 collective-permute-done.refs_0_
  8.7 1.3 %collective-permute-start.3 = (f32[16,1024]{1,0:T(8,128)S(1)}, f32[16,1024]{1,0:T(8,128)S(1)}, u32[]{:S(2)}, u32[]{:S(2)}) collective-permute-start(f32[16,1024]{1,0:T(8,128)S(1)} %constant_dynamic-update-slice_fusion), channel_id=1, source_target_pairs={{0,2},{1,3},{2,0},{3,1},{4,6},{5,7},{6,4},{7,5},{8,10},{9,11},{10,... | collective-permute-start | bytes 196616 | tf_op jit(solution)/shard_map/ppermute | solution.py:318
  10.0 1.3 %collective-permute-start.2 = (f32[16,1024]{1,0:T(8,128)S(1)}, f32[16,1024]{1,0:T(8,128)S(1)}, u32[]{:S(2)}, u32[]{:S(2)}) collective-permute-start(f32[16,1024]{1,0:T(8,128)S(1)} %constant_dynamic-update-slice_fusion), channel_id=1, source_target_pairs={{0,4},{1,5},{2,6},{3,7},{4,0},{5,1},{6,2},{7,3},{8,12},{9,13},{10,... | collective-permute-start | bytes 196616 | tf_op jit(solution)/shard_map/ppermute | solution.py:318
  11.3 1.0 %collective-permute-start.4 = (f32[8,1024]{1,0:T(8,128)S(1)}, f32[8,1024]{1,0:T(8,128)S(1)}, u32[]{:S(2)}, u32[]{:S(2)}) collective-permute-start(f32[8,1024]{1,0:T(8,128)S(1)} %collective-permute-done.refs_0_), channel_id=1, source_target_pairs={{0,1},{1,0},{2,3},{3,2},{4,5},{5,4},{6,7},{7,6},{8,9},{9,8},{10,11... | collective-permute-start | bytes 98312 | tf_op jit(solution)/shard_map/ppermute | solution.py:318
  12.3 1.0 %pairs.9.refs_2_ = f32[24,256]{1,0:T(8,128)S(1)} custom-call(f32[8,1024]{1,0:T(8,128)S(1)} %collective-permute-done.refs_0_, bf16[128,512]{1,0:T(8,128)(2,1)S(1)} %get-tuple-element.14.refs_1_.refs_2_, f32[24,256]{1,0:T(8,128)S(1)} %pairs.8.refs_2_), custom_call_target="tpu_custom_call" | custom-call | flops 262144 | bytes 4096 | tf_op jit(solution)/shard_map/pairs/pallas_call | solution.py:287
  13.3 1.0 %pairs.10.refs_3_ = f32[24,256]{1,0:T(8,128)S(1)} custom-call(f32[8,1024]{1,0:T(8,128)S(1)} %collective-permute-done.4.refs_0_, bf16[128,512]{1,0:T(8,128)(2,1)S(1)} %get-tuple-element.14.refs_1_.refs_2_, f32[24,256]{1,0:T(8,128)S(1)} %pairs.9.refs_2_), custom_call_target="tpu_custom_call" | custom-call | flops 262144 | bytes 4096 | tf_op jit(solution)/shard_map/pairs/pallas_call | solution.py:287
  14.4 0.0 collective-permute-done.2.refs_0_
  14.4 0.6 %collective-permute-start.7 = (f32[16,1024]{1,0:T(8,128)S(1)}, f32[16,1024]{1,0:T(8,128)S(1)}, u32[]{:S(2)}, u32[]{:S(2)}) collective-permute-start(f32[16,1024]{1,0:T(8,128)S(1)} %collective-permute-done.3.refs_1_), channel_id=1, source_target_pairs={{0,1},{1,0},{2,3},{3,2},{4,5},{5,4},{6,7},{7,6},{8,9},{9,8},{10,11... | collective-permute-start | bytes 196616 | tf_op jit(solution)/shard_map/ppermute | solution.py:318
  15.0 0.0 collective-permute-start.6
  15.0 0.2 collective-permute-start.5
  15.2 2.8 %pairs.11.refs_3_ = f32[24,256]{1,0:T(8,128)S(1)} custom-call(f32[16,1024]{1,0:T(8,128)S(1)} %collective-permute-done.2.refs_0_, f32[16,1024]{1,0:T(8,128)S(1)} %collective-permute-done.3.refs_1_, bf16[128,512]{1,0:T(8,128)(2,1)S(1)} %get-tuple-element.14.refs_1_.refs_2_, f32[24,256]{1,0:T(8,128)S(1)} %pairs.10.refs_3_), custom_call_target="tpu_custom_call" | custom-call | flops 1048576 | bytes 16384 | tf_op jit(solution)/shard_map/pairs/pallas_call | solution.py:287
  18.1 0.0 collective-permute-done.6.refs_0_
  18.1 2.9 %pairs.12.refs_2_ = f32[24,256]{1,0:T(8,128)S(1)} custom-call(f32[16,1024]{1,0:T(8,128)S(1)} %collective-permute-done.6.refs_0_, f32[16,1024]{1,0:T(8,128)S(1)} %collective-permute-done.7.refs_1_, bf16[128,512]{1,0:T(8,128)(2,1)S(1)} %get-tuple-element.14.refs_1_.refs_2_, f32[24,256]{1,0:T(8,128)S(1)} %pairs.11.refs_3_), custom_call_target="tpu_custom_call" | custom-call | flops 1048576 | bytes 16384 | tf_op jit(solution)/shard_map/pairs/pallas_call | solution.py:287
  20.9 0.0 copy-start.1
  21.0 0.8 %collective-permute-start.8 = (f32[16,1024]{1,0:T(8,128)S(1)}, f32[16,1024]{1,0:T(8,128)S(1)}, u32[]{:S(2)}, u32[]{:S(2)}) collective-permute-start(f32[16,1024]{1,0:T(8,128)S(1)} %collective-permute-done.5.refs_0_), channel_id=1, source_target_pairs={{0,1},{1,0},{2,3},{3,2},{4,5},{5,4},{6,7},{7,6},{8,9},{9,8},{10,11... | collective-permute-start | bytes 196616 | tf_op jit(solution)/shard_map/ppermute | solution.py:318
  21.8 1.6 %pairs.13.refs_2_ = f32[24,256]{1,0:T(8,128)S(1)} custom-call(f32[16,1024]{1,0:T(8,128)S(1)} %collective-permute-done.5.refs_0_, bf16[128,512]{1,0:T(8,128)(2,1)S(1)} %get-tuple-element.14.refs_1_.refs_2_, f32[24,256]{1,0:T(8,128)S(1)} %pairs.12.refs_2_), custom_call_target="tpu_custom_call" | custom-call | flops 524288 | bytes 8192 | tf_op jit(solution)/shard_map/pairs/pallas_call | solution.py:287
  23.4 0.0 copy-done
  23.4 2.6 %finish.1 = (f32[6,1024]{1,0:T(8,128)}, f32[6,1024]{1,0:T(8,128)}, f32[12,256]{1,0:T(8,128)}) custom-call(f32[16,1024]{1,0:T(8,128)S(1)} %collective-permute-done.8.refs_0_, bf16[128,512]{1,0:T(8,128)(2,1)S(1)} %get-tuple-element.14.refs_1_.refs_2_, f32[24,256]{1,0:T(8,128)S(1)} %pairs.13.refs_2_, f32[24,256]{1,0:T(8,128)S(1)} %get-tuple-element.22.refs_3_, ...), custom_call_target="tpu_custom_call" | custom-call | flops 524288 | bytes 8192 | tf_op jit(solution)/shard_map/finish/pallas_call | solution.py:349
  (9 shorter events, 0.0 us)
Async XLA Ops:
  2.8 4.9 %collective-permute-start.1 = (f32[8,1024]{1,0:T(8,128)S(1)}, f32[8,1024]{1,0:T(8,128)S(1)}, u32[]{:S(2)}, u32[]{:S(2)}) collective-permute-start(f32[8,1024]{1,0:T(8,128)S(1)} %get-tuple-element.13.refs_0_), channel_id=1, source_target_pairs={{0,1},{1,0},{2,3},{3,2},{4,5},{5,4},{6,7},{7,6},{8,9},{9,8},{10,11... | collective-permute-start | bytes 98312 | tf_op jit(solution)/shard_map/ppermute | solution.py:318
  2.9 5.8 %collective-permute-start = (f32[8,1024]{1,0:T(8,128)S(1)}, f32[8,1024]{1,0:T(8,128)S(1)}, u32[]{:S(2)}, u32[]{:S(2)}) collective-permute-start(f32[8,1024]{1,0:T(8,128)S(1)} %get-tuple-element.13.refs_0_), channel_id=1, source_target_pairs={{0,8},{1,9},{2,10},{3,11},{4,12},{5,13},{6,14},{7,15},{8,0},{9,1},... | collective-permute-start | bytes 98312 | tf_op jit(solution)/shard_map/ppermute | solution.py:318
  8.7 5.6 %collective-permute-start.3 = (f32[16,1024]{1,0:T(8,128)S(1)}, f32[16,1024]{1,0:T(8,128)S(1)}, u32[]{:S(2)}, u32[]{:S(2)}) collective-permute-start(f32[16,1024]{1,0:T(8,128)S(1)} %constant_dynamic-update-slice_fusion), channel_id=1, source_target_pairs={{0,2},{1,3},{2,0},{3,1},{4,6},{5,7},{6,4},{7,5},{8,10},{9,11},{10,... | collective-permute-start | bytes 196616 | tf_op jit(solution)/shard_map/ppermute | solution.py:318
  10.0 4.3 %collective-permute-start.2 = (f32[16,1024]{1,0:T(8,128)S(1)}, f32[16,1024]{1,0:T(8,128)S(1)}, u32[]{:S(2)}, u32[]{:S(2)}) collective-permute-start(f32[16,1024]{1,0:T(8,128)S(1)} %constant_dynamic-update-slice_fusion), channel_id=1, source_target_pairs={{0,4},{1,5},{2,6},{3,7},{4,0},{5,1},{6,2},{7,3},{8,12},{9,13},{10,... | collective-permute-start | bytes 196616 | tf_op jit(solution)/shard_map/ppermute | solution.py:318
  11.3 2.0 %collective-permute-start.4 = (f32[8,1024]{1,0:T(8,128)S(1)}, f32[8,1024]{1,0:T(8,128)S(1)}, u32[]{:S(2)}, u32[]{:S(2)}) collective-permute-start(f32[8,1024]{1,0:T(8,128)S(1)} %collective-permute-done.refs_0_), channel_id=1, source_target_pairs={{0,1},{1,0},{2,3},{3,2},{4,5},{5,4},{6,7},{7,6},{8,9},{9,8},{10,11... | collective-permute-start | bytes 98312 | tf_op jit(solution)/shard_map/ppermute | solution.py:318
  14.4 3.7 %collective-permute-start.7 = (f32[16,1024]{1,0:T(8,128)S(1)}, f32[16,1024]{1,0:T(8,128)S(1)}, u32[]{:S(2)}, u32[]{:S(2)}) collective-permute-start(f32[16,1024]{1,0:T(8,128)S(1)} %collective-permute-done.3.refs_1_), channel_id=1, source_target_pairs={{0,1},{1,0},{2,3},{3,2},{4,5},{5,4},{6,7},{7,6},{8,9},{9,8},{10,11... | collective-permute-start | bytes 196616 | tf_op jit(solution)/shard_map/ppermute | solution.py:318
  15.0 3.1 %collective-permute-start.6 = (f32[16,1024]{1,0:T(8,128)S(1)}, f32[16,1024]{1,0:T(8,128)S(1)}, u32[]{:S(2)}, u32[]{:S(2)}) collective-permute-start(f32[16,1024]{1,0:T(8,128)S(1)} %collective-permute-done.2.refs_0_), channel_id=1, source_target_pairs={{0,1},{1,0},{2,3},{3,2},{4,5},{5,4},{6,7},{7,6},{8,9},{9,8},{10,11... | collective-permute-start | bytes 196616 | tf_op jit(solution)/shard_map/ppermute | solution.py:318
  15.0 6.0 %collective-permute-start.5 = (f32[16,1024]{1,0:T(8,128)S(1)}, f32[16,1024]{1,0:T(8,128)S(1)}, u32[]{:S(2)}, u32[]{:S(2)}) collective-permute-start(f32[16,1024]{1,0:T(8,128)S(1)} %collective-permute-done.2.refs_0_), channel_id=1, source_target_pairs={{0,2},{1,3},{2,0},{3,1},{4,6},{5,7},{6,4},{7,5},{8,10},{9,11},{10,... | collective-permute-start | bytes 196616 | tf_op jit(solution)/shard_map/ppermute | solution.py:318
  20.9 2.5 %copy-start = (f32[6,1024]{1,0:T(8,128)S(1)}, f32[6,1024]{1,0:T(8,128)}, u32[]{:S(2)}) copy-start(f32[6,1024]{1,0:T(8,128)} %refs_4_.1) | copy-start | bytes 73732
  20.9 2.5 %copy-start.1 = (f32[6,1024]{1,0:T(8,128)S(1)}, f32[6,1024]{1,0:T(8,128)}, u32[]{:S(2)}) copy-start(f32[6,1024]{1,0:T(8,128)} %refs_5_.1) | copy-start | bytes 73732
  21.0 2.4 %collective-permute-start.8 = (f32[16,1024]{1,0:T(8,128)S(1)}, f32[16,1024]{1,0:T(8,128)S(1)}, u32[]{:S(2)}, u32[]{:S(2)}) collective-permute-start(f32[16,1024]{1,0:T(8,128)S(1)} %collective-permute-done.5.refs_0_), channel_id=1, source_target_pairs={{0,1},{1,0},{2,3},{3,2},{4,5},{5,4},{6,7},{7,6},{8,9},{9,8},{10,11... | collective-permute-start | bytes 196616 | tf_op jit(solution)/shard_map/ppermute | solution.py:318

commit v4 on v3

--- a/solution.py
+++ b/solution.py
@@ -15,6 +15,7 @@
 CHUNK = 128
 TOGETHER = 4
 FACTOR_ROWS = 128
+RING = 16
 PARAMS = pltpu.CompilerParams(vmem_limit_bytes=32 << 20)
 
 
@@ -103,85 +104,80 @@
     )
 
 
-def add_pairs(states, factors_t, acc_ref, products, weights):
-    slots = factors_t.shape[1] // 2
-    per = states[0].shape[1] // CHUNK
+def add_pairs(states, factors, sums, scratch):
+    slots = factors[0].shape[1] // 2
+    products, weights = scratch[:RING], scratch[RING:]
+    per, sets = states[0].shape[1] // CHUNK, len(factors)
     ready = {}
 
     def prepare(b):
         ready[b] = (source_factors(states[b]).T,) + sum_factors(states[b])
 
-    def span(c):
-        return slice(c % per * CHUNK, (c % per + 1) * CHUNK)
+    def place(c):
+        c = c // sets
+        return c // per, slice(c % per * CHUNK, (c % per + 1) * CHUNK)
 
     def multiply(c):
-        products[c][...] = jnp.dot(ready[c // per][0][span(c)], factors_t, preferred_element_type=f32)
+        b, span = place(c)
+        products[c % RING][...] = jnp.dot(ready[b][0][span], factors[c % sets], preferred_element_type=f32)
 
     def weigh(c):
+        product, out = products[c % RING], weights[c % RING]
         for g in range(0, CHUNK, 16):
             for lane in range(0, slots, 128):
                 cols = slice(lane, lane + 128)
-                radial = products[c][g : g + 16, cols]
-                dist_sq = products[c][g : g + 16, slots + lane : slots + lane + 128]
+                radial = product[g : g + 16, cols]
+                dist_sq = product[g : g + 16, slots + lane : slots + lane + 128]
                 inverse = lax.rsqrt(dist_sq)
                 inverse_sq = inverse * inverse
                 weight = inverse * inverse_sq
                 radial = weight * (inverse_sq * radial)
                 weight_hi, radial_hi = weight.astype(bf16), radial.astype(bf16)
-                weights[c][g : g + 16, cols] = weight_hi
-                weights[c][CHUNK + g : CHUNK + g + 16, cols] = (weight - weight_hi.astype(f32)).astype(bf16)
-                weights[c][2 * CHUNK + g : 2 * CHUNK + g + 16, cols] = radial_hi
-                weights[c][3 * CHUNK + g : 3 * CHUNK + g + 16, cols] = (radial - radial_hi.astype(f32)).astype(bf16)
+                out[g : g + 16, cols] = weight_hi
+                out[CHUNK + g : CHUNK + g + 16, cols] = (weight - weight_hi.astype(f32)).astype(bf16)
+                out[2 * CHUNK + g : 2 * CHUNK + g + 16, cols] = radial_hi
+                out[3 * CHUNK + g : 3 * CHUNK + g + 16, cols] = (radial - radial_hi.astype(f32)).astype(bf16)
 
     def total(c):
-        _, by_weight, by_radial = ready[c // per]
-        left = [by_weight[:, span(c)]] * 2 + [by_radial[:, span(c)]] * 2
-        acc_ref[...] += jnp.dot(jnp.concatenate(left, axis=1), weights[c][...], preferred_element_type=f32)
-
-    chunks = len(states) * per
+        b, span = place(c)
+        left = [ready[b][1][:, span]] * 2 + [ready[b][2][:, span]] * 2
+        sums[c % sets][...] += jnp.dot(
+            jnp.concatenate(left, axis=1), weights[c % RING][...], preferred_element_type=f32
+        )
+
+    steps = len(states) * per * sets
     prepare(0)
     multiply(0)
-    for c in range(chunks):
-        if (c + 2) % per == 0 and (c + 2) // per < len(states):
-            prepare((c + 2) // per)
-        if c + 1 < chunks:
+    for c in range(steps):
+        if (c + 2) % (per * sets) == 0 and (c + 2) // (per * sets) < len(states):
+            prepare((c + 2) // (per * sets))
+        if c + 1 < steps:
             multiply(c + 1)
         weigh(c)
         if c > 0:
             total(c - 1)
-    total(chunks - 1)
-
-
-def blocks_together(shapes):
-    counts = [shape[0] // 8 for shape in shapes]
+    total(steps - 1)
+
+
+def add_blocks(sources, factors, sums, scratch):
+    counts = [ref.shape[0] // 8 for ref in sources]
     if sum(counts) <= TOGETHER:
-        return sum(counts)
-    return next(t for t in range(TOGETHER, 0, -1) if all(c % t == 0 for c in counts))
-
-
-def add_blocks(sources, factors_t, acc_ref, scratch):
-    together = blocks_together([ref.shape for ref in sources])
-    products, weights = scratch[: len(scratch) // 2], scratch[len(scratch) // 2 :]
-
-    def block(ref, b):
-        return ref[pl.ds(pl.multiple_of(b * 8, 8), 8), :]
-
-    if sum(ref.shape[0] // 8 for ref in sources) == together:
         rows = [ref[b : b + 8] for ref in sources for b in range(0, ref.shape[0], 8)]
-        add_pairs(rows, factors_t, acc_ref, products, weights)
+        add_pairs(rows, factors, sums, scratch)
         return
-    for ref in sources:
+    together = next(t for t in range(TOGETHER, 0, -1) if all(c % t == 0 for c in counts))
+    for ref, count in zip(sources, counts):
 
         def step(i, _):
-            add_pairs([block(ref, i * together + b) for b in range(together)], factors_t, acc_ref, products, weights)
+            rows = [ref[pl.ds(pl.multiple_of((i * together + b) * 8, 8), 8), :] for b in range(together)]
+            add_pairs(rows, factors, sums, scratch)
             return 0
 
-        lax.fori_loop(0, ref.shape[0] // 8 // together, step, 0)
-
-
-def pair_scratch(sources, slots):
-    chunks = sources[0].shape[1] * blocks_together([s.shape for s in sources]) // CHUNK
-    return [pltpu.VMEM((CHUNK, 2 * slots), f32)] * chunks + [pltpu.VMEM((4 * CHUNK, slots), bf16)] * chunks
+        lax.fori_loop(0, count // together, step, 0)
+
+
+def pair_scratch(slots):
+    return [pltpu.VMEM((CHUNK, 2 * slots), f32)] * RING + [pltpu.VMEM((4 * CHUNK, slots), bf16)] * RING
 
 
 def one_hot(order, stars):
@@ -202,7 +198,7 @@
 
 
 def prepare_kernel(slots, *refs):
-    inputs, (src_ref, old_ref, fac_ref), here, sems = refs[:7], refs[7:10], refs[10:17], refs[17]
+    inputs, (src_ref, tgt_ref, old_ref, fac_ref), here, sems = refs[:7], refs[7:11], refs[11:18], refs[18]
     copies = [pltpu.make_async_copy(src, dst, sems.at[i]) for i, (src, dst) in enumerate(zip(inputs, here))]
     for copy in copies:
         copy.start()
@@ -229,29 +225,35 @@
     src_ref[...] = state
     gap = jnp.zeros((2, stars), f32)
     old = exact_product(jnp.concatenate([state, pv, gap, aj, gap], axis=0), hot, 0)
+    tgt_ref[...] = old[0:8]
     old_ref[...] = jnp.concatenate([old[0:22], live, order.astype(f32)], axis=0)
     fac_ref[...] = target_factors(old[0:8])
 
 
-def pair_kernel(parts, fresh, *refs):
-    sources, fac_ref, refs = refs[:parts], refs[parts], refs[parts + 1 :]
-    if fresh:
-        out_ref, acc_ref, *scratch = refs
-        acc_ref[...] = jnp.zeros_like(acc_ref)
-    else:
-        in_ref, out_ref, acc_ref, *scratch = refs
-        acc_ref[...] = in_ref[...]
-    add_blocks(sources, fac_ref[...], acc_ref, scratch)
-    out_ref[...] = acc_ref[...]
-
-
-def finish_kernel(parts, *refs):
+def first_kernel(src_ref, mine_ref, theirs_ref, out_mine, out_theirs, fac_ref, *scratch):
+    factors = target_factors(theirs_ref[...])
+    fac_ref[...] = factors
+    for out in (out_mine, out_theirs):
+        out[...] = jnp.zeros_like(out)
+    add_blocks([src_ref], [mine_ref[...], factors], [out_mine, out_theirs], scratch)
+
+
+def pair_kernel(parts, sets, folded, *refs):
     sources, refs = refs[:parts], refs[parts:]
-    fac_ref, in_ref, old_ref, pv_ref, aj_ref, new_pv_ref, new_aj_ref, state_ref, acc_ref, *scratch = refs
-    stars, slots = pv_ref.shape[1], in_ref.shape[1]
-    acc_ref[...] = in_ref[...]
-    add_blocks(sources, fac_ref[...], acc_ref, scratch)
-    sums = acc_ref[0:8] + acc_ref[8:16] + acc_ref[16:24]
+    factors, sums_in, outs, scratch = refs[:sets], refs[sets : 2 * sets], refs[2 * sets : 3 * sets], refs[3 * sets :]
+    if folded:
+        outs, folded_outs, scratch = scratch[:sets], outs, scratch[sets:]
+    for out, sums in zip(outs, sums_in):
+        out[...] = sums[...]
+    add_blocks(sources, [ref[...] for ref in factors], outs, scratch)
+    if folded:
+        for out, sums in zip(folded_outs, outs):
+            out[...] = sums[0:8] + sums[8:16] + sums[16:24]
+
+
+def finish_kernel(mine_ref, other_ref, old_ref, pv_ref, aj_ref, new_pv_ref, new_aj_ref, state_ref):
+    stars = pv_ref.shape[1]
+    sums = mine_ref[...] + other_ref[...]
     old = old_ref[...]
     here, there, step_len = old[0:3], old[3:6], old[7:8]
     a1 = sums[0:3] - here * sums[6:7]
@@ -265,7 +267,7 @@
     state = jnp.where(live > 0.5, jnp.concatenate([x1, v1, a1, j1], axis=0), 0.0)
     state_ref[...] = state
     hot = one_hot(old[23:24].astype(jnp.int32), stars)
-    rows = jnp.concatenate([state, jnp.broadcast_to(live, (4, slots))], axis=0)
+    rows = jnp.concatenate([state, jnp.broadcast_to(live, (4, live.shape[1]))], axis=0)
     moved = exact_product(rows, hot, 1)
     active = moved[12:13] > 0.5
     new_pv_ref[...] = jnp.where(active, moved[0:6], pv_ref[...])
@@ -281,17 +283,18 @@
     return pl.CostEstimate(flops=pairs, bytes_accessed=4 * pairs // slots, transcendentals=pairs)
 
 
-def call_pairs(sources, factors, acc):
-    slots = factors.shape[1] // 2
-    operands = list(sources) + [factors] + ([] if acc is None else [acc])
+def call_pairs(sources, factors, sums, folded=False):
+    sets, slots = len(factors), factors[0].shape[1] // 2
+    operands = list(sources) + list(factors) + list(sums)
+    shape = (24, slots)
     return pl.pallas_call(
-        functools.partial(pair_kernel, len(sources), acc is None),
-        out_shape=jax.ShapeDtypeStruct((24, slots), f32),
+        functools.partial(pair_kernel, len(sources), sets, folded),
+        out_shape=(jax.ShapeDtypeStruct((8, slots) if folded else shape, f32),) * sets,
         in_specs=[VMEM] * len(operands),
-        out_specs=VMEM,
-        scratch_shapes=[pltpu.VMEM((24, slots), f32)] + pair_scratch(sources, slots),
+        out_specs=(VMEM,) * sets,
+        scratch_shapes=[pltpu.VMEM(shape, f32)] * (sets if folded else 0) + pair_scratch(slots),
         compiler_params=PARAMS,
-        cost_estimate=cost(sources, slots),
+        cost_estimate=cost(sources, sets * slots),
         name="pairs",
     )(*operands)
 
@@ -300,15 +303,17 @@
     stars = pos_vel.shape[1]
     inputs = [pos_vel, acc_jerk] + [values.reshape(1, -1) for values in (star_mass, step_phase, step_level, counts)]
     inputs.append(star_order)
-    own, old, factors = pl.pallas_call(
+    factor_shape = jax.ShapeDtypeStruct((FACTOR_ROWS, 2 * slots), bf16)
+    own, targets, old, mine = pl.pallas_call(
         functools.partial(prepare_kernel, slots),
         out_shape=(
             jax.ShapeDtypeStruct((8, stars), f32),
+            jax.ShapeDtypeStruct((8, slots), f32),
             jax.ShapeDtypeStruct((24, slots), f32),
-            jax.ShapeDtypeStruct((FACTOR_ROWS, 2 * slots), bf16),
+            factor_shape,
         ),
         in_specs=[HBM] * 7,
-        out_specs=(VMEM,) * 3,
+        out_specs=(VMEM,) * 4,
         scratch_shapes=[pltpu.VMEM(values.shape, values.dtype) for values in inputs] + [pltpu.SemaphoreType.DMA((7,))],
         compiler_params=PARAMS,
         name="prepare",
@@ -317,49 +322,50 @@
     def swap(values, bit):
         return lax.ppermute(values, "ja", [(i, i ^ bit) for i in range(n)])
 
-    def after(acc, *values):
-        return lax.optimization_barrier(values + (acc,))
-
-    def pairs(acc, *sources):
-        return call_pairs(sources, factors, acc)
-
-    across = swap(own, 1)
+    def after(sums, *values):
+        *values, first, second = lax.optimization_barrier(values + tuple(sums))
+        return *values, (first, second)
+
+    theirs = swap(targets, 1)
     held, arrived, bit = own, own, n // 2
     coming = swap(own, bit)
-    acc = pairs(None, own)
-    acc = pairs(acc, across)
+    *sums, theirs = pl.pallas_call(
+        first_kernel,
+        out_shape=(jax.ShapeDtypeStruct((24, slots), f32),) * 2 + (factor_shape,),
+        in_specs=[VMEM] * 3,
+        out_specs=(VMEM,) * 3,
+        scratch_shapes=pair_scratch(slots),
+        compiler_params=PARAMS,
+        cost_estimate=cost([own], 2 * slots),
+        name="first",
+    )(own, mine, theirs)
+    both = (mine, theirs)
     while bit > 4:
-        arrived, acc = after(acc, coming)
+        arrived, sums = after(sums, coming)
         held = jnp.concatenate([held, arrived], axis=0)
         bit //= 2
-        across = swap(arrived, 1)
         beside = swap(held, 2) if bit == 4 else None
         coming = swap(held, bit)
-        acc = pairs(acc, arrived)
-        acc = pairs(acc, across)
-    arrived, beside, acc = after(acc, coming, beside)
-    beside_across = swap(beside, 1)
-    across = swap(arrived, 1)
+        sums = call_pairs([arrived], both, sums)
+    arrived, beside, sums = after(sums, coming, beside)
     coming = swap(arrived, 2)
-    acc = pairs(acc, arrived, beside)
-    acc = pairs(acc, across, beside_across)
-    last, acc = after(acc, coming)
-    across = swap(last, 1)
-    acc = pairs(acc, last)
+    sums = call_pairs([arrived, beside], both, sums)
+    last, sums = after(sums, coming)
+    (for_them,) = call_pairs([last], [theirs], [sums[1]], folded=True)
+    from_them = swap(for_them, 1)
+    (here,) = call_pairs([last], [mine], [sums[0]], folded=True)
     return pl.pallas_call(
-        functools.partial(finish_kernel, 1),
+        finish_kernel,
         out_shape=(
             jax.ShapeDtypeStruct(pos_vel.shape, f32),
             jax.ShapeDtypeStruct(acc_jerk.shape, f32),
             jax.ShapeDtypeStruct((12, slots), f32),
         ),
-        in_specs=[VMEM] * 6,
+        in_specs=[VMEM] * 5,
         out_specs=(VMEM,) * 3,
-        scratch_shapes=[pltpu.VMEM((24, slots), f32)] + pair_scratch([across], slots),
         compiler_params=PARAMS,
-        cost_estimate=cost([across], slots),
         name="finish",
-    )(across, factors, acc, old, pos_vel, acc_jerk)
+    )(here, from_them, old, pos_vel, acc_jerk)
 
 
 A_DEV = 128

time: 26.2 us -> 24.9 us (0.950)
  Pallas kernels: 15.4 us -> 14 us
  waiting for transfers between devices: 0.03 us -> 0.45 us
    pallas_call x8 -> x6, Pallas kernels: 13.9 us -> 12.5 us  [the longest x4 9.96 us: call_pairs(): pl.pallas_call(functools.partial(pair_kernel, len(sources), sets, folded)...]
    ppermute x9 -> x6, waiting for transfers between devices: 0.03 us -> 0.45 us  [swap(): return lax.ppermute(values, 'ja', [(i, i ^ bit) for i in range(n)])]
    ppermute x9 -> x6, starting transfers between devices: 9.09 us -> 8.92 us  [swap(): return lax.ppermute(values, 'ja', [(i, i ^ bit) for i in range(n)])]
  transfers between devices with their start and end apart: 9 -> 6, of which waited for: 0 -> 2; matrix products, arithmetic and copies ran while one was open for 0% -> 0% of each run, Pallas kernels for 44% -> 40%
where the time goes in v4:
time: 24.9 us; the launch traced here: 24.7 us
  Pallas kernels  14 us (56%)
  starting transfers between devices  8.92 us (36%)
  between operations  1.37 us (6%)
  waiting for transfers between devices  0.45 us (2%)
    pallas_call x4, Pallas kernels, call_pairs(): pl.pallas_call(functools.partial(pair_kernel, len(sources), sets, folded)...  9.96 us
    ppermute x6, starting transfers between devices, swap(): return lax.ppermute(values, 'ja', [(i, i ^ bit) for i in range(n)])  8.92 us
    pallas_call x1, Pallas kernels, per_device(): pl.pallas_call(first_kernel, out_shape=(jax.ShapeDtypeStruct((24, slots),...  1.61 us
    pallas_call x1, Pallas kernels, per_device(): pl.pallas_call(functools.partial(prepare_kernel, slots), out_shape=(jax.S...  1.47 us
    pallas_call x1, Pallas kernels, per_device(): pl.pallas_call(finish_kernel, out_shape=(jax.ShapeDtypeStruct(pos_vel.sha...  0.91 us
  transfers between devices with their start and end apart: 6, of which 2 were waited for; matrix products, arithmetic and copies ran while one was open for 0% of the time, Pallas kernels for 40%

profile of v4, /device:TPU:1, one launch (start us, length us, event | category | flops | bytes accessed | tf_op | source)
XLA Modules:
  0.0 24.7 jit_solution(471065696723664747)
XLA Ops:
  1.3 1.5 %prepare.1 = (f32[8,1024]{1,0:T(8,128)S(1)}, f32[8,256]{1,0:T(8,128)S(1)}, f32[24,256]{1,0:T(8,128)S(1)}, bf16[128,512]{1,0:T(8,128)(2,1)S(1)}) custom-call(f32[6,1024]{1,0:T(8,128)} %pv_ref.1, f32[6,1024]{1,0:T(8,128)} %aj_ref.1, f32[1,1024]{1,0:T(1,128)} %bitcast.5, f32[1,1024]{1,0:T(1,128)} %bitcast.6, s32[1,1024]{1,0:T(1,128)} %bitcast.7, ...), custom_call_target="tpu_custom_call" | custom-call | tf_op jit(solution)/shard_map/prepare/pallas_call | solution.py:307
  2.8 0.1 collective-permute-start.1
  2.9 3.8 %collective-permute-start = (f32[8,1024]{1,0:T(8,128)S(1)}, f32[8,1024]{1,0:T(8,128)S(1)}, u32[]{:S(2)}, u32[]{:S(2)}) collective-permute-start(f32[8,1024]{1,0:T(8,128)S(1)} %get-tuple-element.24.src_ref), channel_id=1, source_target_pairs={{0,8},{1,9},{2,10},{3,11},{4,12},{5,13},{6,14},{7,15},{8,0},{9,1},... | collective-permute-start | bytes 98312 | tf_op jit(solution)/shard_map/ppermute | solution.py:323
  6.7 0.0 collective-permute-done.1.theirs_ref
  6.7 1.6 %first.1 = (f32[24,256]{1,0:T(8,128)S(1)}, f32[24,256]{1,0:T(8,128)S(1)}, bf16[128,512]{1,0:T(8,128)(2,1)S(1)}) custom-call(f32[8,1024]{1,0:T(8,128)S(1)} %get-tuple-element.24.src_ref, bf16[128,512]{1,0:T(8,128)(2,1)S(1)} %get-tuple-element.25.mine_ref.refs_1_.refs_2_, f32[8,256]{1,0:T(8,128)S(1)} %collective-permute-done.1.theirs_ref), custom_call_target="tpu_custom_call" | custom-call | flops 524288 | bytes 4096 | tf_op jit(solution)/shard_map/first/pallas_call | solution.py:332
  8.3 0.1 collective-permute-done.refs_0_
  8.3 1.2 %collective-permute-start.3 = (f32[16,1024]{1,0:T(8,128)S(1)}, f32[16,1024]{1,0:T(8,128)S(1)}, u32[]{:S(2)}, u32[]{:S(2)}) collective-permute-start(f32[16,1024]{1,0:T(8,128)S(1)} %constant_dynamic-update-slice_fusion), channel_id=1, source_target_pairs={{0,2},{1,3},{2,0},{3,1},{4,6},{5,7},{6,4},{7,5},{8,10},{9,11},{10,... | collective-permute-start | bytes 196616 | tf_op jit(solution)/shard_map/ppermute | solution.py:323
  9.6 1.3 %collective-permute-start.2 = (f32[16,1024]{1,0:T(8,128)S(1)}, f32[16,1024]{1,0:T(8,128)S(1)}, u32[]{:S(2)}, u32[]{:S(2)}) collective-permute-start(f32[16,1024]{1,0:T(8,128)S(1)} %constant_dynamic-update-slice_fusion), channel_id=1, source_target_pairs={{0,4},{1,5},{2,6},{3,7},{4,0},{5,1},{6,2},{7,3},{8,12},{9,13},{10,... | collective-permute-start | bytes 196616 | tf_op jit(solution)/shard_map/ppermute | solution.py:323
  10.9 1.6 %pairs.4 = (f32[24,256]{1,0:T(8,128)S(1)}, f32[24,256]{1,0:T(8,128)S(1)}) custom-call(f32[8,1024]{1,0:T(8,128)S(1)} %collective-permute-done.refs_0_, bf16[128,512]{1,0:T(8,128)(2,1)S(1)} %get-tuple-element.25.mine_ref.refs_1_.refs_2_, bf16[128,512]{1,0:T(8,128)(2,1)S(1)} %get-tuple-element.30.refs_2_.refs_3_.refs_1_, ...), custom_call_target="tpu_custom_call" | custom-call | flops 524288 | bytes 4096 | tf_op jit(solution)/shard_map/pairs/pallas_call | solution.py:290
  12.5 0.0 collective-permute-done.3.refs_1_
  12.5 0.4 %collective-permute-done.2.refs_0_ = f32[16,1024]{1,0:T(8,128)S(1)} collective-permute-done((f32[16,1024]{1,0:T(8,128)S(1)}, f32[16,1024]{1,0:T(8,128)S(1)}, u32[]{:S(2)}, u32[]{:S(2)}) %collective-permute-start.2) | collective-permute-done | bytes 65568 | tf_op jit(solution)/shard_map/ppermute | solution.py:323
  12.9 0.1 collective-permute-start.4
  12.9 5.1 %pairs.5 = (f32[24,256]{1,0:T(8,128)S(1)}, f32[24,256]{1,0:T(8,128)S(1)}) custom-call(f32[16,1024]{1,0:T(8,128)S(1)} %collective-permute-done.2.refs_0_, f32[16,1024]{1,0:T(8,128)S(1)} %collective-permute-done.3.refs_1_, bf16[128,512]{1,0:T(8,128)(2,1)S(1)} %get-tuple-element.25.mine_ref.refs_1_.refs_2_, ...), custom_call_target="tpu_custom_call" | custom-call | flops 2097152 | bytes 16384 | tf_op jit(solution)/shard_map/pairs/pallas_call | solution.py:290
  18.1 0.0 collective-permute-done.4.refs_0_
  18.1 1.6 %pairs.7 = f32[8,256]{1,0:T(8,128)S(1)} custom-call(f32[16,1024]{1,0:T(8,128)S(1)} %collective-permute-done.4.refs_0_, bf16[128,512]{1,0:T(8,128)(2,1)S(1)} %get-tuple-element.30.refs_2_.refs_3_.refs_1_, f32[24,256]{1,0:T(8,128)S(1)} %get-tuple-element.43.refs_2_), custom_call_target="tpu_custom_call" | custom-call | flops 524288 | bytes 8192 | tf_op jit(solution)/shard_map/pairs/pallas_call | solution.py:290
  19.7 0.0 copy-start
  19.7 0.0 copy-start.1
  19.8 2.4 %collective-permute-start.5 = (f32[8,256]{1,0:T(8,128)S(1)}, f32[8,256]{1,0:T(8,128)S(1)}, u32[]{:S(2)}, u32[]{:S(2)}) collective-permute-start(f32[8,256]{1,0:T(8,128)S(1)} %pairs.7), channel_id=1, source_target_pairs={{0,1},{1,0},{2,3},{3,2},{4,5},{5,4},{6,7},{7,6},{8,9},{9,8},{10,11... | collective-permute-start | bytes 24584 | tf_op jit(solution)/shard_map/ppermute | solution.py:323
  22.2 1.6 %pairs.6.mine_ref = f32[8,256]{1,0:T(8,128)S(1)} custom-call(f32[16,1024]{1,0:T(8,128)S(1)} %collective-permute-done.4.refs_0_, bf16[128,512]{1,0:T(8,128)(2,1)S(1)} %get-tuple-element.25.mine_ref.refs_1_.refs_2_, f32[24,256]{1,0:T(8,128)S(1)} %get-tuple-element.42.refs_2_), custom_call_target="tpu_custom_call" | custom-call | flops 524288 | bytes 8192 | tf_op jit(solution)/shard_map/pairs/pallas_call | solution.py:290
  23.8 0.0 collective-permute-done.5.other_ref
  23.8 0.0 copy-done
  23.8 0.0 copy-done.1
  23.8 0.9 %finish.1 = (f32[6,1024]{1,0:T(8,128)}, f32[6,1024]{1,0:T(8,128)}, f32[12,256]{1,0:T(8,128)}) custom-call(f32[8,256]{1,0:T(8,128)S(1)} %pairs.6.mine_ref, f32[8,256]{1,0:T(8,128)S(1)} %collective-permute-done.5.other_ref, f32[24,256]{1,0:T(8,128)S(1)} %get-tuple-element.44.old_ref, f32[6,1024]{1,0:T(8,128)S(1)} %copy-done, f32[6,1024]{1,0:T(8,128)S(1)} %copy-done.1), custom_call_target="tpu_custom_call" | custom-call | tf_op jit(solution)/shard_map/finish/pallas_call | solution.py:357
  (2 shorter events, 0.0 us)
Async XLA Ops:
  2.8 3.9 %collective-permute-start.1 = (f32[8,256]{1,0:T(8,128)S(1)}, f32[8,256]{1,0:T(8,128)S(1)}, u32[]{:S(2)}, u32[]{:S(2)}) collective-permute-start(f32[8,256]{1,0:T(8,128)S(1)} %get-tuple-element.26), channel_id=1, source_target_pairs={{0,1},{1,0},{2,3},{3,2},{4,5},{5,4},{6,7},{7,6},{8,9},{9,8},{10,11... | collective-permute-start | bytes 24584 | tf_op jit(solution)/shard_map/ppermute | solution.py:323
  2.9 5.4 %collective-permute-start = (f32[8,1024]{1,0:T(8,128)S(1)}, f32[8,1024]{1,0:T(8,128)S(1)}, u32[]{:S(2)}, u32[]{:S(2)}) collective-permute-start(f32[8,1024]{1,0:T(8,128)S(1)} %get-tuple-element.24.src_ref), channel_id=1, source_target_pairs={{0,8},{1,9},{2,10},{3,11},{4,12},{5,13},{6,14},{7,15},{8,0},{9,1},... | collective-permute-start | bytes 98312 | tf_op jit(solution)/shard_map/ppermute | solution.py:323
  8.3 4.2 %collective-permute-start.3 = (f32[16,1024]{1,0:T(8,128)S(1)}, f32[16,1024]{1,0:T(8,128)S(1)}, u32[]{:S(2)}, u32[]{:S(2)}) collective-permute-start(f32[16,1024]{1,0:T(8,128)S(1)} %constant_dynamic-update-slice_fusion), channel_id=1, source_target_pairs={{0,2},{1,3},{2,0},{3,1},{4,6},{5,7},{6,4},{7,5},{8,10},{9,11},{10,... | collective-permute-start | bytes 196616 | tf_op jit(solution)/shard_map/ppermute | solution.py:323
  9.6 3.3 %collective-permute-start.2 = (f32[16,1024]{1,0:T(8,128)S(1)}, f32[16,1024]{1,0:T(8,128)S(1)}, u32[]{:S(2)}, u32[]{:S(2)}) collective-permute-start(f32[16,1024]{1,0:T(8,128)S(1)} %constant_dynamic-update-slice_fusion), channel_id=1, source_target_pairs={{0,4},{1,5},{2,6},{3,7},{4,0},{5,1},{6,2},{7,3},{8,12},{9,13},{10,... | collective-permute-start | bytes 196616 | tf_op jit(solution)/shard_map/ppermute | solution.py:323
  12.9 5.2 %collective-permute-start.4 = (f32[16,1024]{1,0:T(8,128)S(1)}, f32[16,1024]{1,0:T(8,128)S(1)}, u32[]{:S(2)}, u32[]{:S(2)}) collective-permute-start(f32[16,1024]{1,0:T(8,128)S(1)} %collective-permute-done.2.refs_0_), channel_id=1, source_target_pairs={{0,2},{1,3},{2,0},{3,1},{4,6},{5,7},{6,4},{7,5},{8,10},{9,11},{10,... | collective-permute-start | bytes 196616 | tf_op jit(solution)/shard_map/ppermute | solution.py:323
  19.7 4.1 %copy-start = (f32[6,1024]{1,0:T(8,128)S(1)}, f32[6,1024]{1,0:T(8,128)}, u32[]{:S(2)}) copy-start(f32[6,1024]{1,0:T(8,128)} %pv_ref.1) | copy-start | bytes 73732
  19.7 4.1 %copy-start.1 = (f32[6,1024]{1,0:T(8,128)S(1)}, f32[6,1024]{1,0:T(8,128)}, u32[]{:S(2)}) copy-start(f32[6,1024]{1,0:T(8,128)} %aj_ref.1) | copy-start | bytes 73732
  19.8 4.0 %collective-permute-start.5 = (f32[8,256]{1,0:T(8,128)S(1)}, f32[8,256]{1,0:T(8,128)S(1)}, u32[]{:S(2)}, u32[]{:S(2)}) collective-permute-start(f32[8,256]{1,0:T(8,128)S(1)} %pairs.7), channel_id=1, source_target_pairs={{0,1},{1,0},{2,3},{3,2},{4,5},{5,4},{6,7},{7,6},{8,9},{9,8},{10,11... | collective-permute-start | bytes 24584 | tf_op jit(solution)/shard_map/ppermute | solution.py:323

commit v5 on v4

--- a/solution.py
+++ b/solution.py
@@ -15,7 +15,6 @@
 CHUNK = 128
 TOGETHER = 4
 FACTOR_ROWS = 128
-RING = 16
 PARAMS = pltpu.CompilerParams(vmem_limit_bytes=32 << 20)
 
 
@@ -104,80 +103,55 @@
     )
 
 
-def add_pairs(states, factors, sums, scratch):
-    slots = factors[0].shape[1] // 2
-    products, weights = scratch[:RING], scratch[RING:]
-    per, sets = states[0].shape[1] // CHUNK, len(factors)
-    ready = {}
-
-    def prepare(b):
-        ready[b] = (source_factors(states[b]).T,) + sum_factors(states[b])
-
-    def place(c):
-        c = c // sets
-        return c // per, slice(c % per * CHUNK, (c % per + 1) * CHUNK)
-
-    def multiply(c):
-        b, span = place(c)
-        products[c % RING][...] = jnp.dot(ready[b][0][span], factors[c % sets], preferred_element_type=f32)
-
-    def weigh(c):
-        product, out = products[c % RING], weights[c % RING]
-        for g in range(0, CHUNK, 16):
-            for lane in range(0, slots, 128):
-                cols = slice(lane, lane + 128)
-                radial = product[g : g + 16, cols]
-                dist_sq = product[g : g + 16, slots + lane : slots + lane + 128]
-                inverse = lax.rsqrt(dist_sq)
-                inverse_sq = inverse * inverse
-                weight = inverse * inverse_sq
-                radial = weight * (inverse_sq * radial)
-                weight_hi, radial_hi = weight.astype(bf16), radial.astype(bf16)
-                out[g : g + 16, cols] = weight_hi
-                out[CHUNK + g : CHUNK + g + 16, cols] = (weight - weight_hi.astype(f32)).astype(bf16)
-                out[2 * CHUNK + g : 2 * CHUNK + g + 16, cols] = radial_hi
-                out[3 * CHUNK + g : 3 * CHUNK + g + 16, cols] = (radial - radial_hi.astype(f32)).astype(bf16)
-
-    def total(c):
-        b, span = place(c)
-        left = [ready[b][1][:, span]] * 2 + [ready[b][2][:, span]] * 2
-        sums[c % sets][...] += jnp.dot(
-            jnp.concatenate(left, axis=1), weights[c % RING][...], preferred_element_type=f32
-        )
-
-    steps = len(states) * per * sets
-    prepare(0)
-    multiply(0)
-    for c in range(steps):
-        if (c + 2) % (per * sets) == 0 and (c + 2) // (per * sets) < len(states):
-            prepare((c + 2) // (per * sets))
-        if c + 1 < steps:
-            multiply(c + 1)
-        weigh(c)
-        if c > 0:
-            total(c - 1)
-    total(steps - 1)
-
-
-def add_blocks(sources, factors, sums, scratch):
+def pair_weights(products):
+    sources, slots = products.shape[0], products.shape[1] // 2
+    parts = [[], [], [], []]
+    for g in range(0, sources, 16):
+        rows = [[], [], [], []]
+        for lane in range(0, slots, 128):
+            radial = products[g : g + 16, lane : lane + 128]
+            dist_sq = products[g : g + 16, slots + lane : slots + lane + 128]
+            inverse = lax.rsqrt(dist_sq)
+            inverse_sq = inverse * inverse
+            weight = inverse * inverse_sq
+            radial = weight * (inverse_sq * radial)
+            weight_hi, radial_hi = weight.astype(bf16), radial.astype(bf16)
+            rows[0].append(weight_hi)
+            rows[1].append((weight - weight_hi.astype(f32)).astype(bf16))
+            rows[2].append(radial_hi)
+            rows[3].append((radial - radial_hi.astype(f32)).astype(bf16))
+        for part, row in zip(parts, rows):
+            part.append(jnp.concatenate(row, axis=1))
+    return jnp.concatenate(parts[0] + parts[1] + parts[2] + parts[3], axis=0)
+
+
+def add_pairs(states, factors, sums):
+    for state in states:
+        factors_s = source_factors(state).T
+        by_weight, by_radial = sum_factors(state)
+        for at in range(0, state.shape[1], CHUNK):
+            span = slice(at, at + CHUNK)
+            left = jnp.concatenate([by_weight[:, span]] * 2 + [by_radial[:, span]] * 2, axis=1)
+            for factors_t, out in zip(factors, sums):
+                products = jnp.dot(factors_s[span], factors_t, preferred_element_type=f32)
+                out[...] += jnp.dot(left, pair_weights(products), preferred_element_type=f32)
+
+
+def add_blocks(sources, factors, sums):
     counts = [ref.shape[0] // 8 for ref in sources]
     if sum(counts) <= TOGETHER:
         rows = [ref[b : b + 8] for ref in sources for b in range(0, ref.shape[0], 8)]
-        add_pairs(rows, factors, sums, scratch)
+        add_pairs(rows, factors, sums)
         return
     together = next(t for t in range(TOGETHER, 0, -1) if all(c % t == 0 for c in counts))
     for ref, count in zip(sources, counts):
 
         def step(i, _):
             rows = [ref[pl.ds(pl.multiple_of((i * together + b) * 8, 8), 8), :] for b in range(together)]
-            add_pairs(rows, factors, sums, scratch)
+            add_pairs(rows, factors, sums)
             return 0
 
         lax.fori_loop(0, count // together, step, 0)
-
-
-def pair_scratch(slots):
-    return [pltpu.VMEM((CHUNK, 2 * slots), f32)] * RING + [pltpu.VMEM((4 * CHUNK, slots), bf16)] * RING
 
 
 def one_hot(order, stars):
@@ -230,22 +204,22 @@
     fac_ref[...] = target_factors(old[0:8])
 
 
-def first_kernel(src_ref, mine_ref, theirs_ref, out_mine, out_theirs, fac_ref, *scratch):
+def first_kernel(src_ref, mine_ref, theirs_ref, out_mine, out_theirs, fac_ref):
     factors = target_factors(theirs_ref[...])
     fac_ref[...] = factors
     for out in (out_mine, out_theirs):
         out[...] = jnp.zeros_like(out)
-    add_blocks([src_ref], [mine_ref[...], factors], [out_mine, out_theirs], scratch)
+    add_blocks([src_ref], [mine_ref[...], factors], [out_mine, out_theirs])
 
 
 def pair_kernel(parts, sets, folded, *refs):
     sources, refs = refs[:parts], refs[parts:]
-    factors, sums_in, outs, scratch = refs[:sets], refs[sets : 2 * sets], refs[2 * sets : 3 * sets], refs[3 * sets :]
+    factors, sums_in, outs, rest = refs[:sets], refs[sets : 2 * sets], refs[2 * sets : 3 * sets], refs[3 * sets :]
     if folded:
-        outs, folded_outs, scratch = scratch[:sets], outs, scratch[sets:]
+        outs, folded_outs = rest, outs
     for out, sums in zip(outs, sums_in):
         out[...] = sums[...]
-    add_blocks(sources, [ref[...] for ref in factors], outs, scratch)
+    add_blocks(sources, [ref[...] for ref in factors], outs)
     if folded:
         for out, sums in zip(folded_outs, outs):
             out[...] = sums[0:8] + sums[8:16] + sums[16:24]
@@ -292,7 +266,7 @@
         out_shape=(jax.ShapeDtypeStruct((8, slots) if folded else shape, f32),) * sets,
         in_specs=[VMEM] * len(operands),
         out_specs=(VMEM,) * sets,
-        scratch_shapes=[pltpu.VMEM(shape, f32)] * (sets if folded else 0) + pair_scratch(slots),
+        scratch_shapes=[pltpu.VMEM(shape, f32)] * (sets if folded else 0),
         compiler_params=PARAMS,
         cost_estimate=cost(sources, sets * slots),
         name="pairs",
@@ -334,7 +308,6 @@
         out_shape=(jax.ShapeDtypeStruct((24, slots), f32),) * 2 + (factor_shape,),
         in_specs=[VMEM] * 3,
         out_specs=(VMEM,) * 3,
-        scratch_shapes=pair_scratch(slots),
         compiler_params=PARAMS,
         cost_estimate=cost([own], 2 * slots),
         name="first",
@@ -347,8 +320,9 @@
         beside = swap(held, 2) if bit == 4 else None
         coming = swap(held, bit)
         sums = call_pairs([arrived], both, sums)
-    arrived, beside, sums = after(sums, coming, beside)
+    arrived, sums = after(sums, coming)
     coming = swap(arrived, 2)
+    beside, sums = after(sums, beside)
     sums = call_pairs([arrived, beside], both, sums)
     last, sums = after(sums, coming)
     (for_them,) = call_pairs([last], [theirs], [sums[1]], folded=True)

time: 24.9 us -> 24 us (0.964)
  Pallas kernels: 14 us -> 12.9 us
    pallas_call x4, Pallas kernels: 9.96 us -> 9.07 us  [call_pairs(): pl.pallas_call(functools.partial(pair_kernel, len(sources), sets, folded)...]
  transfers between devices with their start and end apart: 6 -> 6, of which waited for: 2 -> 2; matrix products, arithmetic and copies ran while one was open for 0% -> 0% of each run, Pallas kernels for 40% -> 38%
where the time goes in v5:
time: 24 us; the launch traced here: 23.8 us
  Pallas kernels  12.9 us (54%)
  starting transfers between devices  8.91 us (37%)
  between operations  1.37 us (6%)
  waiting for transfers between devices  0.65 us (3%)
    pallas_call x4, Pallas kernels, call_pairs(): pl.pallas_call(functools.partial(pair_kernel, len(sources), sets, folded)...  9.07 us
    ppermute x6, starting transfers between devices, swap(): return lax.ppermute(values, 'ja', [(i, i ^ bit) for i in range(n)])  8.91 us
    pallas_call x1, Pallas kernels, per_device(): pl.pallas_call(functools.partial(prepare_kernel, slots), out_shape=(jax.S...  1.47 us
    pallas_call x1, Pallas kernels, per_device(): pl.pallas_call(first_kernel, out_shape=(jax.ShapeDtypeStruct((24, slots),...  1.4 us
    pallas_call x1, Pallas kernels, per_device(): pl.pallas_call(finish_kernel, out_shape=(jax.ShapeDtypeStruct(pos_vel.sha...  0.91 us
    ppermute x6, waiting for transfers between devices, swap(): return lax.ppermute(values, 'ja', [(i, i ^ bit) for i in range(n)])  0.65 us
  transfers between devices with their start and end apart: 6, of which 2 were waited for; matrix products, arithmetic and copies ran while one was open for 0% of the time, Pallas kernels for 38%

profile of v5, /device:TPU:1, one launch (start us, length us, event | category | flops | bytes accessed | tf_op | source)
XLA Modules:
  0.0 23.8 jit_solution(799402047532360324)
XLA Ops:
  1.3 1.5 %prepare.1 = (f32[8,1024]{1,0:T(8,128)S(1)}, f32[8,256]{1,0:T(8,128)S(1)}, f32[24,256]{1,0:T(8,128)S(1)}, bf16[128,512]{1,0:T(8,128)(2,1)S(1)}) custom-call(f32[6,1024]{1,0:T(8,128)} %pv_ref.1, f32[6,1024]{1,0:T(8,128)} %aj_ref.1, f32[1,1024]{1,0:T(1,128)} %bitcast.5, f32[1,1024]{1,0:T(1,128)} %bitcast.6, s32[1,1024]{1,0:T(1,128)} %bitcast.7, ...), custom_call_target="tpu_custom_call" | custom-call | tf_op jit(solution)/shard_map/prepare/pallas_call | solution.py:281
  2.8 0.1 collective-permute-start.1
  2.9 3.8 %collective-permute-start = (f32[8,1024]{1,0:T(8,128)S(1)}, f32[8,1024]{1,0:T(8,128)S(1)}, u32[]{:S(2)}, u32[]{:S(2)}) collective-permute-start(f32[8,1024]{1,0:T(8,128)S(1)} %get-tuple-element.26.src_ref), channel_id=1, source_target_pairs={{0,8},{1,9},{2,10},{3,11},{4,12},{5,13},{6,14},{7,15},{8,0},{9,1},... | collective-permute-start | bytes 98312 | tf_op jit(solution)/shard_map/ppermute | solution.py:297
  6.7 0.0 collective-permute-done.1.theirs_ref
  6.7 1.4 %first.1 = (f32[24,256]{1,0:T(8,128)S(1)}, f32[24,256]{1,0:T(8,128)S(1)}, bf16[128,512]{1,0:T(8,128)(2,1)S(1)}) custom-call(f32[8,1024]{1,0:T(8,128)S(1)} %get-tuple-element.26.src_ref, bf16[128,512]{1,0:T(8,128)(2,1)S(1)} %get-tuple-element.27.mine_ref.refs_1_.refs_2_, f32[8,256]{1,0:T(8,128)S(1)} %collective-permute-done.1.theirs_ref), custom_call_target="tpu_custom_call" | custom-call | flops 524288 | bytes 4096 | tf_op jit(solution)/shard_map/first/pallas_call | solution.py:306
  8.1 0.3 %collective-permute-done.refs_0_ = f32[8,1024]{1,0:T(8,128)S(1)} collective-permute-done((f32[8,1024]{1,0:T(8,128)S(1)}, f32[8,1024]{1,0:T(8,128)S(1)}, u32[]{:S(2)}, u32[]{:S(2)}) %collective-permute-start) | collective-permute-done | bytes 32800 | tf_op jit(solution)/shard_map/ppermute | solution.py:297
  8.3 1.1 %collective-permute-start.2 = (f32[16,1024]{1,0:T(8,128)S(1)}, f32[16,1024]{1,0:T(8,128)S(1)}, u32[]{:S(2)}, u32[]{:S(2)}) collective-permute-start(f32[16,1024]{1,0:T(8,128)S(1)} %constant_dynamic-update-slice_fusion), channel_id=1, source_target_pairs={{0,4},{1,5},{2,6},{3,7},{4,0},{5,1},{6,2},{7,3},{8,12},{9,13},{10,... | collective-permute-start | bytes 196616 | tf_op jit(solution)/shard_map/ppermute | solution.py:297
  9.5 1.2 %collective-permute-start.4 = (f32[16,1024]{1,0:T(8,128)S(1)}, f32[16,1024]{1,0:T(8,128)S(1)}, u32[]{:S(2)}, u32[]{:S(2)}) collective-permute-start(f32[16,1024]{1,0:T(8,128)S(1)} %constant_dynamic-update-slice_fusion), channel_id=1, source_target_pairs={{0,2},{1,3},{2,0},{3,1},{4,6},{5,7},{6,4},{7,5},{8,10},{9,11},{10,... | collective-permute-start | bytes 196616 | tf_op jit(solution)/shard_map/ppermute | solution.py:297
  10.7 1.4 %pairs.4 = (f32[24,256]{1,0:T(8,128)S(1)}, f32[24,256]{1,0:T(8,128)S(1)}) custom-call(f32[8,1024]{1,0:T(8,128)S(1)} %collective-permute-done.refs_0_, bf16[128,512]{1,0:T(8,128)(2,1)S(1)} %get-tuple-element.27.mine_ref.refs_1_.refs_2_, bf16[128,512]{1,0:T(8,128)(2,1)S(1)} %get-tuple-element.32.refs_2_.refs_3_.refs_1_, ...), custom_call_target="tpu_custom_call" | custom-call | flops 524288 | bytes 4096 | tf_op jit(solution)/shard_map/pairs/pallas_call | solution.py:264
  12.1 0.0 collective-permute-done.2.refs_0_
  12.1 0.4 %collective-permute-start.3 = (f32[16,1024]{1,0:T(8,128)S(1)}, f32[16,1024]{1,0:T(8,128)S(1)}, u32[]{:S(2)}, u32[]{:S(2)}) collective-permute-start(f32[16,1024]{1,0:T(8,128)S(1)} %collective-permute-done.2.refs_0_), channel_id=1, source_target_pairs={{0,2},{1,3},{2,0},{3,1},{4,6},{5,7},{6,4},{7,5},{8,10},{9,11},{10,... | collective-permute-start | bytes 196616 | tf_op jit(solution)/shard_map/ppermute | solution.py:297
  12.5 0.4 %collective-permute-done.4.refs_1_ = f32[16,1024]{1,0:T(8,128)S(1)} collective-permute-done((f32[16,1024]{1,0:T(8,128)S(1)}, f32[16,1024]{1,0:T(8,128)S(1)}, u32[]{:S(2)}, u32[]{:S(2)}) %collective-permute-start.4) | collective-permute-done | bytes 65568 | tf_op jit(solution)/shard_map/ppermute | solution.py:297
  12.9 4.8 %pairs.5 = (f32[24,256]{1,0:T(8,128)S(1)}, f32[24,256]{1,0:T(8,128)S(1)}) custom-call(f32[16,1024]{1,0:T(8,128)S(1)} %collective-permute-done.2.refs_0_, f32[16,1024]{1,0:T(8,128)S(1)} %collective-permute-done.4.refs_1_, bf16[128,512]{1,0:T(8,128)(2,1)S(1)} %get-tuple-element.27.mine_ref.refs_1_.refs_2_, ...), custom_call_target="tpu_custom_call" | custom-call | flops 2097152 | bytes 16384 | tf_op jit(solution)/shard_map/pairs/pallas_call | solution.py:264
  17.7 0.0 collective-permute-done.3.refs_0_
  17.7 1.4 %pairs.7 = f32[8,256]{1,0:T(8,128)S(1)} custom-call(f32[16,1024]{1,0:T(8,128)S(1)} %collective-permute-done.3.refs_0_, bf16[128,512]{1,0:T(8,128)(2,1)S(1)} %get-tuple-element.32.refs_2_.refs_3_.refs_1_, f32[24,256]{1,0:T(8,128)S(1)} %get-tuple-element.47.refs_2_), custom_call_target="tpu_custom_call" | custom-call | flops 524288 | bytes 8192 | tf_op jit(solution)/shard_map/pairs/pallas_call | solution.py:264
  19.1 0.0 copy-start
  19.1 0.0 copy-start.1
  19.1 2.3 %collective-permute-start.5 = (f32[8,256]{1,0:T(8,128)S(1)}, f32[8,256]{1,0:T(8,128)S(1)}, u32[]{:S(2)}, u32[]{:S(2)}) collective-permute-start(f32[8,256]{1,0:T(8,128)S(1)} %pairs.7), channel_id=1, source_target_pairs={{0,1},{1,0},{2,3},{3,2},{4,5},{5,4},{6,7},{7,6},{8,9},{9,8},{10,11... | collective-permute-start | bytes 24584 | tf_op jit(solution)/shard_map/ppermute | solution.py:297
  21.4 1.4 %pairs.6.mine_ref = f32[8,256]{1,0:T(8,128)S(1)} custom-call(f32[16,1024]{1,0:T(8,128)S(1)} %collective-permute-done.3.refs_0_, bf16[128,512]{1,0:T(8,128)(2,1)S(1)} %get-tuple-element.27.mine_ref.refs_1_.refs_2_, f32[24,256]{1,0:T(8,128)S(1)} %get-tuple-element.46.refs_2_), custom_call_target="tpu_custom_call" | custom-call | flops 524288 | bytes 8192 | tf_op jit(solution)/shard_map/pairs/pallas_call | solution.py:264
  22.9 0.0 collective-permute-done.5.other_ref
  22.9 0.0 copy-done
  22.9 0.0 copy-done.1
  22.9 0.9 %finish.1 = (f32[6,1024]{1,0:T(8,128)}, f32[6,1024]{1,0:T(8,128)}, f32[12,256]{1,0:T(8,128)}) custom-call(f32[8,256]{1,0:T(8,128)S(1)} %pairs.6.mine_ref, f32[8,256]{1,0:T(8,128)S(1)} %collective-permute-done.5.other_ref, f32[24,256]{1,0:T(8,128)S(1)} %get-tuple-element.48.old_ref, f32[6,1024]{1,0:T(8,128)S(1)} %copy-done, f32[6,1024]{1,0:T(8,128)S(1)} %copy-done.1), custom_call_target="tpu_custom_call" | custom-call | tf_op jit(solution)/shard_map/finish/pallas_call | solution.py:331
  (2 shorter events, 0.0 us)
Async XLA Ops:
  2.8 3.9 %collective-permute-start.1 = (f32[8,256]{1,0:T(8,128)S(1)}, f32[8,256]{1,0:T(8,128)S(1)}, u32[]{:S(2)}, u32[]{:S(2)}) collective-permute-start(f32[8,256]{1,0:T(8,128)S(1)} %get-tuple-element.28), channel_id=1, source_target_pairs={{0,1},{1,0},{2,3},{3,2},{4,5},{5,4},{6,7},{7,6},{8,9},{9,8},{10,11... | collective-permute-start | bytes 24584 | tf_op jit(solution)/shard_map/ppermute | solution.py:297
  2.9 5.4 %collective-permute-start = (f32[8,1024]{1,0:T(8,128)S(1)}, f32[8,1024]{1,0:T(8,128)S(1)}, u32[]{:S(2)}, u32[]{:S(2)}) collective-permute-start(f32[8,1024]{1,0:T(8,128)S(1)} %get-tuple-element.26.src_ref), channel_id=1, source_target_pairs={{0,8},{1,9},{2,10},{3,11},{4,12},{5,13},{6,14},{7,15},{8,0},{9,1},... | collective-permute-start | bytes 98312 | tf_op jit(solution)/shard_map/ppermute | solution.py:297
  8.3 3.8 %collective-permute-start.2 = (f32[16,1024]{1,0:T(8,128)S(1)}, f32[16,1024]{1,0:T(8,128)S(1)}, u32[]{:S(2)}, u32[]{:S(2)}) collective-permute-start(f32[16,1024]{1,0:T(8,128)S(1)} %constant_dynamic-update-slice_fusion), channel_id=1, source_target_pairs={{0,4},{1,5},{2,6},{3,7},{4,0},{5,1},{6,2},{7,3},{8,12},{9,13},{10,... | collective-permute-start | bytes 196616 | tf_op jit(solution)/shard_map/ppermute | solution.py:297
  9.5 3.4 %collective-permute-start.4 = (f32[16,1024]{1,0:T(8,128)S(1)}, f32[16,1024]{1,0:T(8,128)S(1)}, u32[]{:S(2)}, u32[]{:S(2)}) collective-permute-start(f32[16,1024]{1,0:T(8,128)S(1)} %constant_dynamic-update-slice_fusion), channel_id=1, source_target_pairs={{0,2},{1,3},{2,0},{3,1},{4,6},{5,7},{6,4},{7,5},{8,10},{9,11},{10,... | collective-permute-start | bytes 196616 | tf_op jit(solution)/shard_map/ppermute | solution.py:297
  12.1 5.6 %collective-permute-start.3 = (f32[16,1024]{1,0:T(8,128)S(1)}, f32[16,1024]{1,0:T(8,128)S(1)}, u32[]{:S(2)}, u32[]{:S(2)}) collective-permute-start(f32[16,1024]{1,0:T(8,128)S(1)} %collective-permute-done.2.refs_0_), channel_id=1, source_target_pairs={{0,2},{1,3},{2,0},{3,1},{4,6},{5,7},{6,4},{7,5},{8,10},{9,11},{10,... | collective-permute-start | bytes 196616 | tf_op jit(solution)/shard_map/ppermute | solution.py:297
  19.1 3.8 %copy-start = (f32[6,1024]{1,0:T(8,128)S(1)}, f32[6,1024]{1,0:T(8,128)}, u32[]{:S(2)}) copy-start(f32[6,1024]{1,0:T(8,128)} %pv_ref.1) | copy-start | bytes 73732
  19.1 3.8 %copy-start.1 = (f32[6,1024]{1,0:T(8,128)S(1)}, f32[6,1024]{1,0:T(8,128)}, u32[]{:S(2)}) copy-start(f32[6,1024]{1,0:T(8,128)} %aj_ref.1) | copy-start | bytes 73732
  19.1 3.7 %collective-permute-start.5 = (f32[8,256]{1,0:T(8,128)S(1)}, f32[8,256]{1,0:T(8,128)S(1)}, u32[]{:S(2)}, u32[]{:S(2)}) collective-permute-start(f32[8,256]{1,0:T(8,128)S(1)} %pairs.7), channel_id=1, source_target_pairs={{0,1},{1,0},{2,3},{3,2},{4,5},{5,4},{6,7},{7,6},{8,9},{9,8},{10,11... | collective-permute-start | bytes 24584 | tf_op jit(solution)/shard_map/ppermute | solution.py:297

commit v6 on v5

--- a/solution.py
+++ b/solution.py
@@ -301,8 +301,9 @@
         return *values, (first, second)
 
     theirs = swap(targets, 1)
-    held, arrived, bit = own, own, n // 2
-    coming = swap(own, bit)
+    held, bit = own, n // 2
+    near = swap(held, 4) if bit == 8 else None
+    coming = swap(held, bit)
     *sums, theirs = pl.pallas_call(
         first_kernel,
         out_shape=(jax.ShapeDtypeStruct((24, slots), f32),) * 2 + (factor_shape,),
@@ -313,15 +314,20 @@
         name="first",
     )(own, mine, theirs)
     both = (mine, theirs)
-    while bit > 4:
+    while bit > 8:
         arrived, sums = after(sums, coming)
         held = jnp.concatenate([held, arrived], axis=0)
         bit //= 2
-        beside = swap(held, 2) if bit == 4 else None
+        near = swap(held, 4) if bit == 8 else None
         coming = swap(held, bit)
         sums = call_pairs([arrived], both, sums)
     arrived, sums = after(sums, coming)
-    coming = swap(arrived, 2)
+    beside = swap(jnp.concatenate([held, arrived], axis=0), 2)
+    coming = swap(arrived, 4)
+    near, sums = after(sums, near)
+    sums = call_pairs([arrived, near], both, sums)
+    arrived, sums = after(sums, coming)
+    coming = swap(jnp.concatenate([near, arrived], axis=0), 2)
     beside, sums = after(sums, beside)
     sums = call_pairs([arrived, beside], both, sums)
     last, sums = after(sums, coming)

time: 24 us -> 23.8 us (level)
  waiting for transfers between devices: 0.65 us -> 0.06 us
  starting transfers between devices: 8.91 us -> 9.23 us
    ppermute x6 -> x7, waiting for transfers between devices: 0.65 us -> 0.06 us  [swap(): return lax.ppermute(values, 'ja', [(i, i ^ bit) for i in range(n)])]
    ppermute x6 -> x7, starting transfers between devices: 8.91 us -> 9.23 us  [swap(): return lax.ppermute(values, 'ja', [(i, i ^ bit) for i in range(n)])]
  transfers between devices with their start and end apart: 6 -> 7, of which waited for: 2 -> 0; matrix products, arithmetic and copies ran while one was open for 0% -> 0% of each run, Pallas kernels for 38% -> 38%
where the time goes in v6:
time: 23.8 us; the launch traced here: 23.6 us
  Pallas kernels  12.9 us (54%)
  starting transfers between devices  9.23 us (39%)
  between operations  1.38 us (6%)
    ppermute x7, starting transfers between devices, swap(): return lax.ppermute(values, 'ja', [(i, i ^ bit) for i in range(n)])  9.23 us
    pallas_call x4, Pallas kernels, call_pairs(): pl.pallas_call(functools.partial(pair_kernel, len(sources), sets, folded)...  9.08 us
    pallas_call x1, Pallas kernels, per_device(): pl.pallas_call(functools.partial(prepare_kernel, slots), out_shape=(jax.S...  1.47 us
    pallas_call x1, Pallas kernels, per_device(): pl.pallas_call(first_kernel, out_shape=(jax.ShapeDtypeStruct((24, slots),...  1.41 us
    pallas_call x1, Pallas kernels, per_device(): pl.pallas_call(finish_kernel, out_shape=(jax.ShapeDtypeStruct(pos_vel.sha...  0.91 us
  transfers between devices with their start and end apart: 7, of which 0 were waited for; matrix products, arithmetic and copies ran while one was open for 0% of the time, Pallas kernels for 38%

profile of v6, /device:TPU:1, one launch (start us, length us, event | category | flops | bytes accessed | tf_op | source)
XLA Modules:
  0.0 23.6 jit_solution(1282375036736955891)
XLA Ops:
  1.3 1.5 %prepare.1 = (f32[8,1024]{1,0:T(8,128)S(1)}, f32[8,256]{1,0:T(8,128)S(1)}, f32[24,256]{1,0:T(8,128)S(1)}, bf16[128,512]{1,0:T(8,128)(2,1)S(1)}) custom-call(f32[6,1024]{1,0:T(8,128)} %pv_ref.1, f32[6,1024]{1,0:T(8,128)} %aj_ref.1, f32[1,1024]{1,0:T(1,128)} %bitcast.5, f32[1,1024]{1,0:T(1,128)} %bitcast.6, s32[1,1024]{1,0:T(1,128)} %bitcast.7, ...), custom_call_target="tpu_custom_call" | custom-call | tf_op jit(solution)/shard_map/prepare/pallas_call | solution.py:281
  2.8 3.2 %collective-permute-start.1 = (f32[8,1024]{1,0:T(8,128)S(1)}, f32[8,1024]{1,0:T(8,128)S(1)}, u32[]{:S(2)}, u32[]{:S(2)}) collective-permute-start(f32[8,1024]{1,0:T(8,128)S(1)} %get-tuple-element.29.src_ref), channel_id=1, source_target_pairs={{0,8},{1,9},{2,10},{3,11},{4,12},{5,13},{6,14},{7,15},{8,0},{9,1},... | collective-permute-start | bytes 98312 | tf_op jit(solution)/shard_map/ppermute | solution.py:297
  6.0 1.0 %collective-permute-start.2 = (f32[8,256]{1,0:T(8,128)S(1)}, f32[8,256]{1,0:T(8,128)S(1)}, u32[]{:S(2)}, u32[]{:S(2)}) collective-permute-start(f32[8,256]{1,0:T(8,128)S(1)} %get-tuple-element.31), channel_id=1, source_target_pairs={{0,1},{1,0},{2,3},{3,2},{4,5},{5,4},{6,7},{7,6},{8,9},{9,8},{10,11... | collective-permute-start | bytes 24584 | tf_op jit(solution)/shard_map/ppermute | solution.py:297
  6.9 1.3 %collective-permute-start = (f32[8,1024]{1,0:T(8,128)S(1)}, f32[8,1024]{1,0:T(8,128)S(1)}, u32[]{:S(2)}, u32[]{:S(2)}) collective-permute-start(f32[8,1024]{1,0:T(8,128)S(1)} %get-tuple-element.29.src_ref), channel_id=1, source_target_pairs={{0,4},{1,5},{2,6},{3,7},{4,0},{5,1},{6,2},{7,3},{8,12},{9,13},{10,... | collective-permute-start | bytes 98312 | tf_op jit(solution)/shard_map/ppermute | solution.py:297
  8.2 0.0 collective-permute-done.2.theirs_ref
  8.2 1.4 %first.1 = (f32[24,256]{1,0:T(8,128)S(1)}, f32[24,256]{1,0:T(8,128)S(1)}, bf16[128,512]{1,0:T(8,128)(2,1)S(1)}) custom-call(f32[8,1024]{1,0:T(8,128)S(1)} %get-tuple-element.29.src_ref, bf16[128,512]{1,0:T(8,128)(2,1)S(1)} %get-tuple-element.30.mine_ref.refs_2_.refs_1_, f32[8,256]{1,0:T(8,128)S(1)} %collective-permute-done.2.theirs_ref), custom_call_target="tpu_custom_call" | custom-call | flops 524288 | bytes 4096 | tf_op jit(solution)/shard_map/first/pallas_call | solution.py:307
  9.6 0.0 collective-permute-done.1.refs_0_
  9.7 0.9 %collective-permute-start.3 = (f32[8,1024]{1,0:T(8,128)S(1)}, f32[8,1024]{1,0:T(8,128)S(1)}, u32[]{:S(2)}, u32[]{:S(2)}) collective-permute-start(f32[8,1024]{1,0:T(8,128)S(1)} %collective-permute-done.1.refs_0_), channel_id=1, source_target_pairs={{0,4},{1,5},{2,6},{3,7},{4,0},{5,1},{6,2},{7,3},{8,12},{9,13},{10,... | collective-permute-start | bytes 98312 | tf_op jit(solution)/shard_map/ppermute | solution.py:297
  10.6 0.0 collective-permute-done.refs_1_
  10.6 1.3 %collective-permute-start.5 = (f32[16,1024]{1,0:T(8,128)S(1)}, f32[16,1024]{1,0:T(8,128)S(1)}, u32[]{:S(2)}, u32[]{:S(2)}) collective-permute-start(f32[16,1024]{1,0:T(8,128)S(1)} %pad_maximum_fusion.1), channel_id=1, source_target_pairs={{0,2},{1,3},{2,0},{3,1},{4,6},{5,7},{6,4},{7,5},{8,10},{9,11},{10,... | collective-permute-start | bytes 196616 | tf_op jit(solution)/shard_map/ppermute | solution.py:297
  11.8 2.5 %pairs.4 = (f32[24,256]{1,0:T(8,128)S(1)}, f32[24,256]{1,0:T(8,128)S(1)}) custom-call(f32[8,1024]{1,0:T(8,128)S(1)} %collective-permute-done.1.refs_0_, f32[8,1024]{1,0:T(8,128)S(1)} %collective-permute-done.refs_1_, bf16[128,512]{1,0:T(8,128)(2,1)S(1)} %get-tuple-element.30.mine_ref.refs_2_.refs_1_, bf16[128,512]{1,0:T(8,128)(2,1)S(1)} %get-tuple-element.38.refs_3_.refs_1_, ...), custom_call_target="tpu_custom_call" | custom-call | flops 1048576 | bytes 8192 | tf_op jit(solution)/shard_map/pairs/pallas_call | solution.py:264
  14.4 0.0 collective-permute-done.3.refs_0_
  14.4 0.3 %collective-permute-start.4 = (f32[16,1024]{1,0:T(8,128)S(1)}, f32[16,1024]{1,0:T(8,128)S(1)}, u32[]{:S(2)}, u32[]{:S(2)}) collective-permute-start(f32[16,1024]{1,0:T(8,128)S(1)} %pad_maximum_fusion), channel_id=1, source_target_pairs={{0,2},{1,3},{2,0},{3,1},{4,6},{5,7},{6,4},{7,5},{8,10},{9,11},{10,... | collective-permute-start | bytes 196616 | tf_op jit(solution)/shard_map/ppermute | solution.py:297
  14.7 0.0 collective-permute-done.5.refs_1_
  14.7 3.7 %pairs.5 = (f32[24,256]{1,0:T(8,128)S(1)}, f32[24,256]{1,0:T(8,128)S(1)}) custom-call(f32[8,1024]{1,0:T(8,128)S(1)} %collective-permute-done.3.refs_0_, f32[16,1024]{1,0:T(8,128)S(1)} %collective-permute-done.5.refs_1_, bf16[128,512]{1,0:T(8,128)(2,1)S(1)} %get-tuple-element.30.mine_ref.refs_2_.refs_1_, ...), custom_call_target="tpu_custom_call" | custom-call | flops 1572864 | bytes 12288 | tf_op jit(solution)/shard_map/pairs/pallas_call | solution.py:264
  18.4 0.0 collective-permute-done.4.refs_0_
  18.4 1.4 %pairs.7 = f32[8,256]{1,0:T(8,128)S(1)} custom-call(f32[16,1024]{1,0:T(8,128)S(1)} %collective-permute-done.4.refs_0_, bf16[128,512]{1,0:T(8,128)(2,1)S(1)} %get-tuple-element.38.refs_3_.refs_1_, f32[24,256]{1,0:T(8,128)S(1)} %get-tuple-element.53.refs_2_), custom_call_target="tpu_custom_call" | custom-call | flops 524288 | bytes 8192 | tf_op jit(solution)/shard_map/pairs/pallas_call | solution.py:264
  19.9 0.0 copy-start
  19.9 0.0 copy-start.1
  19.9 1.3 %collective-permute-start.6 = (f32[8,256]{1,0:T(8,128)S(1)}, f32[8,256]{1,0:T(8,128)S(1)}, u32[]{:S(2)}, u32[]{:S(2)}) collective-permute-start(f32[8,256]{1,0:T(8,128)S(1)} %pairs.7), channel_id=1, source_target_pairs={{0,1},{1,0},{2,3},{3,2},{4,5},{5,4},{6,7},{7,6},{8,9},{9,8},{10,11... | collective-permute-start | bytes 24584 | tf_op jit(solution)/shard_map/ppermute | solution.py:297
  21.2 1.4 %pairs.6.mine_ref = f32[8,256]{1,0:T(8,128)S(1)} custom-call(f32[16,1024]{1,0:T(8,128)S(1)} %collective-permute-done.4.refs_0_, bf16[128,512]{1,0:T(8,128)(2,1)S(1)} %get-tuple-element.30.mine_ref.refs_2_.refs_1_, f32[24,256]{1,0:T(8,128)S(1)} %get-tuple-element.52.refs_2_), custom_call_target="tpu_custom_call" | custom-call | flops 524288 | bytes 8192 | tf_op jit(solution)/shard_map/pairs/pallas_call | solution.py:264
  22.6 0.0 collective-permute-done.6.other_ref
  22.6 0.0 copy-done
  22.7 0.9 %finish.1 = (f32[6,1024]{1,0:T(8,128)}, f32[6,1024]{1,0:T(8,128)}, f32[12,256]{1,0:T(8,128)}) custom-call(f32[8,256]{1,0:T(8,128)S(1)} %pairs.6.mine_ref, f32[8,256]{1,0:T(8,128)S(1)} %collective-permute-done.6.other_ref, f32[24,256]{1,0:T(8,128)S(1)} %get-tuple-element.54.old_ref, f32[6,1024]{1,0:T(8,128)S(1)} %copy-done, f32[6,1024]{1,0:T(8,128)S(1)} %copy-done.1), custom_call_target="tpu_custom_call" | custom-call | tf_op jit(solution)/shard_map/finish/pallas_call | solution.py:337
  (3 shorter events, 0.0 us)
Async XLA Ops:
  2.8 6.9 %collective-permute-start.1 = (f32[8,1024]{1,0:T(8,128)S(1)}, f32[8,1024]{1,0:T(8,128)S(1)}, u32[]{:S(2)}, u32[]{:S(2)}) collective-permute-start(f32[8,1024]{1,0:T(8,128)S(1)} %get-tuple-element.29.src_ref), channel_id=1, source_target_pairs={{0,8},{1,9},{2,10},{3,11},{4,12},{5,13},{6,14},{7,15},{8,0},{9,1},... | collective-permute-start | bytes 98312 | tf_op jit(solution)/shard_map/ppermute | solution.py:297
  6.0 2.3 %collective-permute-start.2 = (f32[8,256]{1,0:T(8,128)S(1)}, f32[8,256]{1,0:T(8,128)S(1)}, u32[]{:S(2)}, u32[]{:S(2)}) collective-permute-start(f32[8,256]{1,0:T(8,128)S(1)} %get-tuple-element.31), channel_id=1, source_target_pairs={{0,1},{1,0},{2,3},{3,2},{4,5},{5,4},{6,7},{7,6},{8,9},{9,8},{10,11... | collective-permute-start | bytes 24584 | tf_op jit(solution)/shard_map/ppermute | solution.py:297
  6.9 3.6 %collective-permute-start = (f32[8,1024]{1,0:T(8,128)S(1)}, f32[8,1024]{1,0:T(8,128)S(1)}, u32[]{:S(2)}, u32[]{:S(2)}) collective-permute-start(f32[8,1024]{1,0:T(8,128)S(1)} %get-tuple-element.29.src_ref), channel_id=1, source_target_pairs={{0,4},{1,5},{2,6},{3,7},{4,0},{5,1},{6,2},{7,3},{8,12},{9,13},{10,... | collective-permute-start | bytes 98312 | tf_op jit(solution)/shard_map/ppermute | solution.py:297
  9.7 4.7 %collective-permute-start.3 = (f32[8,1024]{1,0:T(8,128)S(1)}, f32[8,1024]{1,0:T(8,128)S(1)}, u32[]{:S(2)}, u32[]{:S(2)}) collective-permute-start(f32[8,1024]{1,0:T(8,128)S(1)} %collective-permute-done.1.refs_0_), channel_id=1, source_target_pairs={{0,4},{1,5},{2,6},{3,7},{4,0},{5,1},{6,2},{7,3},{8,12},{9,13},{10,... | collective-permute-start | bytes 98312 | tf_op jit(solution)/shard_map/ppermute | solution.py:297
  10.6 4.2 %collective-permute-start.5 = (f32[16,1024]{1,0:T(8,128)S(1)}, f32[16,1024]{1,0:T(8,128)S(1)}, u32[]{:S(2)}, u32[]{:S(2)}) collective-permute-start(f32[16,1024]{1,0:T(8,128)S(1)} %pad_maximum_fusion.1), channel_id=1, source_target_pairs={{0,2},{1,3},{2,0},{3,1},{4,6},{5,7},{6,4},{7,5},{8,10},{9,11},{10,... | collective-permute-start | bytes 196616 | tf_op jit(solution)/shard_map/ppermute | solution.py:297
  14.4 4.0 %collective-permute-start.4 = (f32[16,1024]{1,0:T(8,128)S(1)}, f32[16,1024]{1,0:T(8,128)S(1)}, u32[]{:S(2)}, u32[]{:S(2)}) collective-permute-start(f32[16,1024]{1,0:T(8,128)S(1)} %pad_maximum_fusion), channel_id=1, source_target_pairs={{0,2},{1,3},{2,0},{3,1},{4,6},{5,7},{6,4},{7,5},{8,10},{9,11},{10,... | collective-permute-start | bytes 196616 | tf_op jit(solution)/shard_map/ppermute | solution.py:297
  19.9 2.8 %copy-start = (f32[6,1024]{1,0:T(8,128)S(1)}, f32[6,1024]{1,0:T(8,128)}, u32[]{:S(2)}) copy-start(f32[6,1024]{1,0:T(8,128)} %pv_ref.1) | copy-start | bytes 73732
  19.9 2.8 %copy-start.1 = (f32[6,1024]{1,0:T(8,128)S(1)}, f32[6,1024]{1,0:T(8,128)}, u32[]{:S(2)}) copy-start(f32[6,1024]{1,0:T(8,128)} %aj_ref.1) | copy-start | bytes 73732
  19.9 2.7 %collective-permute-start.6 = (f32[8,256]{1,0:T(8,128)S(1)}, f32[8,256]{1,0:T(8,128)S(1)}, u32[]{:S(2)}, u32[]{:S(2)}) collective-permute-start(f32[8,256]{1,0:T(8,128)S(1)} %pairs.7), channel_id=1, source_target_pairs={{0,1},{1,0},{2,3},{3,2},{4,5},{5,4},{6,7},{7,6},{8,9},{9,8},{10,11... | collective-permute-start | bytes 24584 | tf_op jit(solution)/shard_map/ppermute | solution.py:297

commit v7 on v6

--- a/solution.py
+++ b/solution.py
@@ -254,7 +254,7 @@
 
 def cost(sources, slots):
     pairs = sum(s.size // 8 for s in sources) * slots
-    return pl.CostEstimate(flops=pairs, bytes_accessed=4 * pairs // slots, transcendentals=pairs)
+    return pl.CostEstimate(flops=3072 * pairs, bytes_accessed=4 * pairs // slots, transcendentals=pairs)
 
 
 def call_pairs(sources, factors, sums, folded=False):
@@ -302,7 +302,7 @@
 
     theirs = swap(targets, 1)
     held, bit = own, n // 2
-    near = swap(held, 4) if bit == 8 else None
+    near = swap(held, 2) if bit == 8 else None
     coming = swap(held, bit)
     *sums, theirs = pl.pallas_call(
         first_kernel,
@@ -318,16 +318,16 @@
         arrived, sums = after(sums, coming)
         held = jnp.concatenate([held, arrived], axis=0)
         bit //= 2
-        near = swap(held, 4) if bit == 8 else None
+        near = swap(held, 2) if bit == 8 else None
         coming = swap(held, bit)
         sums = call_pairs([arrived], both, sums)
     arrived, sums = after(sums, coming)
-    beside = swap(jnp.concatenate([held, arrived], axis=0), 2)
-    coming = swap(arrived, 4)
+    beside = swap(jnp.concatenate([held, arrived], axis=0), 4)
+    coming = swap(arrived, 2)
     near, sums = after(sums, near)
     sums = call_pairs([arrived, near], both, sums)
     arrived, sums = after(sums, coming)
-    coming = swap(jnp.concatenate([near, arrived], axis=0), 2)
+    coming = swap(jnp.concatenate([near, arrived], axis=0), 4)
     beside, sums = after(sums, beside)
     sums = call_pairs([arrived, beside], both, sums)
     last, sums = after(sums, coming)

time: 23.8 us -> 23.5 us (0.987)
  starting transfers between devices: 9.23 us -> 8.98 us
    ppermute x7, starting transfers between devices: 9.23 us -> 8.98 us  [swap(): return lax.ppermute(values, 'ja', [(i, i ^ bit) for i in range(n)])]
  transfers between devices with their start and end apart: 7 -> 7, of which waited for: 0 -> 0; matrix products, arithmetic and copies ran while one was open for 0% -> 0% of each run, Pallas kernels for 38% -> 39%
where the time goes in v7:
time: 23.5 us; the launch traced here: 23.3 us
  Pallas kernels  12.9 us (55%)
  starting transfers between devices  8.98 us (38%)
  between operations  1.38 us (6%)
    pallas_call x4, Pallas kernels, call_pairs(): pl.pallas_call(functools.partial(pair_kernel, len(sources), sets, folded)...  9.08 us
    ppermute x7, starting transfers between devices, swap(): return lax.ppermute(values, 'ja', [(i, i ^ bit) for i in range(n)])  8.98 us
    pallas_call x1, Pallas kernels, per_device(): pl.pallas_call(functools.partial(prepare_kernel, slots), out_shape=(jax.S...  1.47 us
    pallas_call x1, Pallas kernels, per_device(): pl.pallas_call(first_kernel, out_shape=(jax.ShapeDtypeStruct((24, slots),...  1.4 us
    pallas_call x1, Pallas kernels, per_device(): pl.pallas_call(finish_kernel, out_shape=(jax.ShapeDtypeStruct(pos_vel.sha...  0.92 us
  transfers between devices with their start and end apart: 7, of which 0 were waited for; matrix products, arithmetic and copies ran while one was open for 0% of the time, Pallas kernels for 39%

profile of v7, /device:TPU:1, one launch (start us, length us, event | category | flops | bytes accessed | tf_op | source)
XLA Modules:
  0.0 23.3 jit_solution(2632699290291316607)
XLA Ops:
  1.3 1.5 %prepare.1 = (f32[8,1024]{1,0:T(8,128)S(1)}, f32[8,256]{1,0:T(8,128)S(1)}, f32[24,256]{1,0:T(8,128)S(1)}, bf16[128,512]{1,0:T(8,128)(2,1)S(1)}) custom-call(f32[6,1024]{1,0:T(8,128)} %pv_ref.1, f32[6,1024]{1,0:T(8,128)} %aj_ref.1, f32[1,1024]{1,0:T(1,128)} %bitcast.5, f32[1,1024]{1,0:T(1,128)} %bitcast.6, s32[1,1024]{1,0:T(1,128)} %bitcast.7, ...), custom_call_target="tpu_custom_call" | custom-call | tf_op jit(solution)/shard_map/prepare/pallas_call | solution.py:281
  2.8 0.1 collective-permute-start.2
  2.9 3.8 %collective-permute-start.1 = (f32[8,1024]{1,0:T(8,128)S(1)}, f32[8,1024]{1,0:T(8,128)S(1)}, u32[]{:S(2)}, u32[]{:S(2)}) collective-permute-start(f32[8,1024]{1,0:T(8,128)S(1)} %get-tuple-element.29.src_ref), channel_id=1, source_target_pairs={{0,8},{1,9},{2,10},{3,11},{4,12},{5,13},{6,14},{7,15},{8,0},{9,1},... | collective-permute-start | bytes 98312 | tf_op jit(solution)/shard_map/ppermute | solution.py:297
  6.7 1.2 %collective-permute-start = (f32[8,1024]{1,0:T(8,128)S(1)}, f32[8,1024]{1,0:T(8,128)S(1)}, u32[]{:S(2)}, u32[]{:S(2)}) collective-permute-start(f32[8,1024]{1,0:T(8,128)S(1)} %get-tuple-element.29.src_ref), channel_id=1, source_target_pairs={{0,2},{1,3},{2,0},{3,1},{4,6},{5,7},{6,4},{7,5},{8,10},{9,11},{10,... | collective-permute-start | bytes 98312 | tf_op jit(solution)/shard_map/ppermute | solution.py:297
  7.9 0.0 collective-permute-done.2.theirs_ref
  7.9 1.4 %first.1 = (f32[24,256]{1,0:T(8,128)S(1)}, f32[24,256]{1,0:T(8,128)S(1)}, bf16[128,512]{1,0:T(8,128)(2,1)S(1)}) custom-call(f32[8,1024]{1,0:T(8,128)S(1)} %get-tuple-element.29.src_ref, bf16[128,512]{1,0:T(8,128)(2,1)S(1)} %get-tuple-element.30.mine_ref.refs_2_.refs_1_, f32[8,256]{1,0:T(8,128)S(1)} %collective-permute-done.2.theirs_ref), custom_call_target="tpu_custom_call" | custom-call | flops 1610612736 | bytes 4096 | tf_op jit(solution)/shard_map/first/pallas_call | solution.py:307
  9.3 0.0 collective-permute-done.1.refs_0_
  9.3 0.3 %collective-permute-start.3 = (f32[8,1024]{1,0:T(8,128)S(1)}, f32[8,1024]{1,0:T(8,128)S(1)}, u32[]{:S(2)}, u32[]{:S(2)}) collective-permute-start(f32[8,1024]{1,0:T(8,128)S(1)} %collective-permute-done.1.refs_0_), channel_id=1, source_target_pairs={{0,2},{1,3},{2,0},{3,1},{4,6},{5,7},{6,4},{7,5},{8,10},{9,11},{10,... | collective-permute-start | bytes 98312 | tf_op jit(solution)/shard_map/ppermute | solution.py:297
  9.6 0.0 collective-permute-done.refs_1_
  9.6 1.4 %collective-permute-start.5 = (f32[16,1024]{1,0:T(8,128)S(1)}, f32[16,1024]{1,0:T(8,128)S(1)}, u32[]{:S(2)}, u32[]{:S(2)}) collective-permute-start(f32[16,1024]{1,0:T(8,128)S(1)} %pad_maximum_fusion.1), channel_id=1, source_target_pairs={{0,4},{1,5},{2,6},{3,7},{4,0},{5,1},{6,2},{7,3},{8,12},{9,13},{10,... | collective-permute-start | bytes 196616 | tf_op jit(solution)/shard_map/ppermute | solution.py:297
  11.0 2.5 %pairs.4 = (f32[24,256]{1,0:T(8,128)S(1)}, f32[24,256]{1,0:T(8,128)S(1)}) custom-call(f32[8,1024]{1,0:T(8,128)S(1)} %collective-permute-done.1.refs_0_, f32[8,1024]{1,0:T(8,128)S(1)} %collective-permute-done.refs_1_, bf16[128,512]{1,0:T(8,128)(2,1)S(1)} %get-tuple-element.30.mine_ref.refs_2_.refs_1_, bf16[128,512]{1,0:T(8,128)(2,1)S(1)} %get-tuple-element.38.refs_3_.refs_1_, ...), custom_call_target="tpu_custom_call" | custom-call | flops 3221225472 | bytes 8192 | tf_op jit(solution)/shard_map/pairs/pallas_call | solution.py:264
  13.5 0.0 collective-permute-done.3.refs_0_
  13.6 0.2 %collective-permute-start.4 = (f32[16,1024]{1,0:T(8,128)S(1)}, f32[16,1024]{1,0:T(8,128)S(1)}, u32[]{:S(2)}, u32[]{:S(2)}) collective-permute-start(f32[16,1024]{1,0:T(8,128)S(1)} %pad_maximum_fusion), channel_id=1, source_target_pairs={{0,4},{1,5},{2,6},{3,7},{4,0},{5,1},{6,2},{7,3},{8,12},{9,13},{10,... | collective-permute-start | bytes 196616 | tf_op jit(solution)/shard_map/ppermute | solution.py:297
  13.8 0.0 collective-permute-done.5.refs_1_
  13.8 3.7 %pairs.5 = (f32[24,256]{1,0:T(8,128)S(1)}, f32[24,256]{1,0:T(8,128)S(1)}) custom-call(f32[8,1024]{1,0:T(8,128)S(1)} %collective-permute-done.3.refs_0_, f32[16,1024]{1,0:T(8,128)S(1)} %collective-permute-done.5.refs_1_, bf16[128,512]{1,0:T(8,128)(2,1)S(1)} %get-tuple-element.30.mine_ref.refs_2_.refs_1_, ...), custom_call_target="tpu_custom_call" | custom-call | flops 4831838208 | bytes 12288 | tf_op jit(solution)/shard_map/pairs/pallas_call | solution.py:264
  17.5 0.0 collective-permute-done.4.refs_0_
  17.5 1.4 %pairs.7 = f32[8,256]{1,0:T(8,128)S(1)} custom-call(f32[16,1024]{1,0:T(8,128)S(1)} %collective-permute-done.4.refs_0_, bf16[128,512]{1,0:T(8,128)(2,1)S(1)} %get-tuple-element.38.refs_3_.refs_1_, f32[24,256]{1,0:T(8,128)S(1)} %get-tuple-element.53.refs_2_), custom_call_target="tpu_custom_call" | custom-call | flops 1610612736 | bytes 8192 | tf_op jit(solution)/shard_map/pairs/pallas_call | solution.py:264
  19.0 0.0 copy-start
  19.0 0.0 copy-start.1
  19.0 2.0 %collective-permute-start.6 = (f32[8,256]{1,0:T(8,128)S(1)}, f32[8,256]{1,0:T(8,128)S(1)}, u32[]{:S(2)}, u32[]{:S(2)}) collective-permute-start(f32[8,256]{1,0:T(8,128)S(1)} %pairs.7), channel_id=1, source_target_pairs={{0,1},{1,0},{2,3},{3,2},{4,5},{5,4},{6,7},{7,6},{8,9},{9,8},{10,11... | collective-permute-start | bytes 24584 | tf_op jit(solution)/shard_map/ppermute | solution.py:297
  20.9 1.4 %pairs.6.mine_ref = f32[8,256]{1,0:T(8,128)S(1)} custom-call(f32[16,1024]{1,0:T(8,128)S(1)} %collective-permute-done.4.refs_0_, bf16[128,512]{1,0:T(8,128)(2,1)S(1)} %get-tuple-element.30.mine_ref.refs_2_.refs_1_, f32[24,256]{1,0:T(8,128)S(1)} %get-tuple-element.52.refs_2_), custom_call_target="tpu_custom_call" | custom-call | flops 1610612736 | bytes 8192 | tf_op jit(solution)/shard_map/pairs/pallas_call | solution.py:264
  22.4 0.0 collective-permute-done.6.other_ref
  22.4 0.0 copy-done
  22.4 0.9 %finish.1 = (f32[6,1024]{1,0:T(8,128)}, f32[6,1024]{1,0:T(8,128)}, f32[12,256]{1,0:T(8,128)}) custom-call(f32[8,256]{1,0:T(8,128)S(1)} %pairs.6.mine_ref, f32[8,256]{1,0:T(8,128)S(1)} %collective-permute-done.6.other_ref, f32[24,256]{1,0:T(8,128)S(1)} %get-tuple-element.54.old_ref, f32[6,1024]{1,0:T(8,128)S(1)} %copy-done, f32[6,1024]{1,0:T(8,128)S(1)} %copy-done.1), custom_call_target="tpu_custom_call" | custom-call | tf_op jit(solution)/shard_map/finish/pallas_call | solution.py:337
  (3 shorter events, 0.0 us)
Async XLA Ops:
  2.8 5.1 %collective-permute-start.2 = (f32[8,256]{1,0:T(8,128)S(1)}, f32[8,256]{1,0:T(8,128)S(1)}, u32[]{:S(2)}, u32[]{:S(2)}) collective-permute-start(f32[8,256]{1,0:T(8,128)S(1)} %get-tuple-element.31), channel_id=1, source_target_pairs={{0,1},{1,0},{2,3},{3,2},{4,5},{5,4},{6,7},{7,6},{8,9},{9,8},{10,11... | collective-permute-start | bytes 24584 | tf_op jit(solution)/shard_map/ppermute | solution.py:297
  2.9 6.4 %collective-permute-start.1 = (f32[8,1024]{1,0:T(8,128)S(1)}, f32[8,1024]{1,0:T(8,128)S(1)}, u32[]{:S(2)}, u32[]{:S(2)}) collective-permute-start(f32[8,1024]{1,0:T(8,128)S(1)} %get-tuple-element.29.src_ref), channel_id=1, source_target_pairs={{0,8},{1,9},{2,10},{3,11},{4,12},{5,13},{6,14},{7,15},{8,0},{9,1},... | collective-permute-start | bytes 98312 | tf_op jit(solution)/shard_map/ppermute | solution.py:297
  6.7 3.0 %collective-permute-start = (f32[8,1024]{1,0:T(8,128)S(1)}, f32[8,1024]{1,0:T(8,128)S(1)}, u32[]{:S(2)}, u32[]{:S(2)}) collective-permute-start(f32[8,1024]{1,0:T(8,128)S(1)} %get-tuple-element.29.src_ref), channel_id=1, source_target_pairs={{0,2},{1,3},{2,0},{3,1},{4,6},{5,7},{6,4},{7,5},{8,10},{9,11},{10,... | collective-permute-start | bytes 98312 | tf_op jit(solution)/shard_map/ppermute | solution.py:297
  9.3 4.2 %collective-permute-start.3 = (f32[8,1024]{1,0:T(8,128)S(1)}, f32[8,1024]{1,0:T(8,128)S(1)}, u32[]{:S(2)}, u32[]{:S(2)}) collective-permute-start(f32[8,1024]{1,0:T(8,128)S(1)} %collective-permute-done.1.refs_0_), channel_id=1, source_target_pairs={{0,2},{1,3},{2,0},{3,1},{4,6},{5,7},{6,4},{7,5},{8,10},{9,11},{10,... | collective-permute-start | bytes 98312 | tf_op jit(solution)/shard_map/ppermute | solution.py:297
  9.6 4.2 %collective-permute-start.5 = (f32[16,1024]{1,0:T(8,128)S(1)}, f32[16,1024]{1,0:T(8,128)S(1)}, u32[]{:S(2)}, u32[]{:S(2)}) collective-permute-start(f32[16,1024]{1,0:T(8,128)S(1)} %pad_maximum_fusion.1), channel_id=1, source_target_pairs={{0,4},{1,5},{2,6},{3,7},{4,0},{5,1},{6,2},{7,3},{8,12},{9,13},{10,... | collective-permute-start | bytes 196616 | tf_op jit(solution)/shard_map/ppermute | solution.py:297
  13.6 3.9 %collective-permute-start.4 = (f32[16,1024]{1,0:T(8,128)S(1)}, f32[16,1024]{1,0:T(8,128)S(1)}, u32[]{:S(2)}, u32[]{:S(2)}) collective-permute-start(f32[16,1024]{1,0:T(8,128)S(1)} %pad_maximum_fusion), channel_id=1, source_target_pairs={{0,4},{1,5},{2,6},{3,7},{4,0},{5,1},{6,2},{7,3},{8,12},{9,13},{10,... | collective-permute-start | bytes 196616 | tf_op jit(solution)/shard_map/ppermute | solution.py:297
  19.0 3.4 %copy-start = (f32[6,1024]{1,0:T(8,128)S(1)}, f32[6,1024]{1,0:T(8,128)}, u32[]{:S(2)}) copy-start(f32[6,1024]{1,0:T(8,128)} %pv_ref.1) | copy-start | bytes 73732
  19.0 3.4 %copy-start.1 = (f32[6,1024]{1,0:T(8,128)S(1)}, f32[6,1024]{1,0:T(8,128)}, u32[]{:S(2)}) copy-start(f32[6,1024]{1,0:T(8,128)} %aj_ref.1) | copy-start | bytes 73732
  19.0 3.4 %collective-permute-start.6 = (f32[8,256]{1,0:T(8,128)S(1)}, f32[8,256]{1,0:T(8,128)S(1)}, u32[]{:S(2)}, u32[]{:S(2)}) collective-permute-start(f32[8,256]{1,0:T(8,128)S(1)} %pairs.7), channel_id=1, source_target_pairs={{0,1},{1,0},{2,3},{3,2},{4,5},{5,4},{6,7},{7,6},{8,9},{9,8},{10,11... | collective-permute-start | bytes 24584 | tf_op jit(solution)/shard_map/ppermute | solution.py:297

commit v8 on v7

--- a/solution.py
+++ b/solution.py
@@ -172,7 +172,7 @@
 
 
 def prepare_kernel(slots, *refs):
-    inputs, (src_ref, tgt_ref, old_ref, fac_ref), here, sems = refs[:7], refs[7:11], refs[11:18], refs[18]
+    inputs, (src_ref, tgt_ref, old_ref, fac_ref, turned_ref), here, sems = refs[:7], refs[7:12], refs[12:19], refs[19]
     copies = [pltpu.make_async_copy(src, dst, sems.at[i]) for i, (src, dst) in enumerate(zip(inputs, here))]
     for copy in copies:
         copy.start()
@@ -202,6 +202,7 @@
     tgt_ref[...] = old[0:8]
     old_ref[...] = jnp.concatenate([old[0:22], live, order.astype(f32)], axis=0)
     fac_ref[...] = target_factors(old[0:8])
+    turned_ref[...] = hot.T
 
 
 def first_kernel(src_ref, mine_ref, theirs_ref, out_mine, out_theirs, fac_ref):
@@ -225,8 +226,7 @@
             out[...] = sums[0:8] + sums[8:16] + sums[16:24]
 
 
-def finish_kernel(mine_ref, other_ref, old_ref, pv_ref, aj_ref, new_pv_ref, new_aj_ref, state_ref):
-    stars = pv_ref.shape[1]
+def finish_kernel(mine_ref, other_ref, turned_ref, old_ref, pv_ref, aj_ref, new_pv_ref, new_aj_ref, state_ref):
     sums = mine_ref[...] + other_ref[...]
     old = old_ref[...]
     here, there, step_len = old[0:3], old[3:6], old[7:8]
@@ -240,9 +240,8 @@
     live = old[22:23]
     state = jnp.where(live > 0.5, jnp.concatenate([x1, v1, a1, j1], axis=0), 0.0)
     state_ref[...] = state
-    hot = one_hot(old[23:24].astype(jnp.int32), stars)
     rows = jnp.concatenate([state, jnp.broadcast_to(live, (4, live.shape[1]))], axis=0)
-    moved = exact_product(rows, hot, 1)
+    moved = exact_product(rows, turned_ref[...], 0)
     active = moved[12:13] > 0.5
     new_pv_ref[...] = jnp.where(active, moved[0:6], pv_ref[...])
     new_aj_ref[...] = jnp.where(active, moved[6:12], aj_ref[...])
@@ -278,16 +277,17 @@
     inputs = [pos_vel, acc_jerk] + [values.reshape(1, -1) for values in (star_mass, step_phase, step_level, counts)]
     inputs.append(star_order)
     factor_shape = jax.ShapeDtypeStruct((FACTOR_ROWS, 2 * slots), bf16)
-    own, targets, old, mine = pl.pallas_call(
+    own, targets, old, mine, turned = pl.pallas_call(
         functools.partial(prepare_kernel, slots),
         out_shape=(
             jax.ShapeDtypeStruct((8, stars), f32),
             jax.ShapeDtypeStruct((8, slots), f32),
             jax.ShapeDtypeStruct((24, slots), f32),
             factor_shape,
+            jax.ShapeDtypeStruct((slots, stars), bf16),
         ),
         in_specs=[HBM] * 7,
-        out_specs=(VMEM,) * 4,
+        out_specs=(VMEM,) * 5,
         scratch_shapes=[pltpu.VMEM(values.shape, values.dtype) for values in inputs] + [pltpu.SemaphoreType.DMA((7,))],
         compiler_params=PARAMS,
         name="prepare",
@@ -341,11 +341,11 @@
             jax.ShapeDtypeStruct(acc_jerk.shape, f32),
             jax.ShapeDtypeStruct((12, slots), f32),
         ),
-        in_specs=[VMEM] * 5,
+        in_specs=[VMEM] * 6,
         out_specs=(VMEM,) * 3,
         compiler_params=PARAMS,
         name="finish",
-    )(here, from_them, old, pos_vel, acc_jerk)
+    )(here, from_them, turned, old, pos_vel, acc_jerk)
 
 
 A_DEV = 128

time: 23.5 us -> 23.5 us (level)
  no operation moved by 1% of the time
where the time goes in v8:
time: 23.5 us; the launch traced here: 23.3 us
  Pallas kernels  12.9 us (55%)
  starting transfers between devices  8.97 us (38%)
  between operations  1.38 us (6%)
    pallas_call x4, Pallas kernels, call_pairs(): pl.pallas_call(functools.partial(pair_kernel, len(sources), sets, folded)...  9.08 us
    ppermute x7, starting transfers between devices, swap(): return lax.ppermute(values, 'ja', [(i, i ^ bit) for i in range(n)])  8.97 us
    pallas_call x1, Pallas kernels, per_device(): pl.pallas_call(functools.partial(prepare_kernel, slots), out_shape=(jax.S...  1.56 us
    pallas_call x1, Pallas kernels, per_device(): pl.pallas_call(first_kernel, out_shape=(jax.ShapeDtypeStruct((24, slots),...  1.41 us
    pallas_call x1, Pallas kernels, per_device(): pl.pallas_call(finish_kernel, out_shape=(jax.ShapeDtypeStruct(pos_vel.sha...  0.84 us
  transfers between devices with their start and end apart: 7, of which 0 were waited for; matrix products, arithmetic and copies ran while one was open for 0% of the time, Pallas kernels for 39%

profile of v8, /device:TPU:1, one launch (start us, length us, event | category | flops | bytes accessed | tf_op | source)
XLA Modules:
  0.0 23.3 jit_solution(2113253594166087835)
XLA Ops:
  1.3 1.6 %prepare.1 = (f32[8,1024]{1,0:T(8,128)S(1)}, f32[8,256]{1,0:T(8,128)S(1)}, f32[24,256]{1,0:T(8,128)S(1)}, bf16[128,512]{1,0:T(8,128)(2,1)S(1)}, bf16[256,1024]{1,0:T(8,128)(2,1)S(1)}) custom-call(f32[6,1024]{1,0:T(8,128)} %pv_ref.1, f32[6,1024]{1,0:T(8,128)} %aj_ref.1, f32[1,1024]{1,0:T(1,128)} %bitcast.5, f32[1,1024]{1,0:T(1,128)} %bitcast.6, ...), custom_call_target="tpu_custom_call" | custom-call | tf_op jit(solution)/shard_map/prepare/pallas_call | solution.py:280
  2.8 0.1 collective-permute-start.2
  3.0 3.8 %collective-permute-start.1 = (f32[8,1024]{1,0:T(8,128)S(1)}, f32[8,1024]{1,0:T(8,128)S(1)}, u32[]{:S(2)}, u32[]{:S(2)}) collective-permute-start(f32[8,1024]{1,0:T(8,128)S(1)} %get-tuple-element.30.src_ref), channel_id=1, source_target_pairs={{0,8},{1,9},{2,10},{3,11},{4,12},{5,13},{6,14},{7,15},{8,0},{9,1},... | collective-permute-start | bytes 98312 | tf_op jit(solution)/shard_map/ppermute | solution.py:297
  6.7 1.2 %collective-permute-start = (f32[8,1024]{1,0:T(8,128)S(1)}, f32[8,1024]{1,0:T(8,128)S(1)}, u32[]{:S(2)}, u32[]{:S(2)}) collective-permute-start(f32[8,1024]{1,0:T(8,128)S(1)} %get-tuple-element.30.src_ref), channel_id=1, source_target_pairs={{0,2},{1,3},{2,0},{3,1},{4,6},{5,7},{6,4},{7,5},{8,10},{9,11},{10,... | collective-permute-start | bytes 98312 | tf_op jit(solution)/shard_map/ppermute | solution.py:297
  7.9 0.0 collective-permute-done.2.theirs_ref
  8.0 1.4 %first.1 = (f32[24,256]{1,0:T(8,128)S(1)}, f32[24,256]{1,0:T(8,128)S(1)}, bf16[128,512]{1,0:T(8,128)(2,1)S(1)}) custom-call(f32[8,1024]{1,0:T(8,128)S(1)} %get-tuple-element.30.src_ref, bf16[128,512]{1,0:T(8,128)(2,1)S(1)} %get-tuple-element.31.mine_ref.refs_2_.refs_1_, f32[8,256]{1,0:T(8,128)S(1)} %collective-permute-done.2.theirs_ref), custom_call_target="tpu_custom_call" | custom-call | flops 1610612736 | bytes 4096 | tf_op jit(solution)/shard_map/first/pallas_call | solution.py:307
  9.4 0.0 collective-permute-done.1.refs_0_
  9.4 0.3 %collective-permute-start.3 = (f32[8,1024]{1,0:T(8,128)S(1)}, f32[8,1024]{1,0:T(8,128)S(1)}, u32[]{:S(2)}, u32[]{:S(2)}) collective-permute-start(f32[8,1024]{1,0:T(8,128)S(1)} %collective-permute-done.1.refs_0_), channel_id=1, source_target_pairs={{0,2},{1,3},{2,0},{3,1},{4,6},{5,7},{6,4},{7,5},{8,10},{9,11},{10,... | collective-permute-start | bytes 98312 | tf_op jit(solution)/shard_map/ppermute | solution.py:297
  9.7 0.0 collective-permute-done.refs_1_
  9.7 1.4 %collective-permute-start.5 = (f32[16,1024]{1,0:T(8,128)S(1)}, f32[16,1024]{1,0:T(8,128)S(1)}, u32[]{:S(2)}, u32[]{:S(2)}) collective-permute-start(f32[16,1024]{1,0:T(8,128)S(1)} %pad_maximum_fusion.1), channel_id=1, source_target_pairs={{0,4},{1,5},{2,6},{3,7},{4,0},{5,1},{6,2},{7,3},{8,12},{9,13},{10,... | collective-permute-start | bytes 196616 | tf_op jit(solution)/shard_map/ppermute | solution.py:297
  11.1 2.5 %pairs.4 = (f32[24,256]{1,0:T(8,128)S(1)}, f32[24,256]{1,0:T(8,128)S(1)}) custom-call(f32[8,1024]{1,0:T(8,128)S(1)} %collective-permute-done.1.refs_0_, f32[8,1024]{1,0:T(8,128)S(1)} %collective-permute-done.refs_1_, bf16[128,512]{1,0:T(8,128)(2,1)S(1)} %get-tuple-element.31.mine_ref.refs_2_.refs_1_, bf16[128,512]{1,0:T(8,128)(2,1)S(1)} %get-tuple-element.39.refs_3_.refs_1_, ...), custom_call_target="tpu_custom_call" | custom-call | flops 3221225472 | bytes 8192 | tf_op jit(solution)/shard_map/pairs/pallas_call | solution.py:263
  13.6 0.0 collective-permute-done.3.refs_0_
  13.7 0.2 %collective-permute-start.4 = (f32[16,1024]{1,0:T(8,128)S(1)}, f32[16,1024]{1,0:T(8,128)S(1)}, u32[]{:S(2)}, u32[]{:S(2)}) collective-permute-start(f32[16,1024]{1,0:T(8,128)S(1)} %pad_maximum_fusion), channel_id=1, source_target_pairs={{0,4},{1,5},{2,6},{3,7},{4,0},{5,1},{6,2},{7,3},{8,12},{9,13},{10,... | collective-permute-start | bytes 196616 | tf_op jit(solution)/shard_map/ppermute | solution.py:297
  13.9 0.0 collective-permute-done.5.refs_1_
  13.9 3.7 %pairs.5 = (f32[24,256]{1,0:T(8,128)S(1)}, f32[24,256]{1,0:T(8,128)S(1)}) custom-call(f32[8,1024]{1,0:T(8,128)S(1)} %collective-permute-done.3.refs_0_, f32[16,1024]{1,0:T(8,128)S(1)} %collective-permute-done.5.refs_1_, bf16[128,512]{1,0:T(8,128)(2,1)S(1)} %get-tuple-element.31.mine_ref.refs_2_.refs_1_, ...), custom_call_target="tpu_custom_call" | custom-call | flops 4831838208 | bytes 12288 | tf_op jit(solution)/shard_map/pairs/pallas_call | solution.py:263
  17.6 0.0 collective-permute-done.4.refs_0_
  17.6 1.4 %pairs.7 = f32[8,256]{1,0:T(8,128)S(1)} custom-call(f32[16,1024]{1,0:T(8,128)S(1)} %collective-permute-done.4.refs_0_, bf16[128,512]{1,0:T(8,128)(2,1)S(1)} %get-tuple-element.39.refs_3_.refs_1_, f32[24,256]{1,0:T(8,128)S(1)} %get-tuple-element.54.refs_2_), custom_call_target="tpu_custom_call" | custom-call | flops 1610612736 | bytes 8192 | tf_op jit(solution)/shard_map/pairs/pallas_call | solution.py:263
  19.0 0.0 copy-start
  19.0 0.0 copy-start.1
  19.1 2.0 %collective-permute-start.6 = (f32[8,256]{1,0:T(8,128)S(1)}, f32[8,256]{1,0:T(8,128)S(1)}, u32[]{:S(2)}, u32[]{:S(2)}) collective-permute-start(f32[8,256]{1,0:T(8,128)S(1)} %pairs.7), channel_id=1, source_target_pairs={{0,1},{1,0},{2,3},{3,2},{4,5},{5,4},{6,7},{7,6},{8,9},{9,8},{10,11... | collective-permute-start | bytes 24584 | tf_op jit(solution)/shard_map/ppermute | solution.py:297
  21.0 1.4 %pairs.6.mine_ref = f32[8,256]{1,0:T(8,128)S(1)} custom-call(f32[16,1024]{1,0:T(8,128)S(1)} %collective-permute-done.4.refs_0_, bf16[128,512]{1,0:T(8,128)(2,1)S(1)} %get-tuple-element.31.mine_ref.refs_2_.refs_1_, f32[24,256]{1,0:T(8,128)S(1)} %get-tuple-element.53.refs_2_), custom_call_target="tpu_custom_call" | custom-call | flops 1610612736 | bytes 8192 | tf_op jit(solution)/shard_map/pairs/pallas_call | solution.py:263
  22.5 0.0 collective-permute-done.6.other_ref
  22.5 0.0 copy-done
  22.5 0.8 %finish.1 = (f32[6,1024]{1,0:T(8,128)}, f32[6,1024]{1,0:T(8,128)}, f32[12,256]{1,0:T(8,128)}) custom-call(f32[8,256]{1,0:T(8,128)S(1)} %pairs.6.mine_ref, f32[8,256]{1,0:T(8,128)S(1)} %collective-permute-done.6.other_ref, bf16[256,1024]{1,0:T(8,128)(2,1)S(1)} %get-tuple-element.55.turned_ref, f32[24,256]{1,0:T(8,128)S(1)} %get-tuple-element.56.old_ref, ...), custom_call_target="tpu_custom_call" | custom-call | tf_op jit(solution)/shard_map/finish/pallas_call | solution.py:337
  (3 shorter events, 0.0 us)
Async XLA Ops:
  2.8 5.1 %collective-permute-start.2 = (f32[8,256]{1,0:T(8,128)S(1)}, f32[8,256]{1,0:T(8,128)S(1)}, u32[]{:S(2)}, u32[]{:S(2)}) collective-permute-start(f32[8,256]{1,0:T(8,128)S(1)} %get-tuple-element.32), channel_id=1, source_target_pairs={{0,1},{1,0},{2,3},{3,2},{4,5},{5,4},{6,7},{7,6},{8,9},{9,8},{10,11... | collective-permute-start | bytes 24584 | tf_op jit(solution)/shard_map/ppermute | solution.py:297
  3.0 6.4 %collective-permute-start.1 = (f32[8,1024]{1,0:T(8,128)S(1)}, f32[8,1024]{1,0:T(8,128)S(1)}, u32[]{:S(2)}, u32[]{:S(2)}) collective-permute-start(f32[8,1024]{1,0:T(8,128)S(1)} %get-tuple-element.30.src_ref), channel_id=1, source_target_pairs={{0,8},{1,9},{2,10},{3,11},{4,12},{5,13},{6,14},{7,15},{8,0},{9,1},... | collective-permute-start | bytes 98312 | tf_op jit(solution)/shard_map/ppermute | solution.py:297
  6.7 3.0 %collective-permute-start = (f32[8,1024]{1,0:T(8,128)S(1)}, f32[8,1024]{1,0:T(8,128)S(1)}, u32[]{:S(2)}, u32[]{:S(2)}) collective-permute-start(f32[8,1024]{1,0:T(8,128)S(1)} %get-tuple-element.30.src_ref), channel_id=1, source_target_pairs={{0,2},{1,3},{2,0},{3,1},{4,6},{5,7},{6,4},{7,5},{8,10},{9,11},{10,... | collective-permute-start | bytes 98312 | tf_op jit(solution)/shard_map/ppermute | solution.py:297
  9.4 4.2 %collective-permute-start.3 = (f32[8,1024]{1,0:T(8,128)S(1)}, f32[8,1024]{1,0:T(8,128)S(1)}, u32[]{:S(2)}, u32[]{:S(2)}) collective-permute-start(f32[8,1024]{1,0:T(8,128)S(1)} %collective-permute-done.1.refs_0_), channel_id=1, source_target_pairs={{0,2},{1,3},{2,0},{3,1},{4,6},{5,7},{6,4},{7,5},{8,10},{9,11},{10,... | collective-permute-start | bytes 98312 | tf_op jit(solution)/shard_map/ppermute | solution.py:297
  9.7 4.2 %collective-permute-start.5 = (f32[16,1024]{1,0:T(8,128)S(1)}, f32[16,1024]{1,0:T(8,128)S(1)}, u32[]{:S(2)}, u32[]{:S(2)}) collective-permute-start(f32[16,1024]{1,0:T(8,128)S(1)} %pad_maximum_fusion.1), channel_id=1, source_target_pairs={{0,4},{1,5},{2,6},{3,7},{4,0},{5,1},{6,2},{7,3},{8,12},{9,13},{10,... | collective-permute-start | bytes 196616 | tf_op jit(solution)/shard_map/ppermute | solution.py:297
  13.7 3.9 %collective-permute-start.4 = (f32[16,1024]{1,0:T(8,128)S(1)}, f32[16,1024]{1,0:T(8,128)S(1)}, u32[]{:S(2)}, u32[]{:S(2)}) collective-permute-start(f32[16,1024]{1,0:T(8,128)S(1)} %pad_maximum_fusion), channel_id=1, source_target_pairs={{0,4},{1,5},{2,6},{3,7},{4,0},{5,1},{6,2},{7,3},{8,12},{9,13},{10,... | collective-permute-start | bytes 196616 | tf_op jit(solution)/shard_map/ppermute | solution.py:297
  19.0 3.4 %copy-start = (f32[6,1024]{1,0:T(8,128)S(1)}, f32[6,1024]{1,0:T(8,128)}, u32[]{:S(2)}) copy-start(f32[6,1024]{1,0:T(8,128)} %pv_ref.1) | copy-start | bytes 73732
  19.0 3.4 %copy-start.1 = (f32[6,1024]{1,0:T(8,128)S(1)}, f32[6,1024]{1,0:T(8,128)}, u32[]{:S(2)}) copy-start(f32[6,1024]{1,0:T(8,128)} %aj_ref.1) | copy-start | bytes 73732
  19.1 3.4 %collective-permute-start.6 = (f32[8,256]{1,0:T(8,128)S(1)}, f32[8,256]{1,0:T(8,128)S(1)}, u32[]{:S(2)}, u32[]{:S(2)}) collective-permute-start(f32[8,256]{1,0:T(8,128)S(1)} %pairs.7), channel_id=1, source_target_pairs={{0,1},{1,0},{2,3},{3,2},{4,5},{5,4},{6,7},{7,6},{8,9},{9,8},{10,11... | collective-permute-start | bytes 24584 | tf_op jit(solution)/shard_map/ppermute | solution.py:297
